TPU v7x, 32 devices: a whole 2x2x4 slice. The times are simulated.
32 devices in a mesh: lang: 16 (over z, y, x), fsdp: 2 (over core).
Axes of the slice: x: 2, y: 2, z: 4, core: 2. Of those that a mesh axis runs over, the one named last changes fastest.
Arguments:
- tokens: bfloat16 [8192, 1920], P(('lang', 'fsdp')), may hold values from -6 to 6
- lengths: int32 [512], P(('lang', 'fsdp')), may hold values from 1 to 31, as said below
- target: int32 [512], P(('lang', 'fsdp')), may hold values from 0 to 201, as said below
- lang_group: int32 [202], replicated, may hold values from 0 to 15, as said below
- blocks: int32 [16, 2], P('lang', 'fsdp'), may hold values from 0 to 4, as said below
- enc_gain: float32 [1920], replicated, may hold values from 0.5 to 1.5
- w_query: bfloat16 [1920, 1024], P('fsdp'), may hold values from -1 to 1
- w_key: bfloat16 [1920, 1024], P('fsdp'), may hold values from -1 to 1
- w_value: bfloat16 [1920, 1024], P('fsdp'), may hold values from -0.125 to 0.125
- w_output: bfloat16 [1024, 1920], P('fsdp'), may hold values from -0.1875 to 0.1875
- moe_gain: float32 [1920], replicated, may hold values from 0.5 to 1.5
- expert_in: bfloat16 [16, 1920, 4096], P('lang', None, 'fsdp'), may hold values from -0.125 to 0.125
- expert_out: bfloat16 [16, 4096, 1920], P('lang', 'fsdp'), may hold values from -0.09375 to 0.09375
Outputs:
- mixed: bfloat16 [8192, 1920], P(('lang', 'fsdp'))
Inputs may be any that keep to these rules, and one draw needn't show every extreme that they name: The lengths of one device sum to 256; its tokens come in 8 consecutive runs of 32 tokens, each run holding whole sentences. All sentences of one run of 32 tokens have target languages of one group, and the runs of one device have different groups. At most 512 tokens reach one group from the devices of one fsdp index, and for every fsdp index some group receives exactly 512. `lang_group`: every group has at least one language. blocks[g, f] is the number of tokens that reach group g from the devices of fsdp index f, divided by 128 and rounded up.
All inputs are finite; a program needn't handle non-finite values.
Results may differ from a plain program's by a relative error of at most 0.0066.
Values may be sent and summed in bfloat16 or wider, within the bound.
No kernel may reach another device: no remote copies, remote signals or barrier semaphores. Data moves between devices by JAX's collectives and lax.ppermute only.
A program may use at most 128 MiB of HBM per device.

v0:
```python
import jax
import jax.numpy as jnp
from jax import lax
from jax.sharding import PartitionSpec as P

HDIM = 128
BLOCK = 128


epsilon = 1e-05


def layer_norm(values, gain):
    floats = values.astype(jnp.float32)
    center = floats - jnp.mean(floats, axis=-1, keepdims=True)
    spread = jnp.mean(center * center, axis=-1, keepdims=True)
    return center * lax.rsqrt(spread + epsilon) * gain


def sentence_ids(lengths, count):
    ends = jnp.cumsum(lengths)
    positions = jnp.arange(count, dtype=ends.dtype)
    return jnp.sum((positions[:, None] >= ends[None, :]).astype(jnp.int32), axis=1)


def attend(query_rows, key_rows, value_rows, sentence):
    count = query_rows.shape[0]
    heads = query_rows.shape[1] // HDIM
    query_heads = query_rows.reshape(count, heads, HDIM)
    key_heads = key_rows.reshape(count, heads, HDIM)
    value_heads = value_rows.reshape(count, heads, HDIM)
    scores = jnp.einsum(
        "qhd,khd->hqk", query_heads, key_heads, preferred_element_type=jnp.float32
    ) / jnp.sqrt(jnp.float32(HDIM))
    same = sentence[:, None] == sentence[None, :]
    scores = jnp.where(same[None], scores, jnp.float32(-1e30))
    top = jnp.max(scores, axis=-1, keepdims=True)
    weights = jnp.exp(scores - top)
    probs = (weights / jnp.sum(weights, axis=-1, keepdims=True)).astype(jnp.bfloat16)
    context = jnp.einsum("hqk,khd->qhd", probs, value_heads, preferred_element_type=jnp.float32)
    return context.astype(jnp.bfloat16).reshape(count, heads * HDIM)


def body(
    tokens,
    lengths,
    target,
    lang_group,
    blocks,
    enc_gain,
    w_query,
    w_key,
    w_value,
    w_output,
    moe_gain,
    expert_in,
    expert_out,
):
    count = tokens.shape[0]
    width = tokens.shape[1]
    normed = layer_norm(tokens, enc_gain).astype(jnp.bfloat16)
    pieces = (
        lax.all_gather(w_query, "fsdp", axis=0, tiled=True),
        lax.all_gather(w_key, "fsdp", axis=0, tiled=True),
        lax.all_gather(w_value, "fsdp", axis=0, tiled=True),
    )
    columns = normed
    query_sum, key_sum, value_sum = tuple(
        (jnp.dot(columns, piece, preferred_element_type=jnp.float32) for piece in pieces)
    )
    sentence = sentence_ids(lengths, count)
    context = attend(
        query_sum.astype(jnp.bfloat16),
        key_sum.astype(jnp.bfloat16),
        value_sum.astype(jnp.bfloat16),
        sentence,
    )
    columns = context
    attention = jnp.dot(
        columns,
        lax.all_gather(w_output, "fsdp", axis=0, tiled=True),
        preferred_element_type=jnp.float32,
    )
    hidden = (tokens.astype(jnp.float32) + attention).astype(jnp.bfloat16)
    routed = layer_norm(hidden, moe_gain).astype(jnp.bfloat16)
    lang_count = lax.axis_size("lang")
    slots_dev = min(32, lang_count // 2)
    capacity = count // slots_dev
    group_cap = min(2 * slots_dev, lang_count) * capacity
    lang_ids = jnp.arange(lang_group.shape[0], dtype=jnp.int32)
    sent_group = jnp.sum(
        jnp.where(target[:, None] == lang_ids[None, :], lang_group[None, :], 0), axis=1
    )
    sent_index = jnp.arange(lengths.shape[0], dtype=jnp.int32)
    tok_group = jnp.sum(
        jnp.where(sentence[:, None] == sent_index[None, :], sent_group[None, :], 0), axis=1
    )
    positions = jnp.arange(count, dtype=jnp.int32)
    earlier = (tok_group[:, None] == tok_group[None, :]) & (positions[None, :] < positions[:, None])
    rank = jnp.sum(earlier.astype(jnp.int32), axis=1)
    slot = tok_group * capacity + rank
    dispatch = (
        jnp.arange(lang_count * capacity, dtype=jnp.int32)[:, None] == slot[None, :]
    ).astype(jnp.bfloat16)
    outgoing = (
        jnp.dot(dispatch, routed, preferred_element_type=jnp.float32)
        .astype(jnp.bfloat16)
        .reshape(lang_count, capacity, width)
    )
    group_ids = jnp.arange(lang_count, dtype=jnp.int32)
    sent_counts = jnp.sum(
        (tok_group[:, None] == group_ids[None, :]).astype(jnp.float32), axis=0
    ).astype(jnp.bfloat16)
    incoming, in_counts = (
        lax.all_to_all(outgoing, "lang", split_axis=0, concat_axis=0, tiled=True),
        lax.all_to_all(sent_counts, "lang", split_axis=0, concat_axis=0, tiled=True),
    )
    in_counts = in_counts.astype(jnp.int32)
    offsets = jnp.cumsum(in_counts) - in_counts
    slot_ids = jnp.arange(capacity, dtype=jnp.int32)
    occupied = slot_ids[None, :] < in_counts[:, None]
    place = jnp.where(occupied, offsets[:, None] + slot_ids[None, :], -1).reshape(-1)
    compact_map = (jnp.arange(group_cap, dtype=jnp.int32)[:, None] == place[None, :]).astype(
        jnp.bfloat16
    )
    packed = jnp.dot(
        compact_map,
        incoming.reshape(lang_count * capacity, width),
        preferred_element_type=jnp.float32,
    ).astype(jnp.bfloat16)
    own_blocks = blocks.astype(jnp.bfloat16)
    group_rows, group_blocks = (
        lax.all_gather(packed, "fsdp", axis=0, tiled=True),
        lax.all_gather(own_blocks, "fsdp", axis=0, tiled=True),
    )
    live_blocks = group_blocks.reshape(-1).astype(jnp.int32)

    def one_block(index):
        first = index * BLOCK
        source = first // group_cap
        local = first % group_cap // BLOCK
        picked = lax.dynamic_slice_in_dim(group_rows, first, BLOCK, 0)

        def compute():
            inner = jax.nn.relu(
                jnp.dot(picked, expert_in[0], preferred_element_type=jnp.float32)
            ).astype(jnp.bfloat16)
            return jnp.dot(inner, expert_out[0], preferred_element_type=jnp.float32)

        def nothing():
            return jnp.zeros((BLOCK, width), jnp.float32)

        return lax.cond(local < live_blocks[source], compute, nothing)

    result = lax.psum_scatter(
        lax.map(
            one_block, jnp.arange(lax.axis_size("fsdp") * group_cap // BLOCK, dtype=jnp.int32)
        ).reshape(lax.axis_size("fsdp") * group_cap, width),
        "fsdp",
        scatter_dimension=0,
        tiled=True,
    ).astype(jnp.bfloat16)
    returned = lax.dot_general(
        compact_map, result, (((0,), (0,)), ((), ())), preferred_element_type=jnp.float32
    )
    returned = returned.astype(jnp.bfloat16).reshape(lang_count, capacity, width)
    back = lax.all_to_all(returned, "lang", split_axis=0, concat_axis=0, tiled=True)
    expert = lax.dot_general(
        dispatch,
        back.reshape(lang_count * capacity, width),
        (((0,), (0,)), ((), ())),
        preferred_element_type=jnp.float32,
    )
    return (hidden.astype(jnp.float32) + expert).astype(jnp.bfloat16)


def solution(mesh):
    return jax.shard_map(
        body,
        mesh=mesh,
        in_specs=(
            P(("lang", "fsdp"), None),
            P(("lang", "fsdp")),
            P(("lang", "fsdp")),
            P(),
            P("lang", "fsdp"),
            P(),
            P("fsdp", None),
            P("fsdp", None),
            P("fsdp", None),
            P("fsdp", None),
            P(),
            P("lang", None, "fsdp"),
            P("lang", "fsdp", None),
        ),
        out_specs=P(("lang", "fsdp"), None),
        check_vma=False,
    )
```

profile of v0, /device:TPU:16, one launch (start us, length us, event | category | flops | bytes accessed | tf_op | source)
XLA Modules:
  0.0 301.5 jit_solution(14235397443116394037)
XLA Ops:
  6.5 0.7 all-gather.6.cloned.1.call-update
  7.3 0.7 all-gather.8.cloned.1.call-update
  8.1 0.7 all-gather.10.cloned.1.call-update
  8.8 0.5 all-gather.12.cloned.1.call-update
  10.1 0.7 copy.45
  10.8 7.1 %all-to-all-start = ((bf16[16,1,1]{2,1,0:T(2,128)(2,1)}), bf16[16,1,1]{2,1,0:T(2,128)(2,1)S(1)}, u32[]{:S(2)}, u32[]{:S(2)}) async-start(bf16[16,1,1]{2,1,0:T(2,128)(2,1)} %copy.45), calls=%async_computation | async-start | bytes 16384 | tf_op jit(solution)/shard_map/all_to_all | solution.py:116
  18.3 0.4 fusion.31
  18.9 4.7 %all-gather.6.cloned.1.call-done = bf16[1920,1024]{1,0:T(8,128)(2,1)} async-done(((bf16[960,1024]{1,0:T(8,128)(2,1)}), bf16[1920,1024]{1,0:T(8,128)(2,1)}) %all-gather.6.cloned.1.call-update) | async-done | bytes 3932176 | tf_op jit(solution)/shard_map/all_gather | solution.py:65
  23.6 3.4 %convolution_convert_fusion.6 = bf16[256,1024]{1,0:T(8,128)(2,1)S(1)} fusion(bf16[1920,1024]{1,0:T(8,128)(2,1)} %all-gather.6.cloned.1.call-done, bf16[256,1920]{1,0:T(8,128)(2,1)S(1)} %copy-done, f32[1920]{0:T(1024)S(1)} %copy-done.4, f32[256]{0:T(256)S(1)} %add_rsqrt_fusion.1, f32[256]{0:T(256)S(1)} %broadcast_multiply_fusion.1), kind=kOutput, calls=%fused_computation.42 | convolution fusion | flops 1009352704 | bytes 5449216 | tf_op jit(solution)/shard_map/dot_general | solution.py:69
  27.2 12.4 %all-gather.8.cloned.1.call-done = bf16[1920,1024]{1,0:T(8,128)(2,1)} async-done(((bf16[960,1024]{1,0:T(8,128)(2,1)}), bf16[1920,1024]{1,0:T(8,128)(2,1)}) %all-gather.8.cloned.1.call-update) | async-done | bytes 3932176 | tf_op jit(solution)/shard_map/all_gather | solution.py:63
  39.6 3.4 %fusion.36 = bf16[32,8,8,128]{3,2,1,0:T(8,128)(2,1)S(1)} fusion(bf16[1920,1024]{1,0:T(8,128)(2,1)} %all-gather.8.cloned.1.call-done, bf16[256,1920]{1,0:T(8,128)(2,1)S(1)} %copy-done, f32[1920]{0:T(1024)S(1)} %copy-done.4, f32[256]{0:T(256)S(1)} %add_rsqrt_fusion.1, f32[256]{0:T(256)S(1)} %broadcast_multiply_fusion.1), kind=kOutput, calls=%fused_computation.43 | convolution fusion | flops 1009352704 | bytes 5449216 | tf_op jit(solution)/shard_map/dot_general | solution.py:69
  43.0 12.6 %all-gather.10.cloned.1.call-done = bf16[1920,1024]{1,0:T(8,128)(2,1)} async-done(((bf16[960,1024]{1,0:T(8,128)(2,1)}), bf16[1920,1024]{1,0:T(8,128)(2,1)}) %all-gather.10.cloned.1.call-update) | async-done | bytes 3932176 | tf_op jit(solution)/shard_map/all_gather | solution.py:64
  55.6 3.4 %fusion.37 = bf16[32,8,8,128]{3,2,1,0:T(8,128)(2,1)S(1)} fusion(bf16[1920,1024]{1,0:T(8,128)(2,1)} %all-gather.10.cloned.1.call-done, bf16[256,1920]{1,0:T(8,128)(2,1)S(1)} %copy-done, f32[1920]{0:T(1024)S(1)} %copy-done.4, f32[256]{0:T(256)S(1)} %add_rsqrt_fusion.1, f32[256]{0:T(256)S(1)} %broadcast_multiply_fusion.1), kind=kOutput, calls=%fused_computation.44 | convolution fusion | flops 1009352704 | bytes 5449216 | tf_op jit(solution)/shard_map/dot_general | solution.py:69
  59.1 2.2 fusion.72
  61.2 1.9 convolution_convert_fusion.3
  63.1 8.4 %all-gather.12.cloned.1.call-done = bf16[1024,1920]{1,0:T(8,128)(2,1)} async-done(((bf16[512,1920]{1,0:T(8,128)(2,1)}), bf16[1024,1920]{1,0:T(8,128)(2,1)}) %all-gather.12.cloned.1.call-update) | async-done | bytes 3932176 | tf_op jit(solution)/shard_map/all_gather | solution.py:81
  71.5 3.5 %convert_reduce_fusion = (f32[256]{0:T(256)S(1)}, bf16[256,1920]{1,0:T(8,128)(2,1)S(1)}) fusion(bf16[256,1024]{0,1:T(8,128)(2,1)S(1)} %bitcast.80, bf16[1024,1920]{1,0:T(8,128)(2,1)} %all-gather.12.cloned.1.call-done, bf16[256,1920]{1,0:T(8,128)(2,1)S(1)} %copy-done), kind=kOutput, calls=%fused_computation.18 | convolution fusion | flops 1009090304 | bytes 6423552 | tf_op jit(solution)/shard_map/dot_general | solution.py:79
  75.0 0.4 fusion.28
  75.4 2.2 convolution_convert_fusion
  77.6 7.0 %all-to-all-start.1 = ((bf16[16,32,1920]{2,1,0:T(8,128)(2,1)}), bf16[16,32,1920]{2,1,0:T(8,128)(2,1)}, u32[]{:S(2)}, u32[]{:S(2)}) async-start(bf16[16,32,1920]{2,1,0:T(8,128)(2,1)} %bitcast.75), calls=%async_computation.1 | async-start | bytes 3932160 | tf_op jit(solution)/shard_map/all_to_all | solution.py:115
  84.8 0.4 convert_reduce_fusion.5
  85.3 45.1 %all-to-all-done.1 = bf16[16,32,1920]{2,1,0:T(8,128)(2,1)} async-done(((bf16[16,32,1920]{2,1,0:T(8,128)(2,1)}), bf16[16,32,1920]{2,1,0:T(8,128)(2,1)}, u32[]{:S(2)}, u32[]{:S(2)}) %all-to-all-start.1) | async-done | bytes 1966112 | tf_op jit(solution)/shard_map/all_to_all | solution.py:115
  130.5 4.2 %convolution_convert_fusion.2 = bf16[512,1920]{1,0:T(8,128)(2,1)} fusion(bf16[512,1920]{1,0:T(8,128)(2,1)} %bitcast.14, s32[512]{0:T(512)S(1)} %select_n.69), kind=kOutput, calls=%fused_computation.15 | convolution fusion | flops 1007878144 | bytes 3934208 | tf_op jit(solution)/shard_map/dot_general | solution.py:126
  135.4 0.7 dynamic-slice
  136.0 0.8 dynamic-update-slice
  136.8 2.6 all-reduce
  139.5 7.9 %all-gather.14.cloned.1.call-done = bf16[1024,1920]{1,0:T(8,128)(2,1)} async-done(((bf16[512,1920]{1,0:T(8,128)(2,1)}), bf16[1024,1920]{1,0:T(8,128)(2,1)}) %all-gather.14.cloned.1.call-update) | async-done | bytes 3932176 | tf_op jit(solution)/shard_map/all_gather | solution.py:133
  147.4 61.0 %while.13 = (s32[]{:T(128)}, f32[8,128,1920]{2,1,0:T(8,128)}, s32[8]{0:T(128)S(1)}, s32[2]{0:T(128)S(1)}, bf16[1024,1920]{1,0:T(8,128)(2,1)}, /*index=5*/bf16[1,...) while((s32[]{:T(128)}, f32[8,128,1920]{2,1,0:T(8,128)}, ...), condition=%wide.region_16.17_spmd, body=%wide.region_13.16_spmd.sunk | while | flops 2013790208 | bytes 19170444 | solution.py:156
  147.4 0.6 dynamic_slice.29
  148.7 0.6 dynamic_slice.30
  149.9 8.0 %conditional.2 = (f32[1,128,1920]{2,1,0:T(8,128)S(1)}) conditional(s32[]{:T(128)} %convert_element_type.216, () %tuple.49, (s32[]{:T(128)}, pred[]{:T(512)}, bf16[1024,1920]{1,0:T(8,128)(2,1)}, bf16[1,1920,2048]{2,1,0:T(8,128)(2,1)}, bf16[1,2048,1920]{2,1,0:T(8,128)(2,1)}) %tuple.50), branch_computations={%region_14.14_spmd, %region_15.15_spmd} | conditional | flops 2013790208 | bytes 17203236 | solution.py:153
  149.9 8.0 %fusion.4 = f32[1,128,1920]{2,1,0:T(8,128)S(1)} fusion(bf16[1,2048,1920]{2,1,0:T(8,128)(2,1)} %get-tuple-element.171, bf16[1,1920,2048]{2,1,0:T(8,128)(2,1)} %get-tuple-element.170, bf16[1024,1920]{1,0:T(8,128)(2,1)} %get-tuple-element.167, s32[]{:T(128)S(6)} %select_n.55), kind=kOutput, calls=%fused_computation.4 | convolution fusion | flops 2013790208 | bytes 17203204 | tf_op jit(solution)/shard_map/while/body/eval_jaxpr/cond/branch_1_fun/dot_general | solution.py:148
  157.9 1.0 constant_dynamic-update-slice_fusion.2
  159.0 0.6 dynamic_slice.29
  160.2 0.6 dynamic_slice.30
  161.5 8.0 %conditional.2 = (f32[1,128,1920]{2,1,0:T(8,128)S(1)}) conditional(s32[]{:T(128)} %convert_element_type.216, () %tuple.49, (s32[]{:T(128)}, pred[]{:T(512)}, bf16[1024,1920]{1,0:T(8,128)(2,1)}, bf16[1,1920,2048]{2,1,0:T(8,128)(2,1)}, bf16[1,2048,1920]{2,1,0:T(8,128)(2,1)}) %tuple.50), branch_computations={%region_14.14_spmd, %region_15.15_spmd} | conditional | flops 2013790208 | bytes 17203236 | solution.py:153
  161.5 8.0 %fusion.4 = f32[1,128,1920]{2,1,0:T(8,128)S(1)} fusion(bf16[1,2048,1920]{2,1,0:T(8,128)(2,1)} %get-tuple-element.171, bf16[1,1920,2048]{2,1,0:T(8,128)(2,1)} %get-tuple-element.170, bf16[1024,1920]{1,0:T(8,128)(2,1)} %get-tuple-element.167, s32[]{:T(128)S(6)} %select_n.55), kind=kOutput, calls=%fused_computation.4 | convolution fusion | flops 2013790208 | bytes 17203204 | tf_op jit(solution)/shard_map/while/body/eval_jaxpr/cond/branch_1_fun/dot_general | solution.py:148
  169.5 1.1 constant_dynamic-update-slice_fusion.2
  170.6 0.6 dynamic_slice.29
  171.8 0.6 dynamic_slice.30
  173.2 1.0 constant_dynamic-update-slice_fusion.2
  174.2 0.6 dynamic_slice.29
  175.5 0.6 dynamic_slice.30
  176.8 1.0 constant_dynamic-update-slice_fusion.2
  177.9 0.6 dynamic_slice.29
  179.1 0.6 dynamic_slice.30
  180.4 8.0 %conditional.2 = (f32[1,128,1920]{2,1,0:T(8,128)S(1)}) conditional(s32[]{:T(128)} %convert_element_type.216, () %tuple.49, (s32[]{:T(128)}, pred[]{:T(512)}, bf16[1024,1920]{1,0:T(8,128)(2,1)}, bf16[1,1920,2048]{2,1,0:T(8,128)(2,1)}, bf16[1,2048,1920]{2,1,0:T(8,128)(2,1)}) %tuple.50), branch_computations={%region_14.14_spmd, %region_15.15_spmd} | conditional | flops 2013790208 | bytes 17203236 | solution.py:153
  180.4 8.0 %fusion.4 = f32[1,128,1920]{2,1,0:T(8,128)S(1)} fusion(bf16[1,2048,1920]{2,1,0:T(8,128)(2,1)} %get-tuple-element.171, bf16[1,1920,2048]{2,1,0:T(8,128)(2,1)} %get-tuple-element.170, bf16[1024,1920]{1,0:T(8,128)(2,1)} %get-tuple-element.167, s32[]{:T(128)S(6)} %select_n.55), kind=kOutput, calls=%fused_computation.4 | convolution fusion | flops 2013790208 | bytes 17203204 | tf_op jit(solution)/shard_map/while/body/eval_jaxpr/cond/branch_1_fun/dot_general | solution.py:148
  188.4 1.0 constant_dynamic-update-slice_fusion.2
  189.4 0.6 dynamic_slice.29
  190.7 0.6 dynamic_slice.30
  192.0 8.0 %conditional.2 = (f32[1,128,1920]{2,1,0:T(8,128)S(1)}) conditional(s32[]{:T(128)} %convert_element_type.216, () %tuple.49, (s32[]{:T(128)}, pred[]{:T(512)}, bf16[1024,1920]{1,0:T(8,128)(2,1)}, bf16[1,1920,2048]{2,1,0:T(8,128)(2,1)}, bf16[1,2048,1920]{2,1,0:T(8,128)(2,1)}) %tuple.50), branch_computations={%region_14.14_spmd, %region_15.15_spmd} | conditional | flops 2013790208 | bytes 17203236 | solution.py:153
  192.0 8.0 %fusion.4 = f32[1,128,1920]{2,1,0:T(8,128)S(1)} fusion(bf16[1,2048,1920]{2,1,0:T(8,128)(2,1)} %get-tuple-element.171, bf16[1,1920,2048]{2,1,0:T(8,128)(2,1)} %get-tuple-element.170, bf16[1024,1920]{1,0:T(8,128)(2,1)} %get-tuple-element.167, s32[]{:T(128)S(6)} %select_n.55), kind=kOutput, calls=%fused_computation.4 | convolution fusion | flops 2013790208 | bytes 17203204 | tf_op jit(solution)/shard_map/while/body/eval_jaxpr/cond/branch_1_fun/dot_general | solution.py:148
  200.0 1.0 constant_dynamic-update-slice_fusion.2
  201.0 0.6 dynamic_slice.29
  202.3 0.6 dynamic_slice.30
  203.7 1.0 constant_dynamic-update-slice_fusion.2
  204.7 0.6 dynamic_slice.29
  206.0 0.6 dynamic_slice.30
  207.3 1.0 constant_dynamic-update-slice_fusion.2
  208.4 30.0 %reduce-scatter.2.cloned.1.call-done = f32[512,1920]{1,0:T(8,128)} async-done(((f32[1024,1920]{1,0:T(8,128)}), f32[512,1920]{1,0:T(8,128)}) %reduce-scatter.2.cloned.1.call-update) | async-done | bytes 3932176 | tf_op jit(solution)/shard_map/reduce_scatter | solution.py:155
  238.4 3.4 %convolution_convert_fusion.1 = bf16[512,1920]{1,0:T(8,128)(2,1)S(1)} fusion(f32[512,1920]{1,0:T(8,128)} %reduce-scatter.2.cloned.1.call-done, s32[512]{0:T(512)S(1)} %select_n.69), kind=kOutput, calls=%fused_computation.14 | convolution fusion | flops 1008861184 | bytes 5900288 | tf_op jit(solution)/shard_map/dot_general | solution.py:163
  241.8 51.2 %all_to_all.16 = bf16[16,32,1920]{2,1,0:T(8,128)(2,1)S(1)} all-to-all(bf16[16,32,1920]{2,1,0:T(8,128)(2,1)S(1)} %bitcast.74), channel_id=1, replica_groups=mesh['lang'=16,'fsdp'=2] {'lang'}, dimensions={0} | all-to-all | bytes 3932160 | tf_op jit(solution)/shard_map/all_to_all | solution.py:167
  292.9 1.7 fusion.22
  (57 shorter events, 2.6 us)
Async XLA Ops:
  6.5 17.0 %all-gather.6.cloned.1.call-start = ((), (), s32[]{:S(2)}) async-start(), calls=%async_computation.4 | async-start | bytes 5898240 | tf_op jit(solution)/shard_map/all_gather | solution.py:65
  7.3 32.3 %all-gather.8.cloned.1.call-start = ((), (), s32[]{:S(2)}) async-start(), calls=%async_computation.5 | async-start | bytes 5898240 | tf_op jit(solution)/shard_map/all_gather | solution.py:63
  8.0 1.4 copy-start.2
  8.0 1.7 copy-start.1
  8.0 1.7 copy-start.3
  8.0 10.1 %copy-start = (bf16[256,1920]{1,0:T(8,128)(2,1)S(1)}, bf16[256,1920]{1,0:T(8,128)(2,1)}, u32[]{:S(2)}) copy-start(bf16[256,1920]{1,0:T(8,128)(2,1)} %param.17) | copy-start | bytes 2949124
  8.0 47.6 %all-gather.10.cloned.1.call-start = ((), (), s32[]{:S(2)}) async-start(), calls=%async_computation.6 | async-start | bytes 5898240 | tf_op jit(solution)/shard_map/all_gather | solution.py:64
  8.8 14.8 %copy-start.4 = (f32[1920]{0:T(1024)S(1)}, f32[1920]{0:T(1024)}, u32[]{:S(2)}) copy-start(f32[1920]{0:T(1024)} %param.22) | copy-start | bytes 23044
  8.8 62.7 %all-gather.12.cloned.1.call-start = ((), (), s32[]{:S(2)}) async-start(), calls=%async_computation.7 | async-start | bytes 5898240 | tf_op jit(solution)/shard_map/all_gather | solution.py:81
  10.8 66.8 %all-to-all-start = ((bf16[16,1,1]{2,1,0:T(2,128)(2,1)}), bf16[16,1,1]{2,1,0:T(2,128)(2,1)S(1)}, u32[]{:S(2)}, u32[]{:S(2)}) async-start(bf16[16,1,1]{2,1,0:T(2,128)(2,1)} %copy.45), calls=%async_computation | async-start | bytes 16384 | tf_op jit(solution)/shard_map/all_to_all | solution.py:116
  71.5 3.9 %copy-start.5 = (f32[1920]{0:T(1024)S(1)}, f32[1920]{0:T(1024)}, u32[]{:S(2)}) copy-start(f32[1920]{0:T(1024)} %param.27) | copy-start | bytes 23044
  77.6 52.8 %all-to-all-start.1 = ((bf16[16,32,1920]{2,1,0:T(8,128)(2,1)}), bf16[16,32,1920]{2,1,0:T(8,128)(2,1)}, u32[]{:S(2)}, u32[]{:S(2)}) async-start(bf16[16,32,1920]{2,1,0:T(8,128)(2,1)} %bitcast.75), calls=%async_computation.1 | async-start | bytes 3932160 | tf_op jit(solution)/shard_map/all_to_all | solution.py:115
  84.6 62.8 %all-gather.14.cloned.1.call-start = ((), (), s32[]{:S(2)}) async-start(), calls=%async_computation.8 | async-start | bytes 5898240 | tf_op jit(solution)/shard_map/all_gather | solution.py:133
  134.6 0.7 copy-start.6
  134.7 103.7 %reduce-scatter.2.cloned.1.call-start = ((), (), s32[]{:S(2)}) async-start(), calls=%async_computation.9 | async-start | bytes 11796480 | tf_op jit(solution)/shard_map/reduce_scatter | solution.py:155
Sparse Core Ops, SparseCore 0:
  8.9 14.6 all-gather.5
  25.1 14.4 all-gather.7
  41.1 14.4 all-gather.9
  57.0 14.4 all-gather.11
  134.8 12.5 all-gather.13
  208.5 29.8 reduce-scatter.1
where the time goes:
time: 307 us; the launch traced here: 302 us
  waiting for transfers between devices  124 us (40%)
  matrix products  61.2 us (20%)
  blocking collectives  53.8 us (18%)
  local copies, waits for them, and re-layouts  20.8 us (7%)
  starting transfers between devices  14.3 us (5%)
  between operations  14.3 us (5%)
  loops' own time  10.7 us (3%)
    all_to_all x1, blocking collectives, body(): lax.all_to_all(returned, 'lang', split_axis=0, concat_axis=0, tiled=True)  51.2 us
    all_to_all x1, waiting for transfers between devices, body(): lax.all_to_all(outgoing, 'lang', split_axis=0, concat_axis=0, tiled=True)  45.1 us
    dot_general x4, matrix products, compute(): return jnp.dot(inner, expert_out[0], preferred_element_type=jnp.float32)  31.9 us
    reduce_scatter x1, waiting for transfers between devices, body(): lax.psum_scatter(lax.map(one_block, jnp.arange(lax.axis_size('fsdp') * gr...  30 us
    all_gather x1, waiting for transfers between devices, body(): lax.all_gather(w_key, 'fsdp', axis=0, tiled=True)  12.6 us
    all_gather x1, waiting for transfers between devices, body(): lax.all_gather(w_query, 'fsdp', axis=0, tiled=True)  12.4 us
    another operation x1, loops' own time, body(): lax.map(one_block, jnp.arange(lax.axis_size('fsdp') * group_cap // BLOCK,...  10.6 us
    dot_general x3, matrix products, body(): jnp.dot(columns, piece, preferred_element_type=jnp.float32)  10.2 us
  transfers between devices with their start and end apart: 8, of which 7 were waited for; matrix products, arithmetic and copies ran while one was open for 8% of the time, Pallas kernels for 0%

commit v1 on v0

v1 whole, which is shorter than its diff:
```python
import functools

import jax
import jax.numpy as jnp
from jax import lax
from jax.experimental import pallas as pl
from jax.experimental.pallas import tpu as pltpu
from jax.sharding import PartitionSpec as P

HDIM = 128
BLOCK = 128
VMEM_LIMIT = 56 * 1024 * 1024

epsilon = 1e-05


def layer_norm(values, gain):
    floats = values.astype(jnp.float32)
    center = floats - jnp.mean(floats, axis=-1, keepdims=True)
    spread = jnp.mean(center * center, axis=-1, keepdims=True)
    return center * lax.rsqrt(spread + epsilon) * gain


def attend(query_rows, key_rows, value_rows, sentence):
    count = query_rows.shape[0]
    heads = query_rows.shape[1] // HDIM
    query_heads = query_rows.reshape(count, heads, HDIM)
    key_heads = key_rows.reshape(count, heads, HDIM)
    value_heads = value_rows.reshape(count, heads, HDIM)
    scores = jnp.einsum(
        "qhd,khd->hqk", query_heads, key_heads, preferred_element_type=jnp.float32
    ) / jnp.sqrt(jnp.float32(HDIM))
    same = sentence[:, None] == sentence[None, :]
    scores = jnp.where(same[None], scores, jnp.float32(-1e30))
    top = jnp.max(scores, axis=-1, keepdims=True)
    weights = jnp.exp(scores - top)
    probs = (weights / jnp.sum(weights, axis=-1, keepdims=True)).astype(jnp.bfloat16)
    context = jnp.einsum("hqk,khd->qhd", probs, value_heads, preferred_element_type=jnp.float32)
    return context.astype(jnp.bfloat16).reshape(count, heads * HDIM)


def expert_kernel(slots, rows, pieces, per, *refs):
    ins = refs[:slots]
    first = refs[slots : slots + pieces]
    second = refs[slots + pieces : slots + 2 * pieces]
    outs = refs[slots + 2 * pieces : 2 * slots + 2 * pieces]
    packed, total = refs[2 * slots + 2 * pieces :]
    step = pl.program_id(0)

    @pl.when(step == 0)
    def _():
        for s in range(slots):
            packed[s * rows : (s + 1) * rows, :] = ins[s][...]
        total[...] = jnp.zeros_like(total)

    for p in range(pieces):

        @pl.when(step // per == p)
        def _():
            inner = jnp.dot(packed[...], first[p][...], preferred_element_type=jnp.float32)
            inner = jnp.maximum(inner, 0.0).astype(jnp.bfloat16)
            total[...] += jnp.dot(inner, second[p][...], preferred_element_type=jnp.float32)

    @pl.when(step == pieces * per - 1)
    def _():
        for s in range(slots):
            outs[s][...] = total[s * rows : (s + 1) * rows, :].astype(jnp.bfloat16)


def expert_ffn(ins, first, second):
    slots, pieces = len(ins), len(first)
    rows, width = ins[0].shape
    hidden = first[0].shape[1]
    chunk = 512 if hidden % 512 == 0 else hidden
    per = hidden // chunk

    def at(p, i):
        return jnp.clip(i - p * per, 0, per - 1)

    whole = pl.BlockSpec((rows, width), lambda i: (0, 0))
    return pl.pallas_call(
        functools.partial(expert_kernel, slots, rows, pieces, per),
        grid=(pieces * per,),
        in_specs=[whole] * slots
        + [pl.BlockSpec((width, chunk), lambda i, p=p: (0, at(p, i))) for p in range(pieces)]
        + [pl.BlockSpec((chunk, width), lambda i, p=p: (at(p, i), 0)) for p in range(pieces)],
        out_specs=[whole] * slots,
        out_shape=[jax.ShapeDtypeStruct((rows, width), jnp.bfloat16)] * slots,
        scratch_shapes=[
            pltpu.VMEM((slots * rows, width), jnp.bfloat16),
            pltpu.VMEM((slots * rows, width), jnp.float32),
        ],
        compiler_params=pltpu.CompilerParams(
            dimension_semantics=("arbitrary",), vmem_limit_bytes=VMEM_LIMIT
        ),
    )(*ins, *first, *second)


def body(
    tokens,
    lengths,
    target,
    lang_group,
    blocks,
    enc_gain,
    w_query,
    w_key,
    w_value,
    w_output,
    moe_gain,
    expert_in,
    expert_out,
):
    count, width = tokens.shape
    lang_count, fsdp_count = lax.axis_size("lang"), lax.axis_size("fsdp")
    lang_at, fsdp_at = lax.axis_index("lang"), lax.axis_index("fsdp")
    slots_dev = min(32, lang_count // 2)
    capacity = count // slots_dev

    def pieces_of(shard):
        return [shard] + [
            lax.ppermute(shard, "fsdp", [(i, (i + s) % fsdp_count) for i in range(fsdp_count)])
            for s in range(1, fsdp_count)
        ]

    def columns_of(rows):
        part = rows.shape[1] // fsdp_count
        return [
            lax.dynamic_slice_in_dim(rows, (fsdp_at - s) % fsdp_count * part, part, 1)
            for s in range(fsdp_count)
        ]

    def product(columns, pieces):
        return sum(
            jnp.dot(c, w, preferred_element_type=jnp.float32) for c, w in zip(columns, pieces)
        )

    query_w, key_w, value_w, output_w = map(pieces_of, (w_query, w_key, w_value, w_output))

    ends = jnp.cumsum(lengths)
    positions = jnp.arange(count, dtype=jnp.int32)
    sentence = jnp.sum((positions[:, None] >= ends[None, :]).astype(jnp.int32), axis=1)
    lang_ids = jnp.arange(lang_group.shape[0], dtype=jnp.int32)
    sent_group = jnp.sum(
        jnp.where(target[:, None] == lang_ids[None, :], lang_group[None, :], 0), axis=1
    )
    run_ids = jnp.arange(slots_dev, dtype=jnp.int32)
    run_sent = jnp.sum((run_ids[:, None] * capacity >= ends[None, :]).astype(jnp.int32), axis=1)
    sent_ids = jnp.arange(lengths.shape[0], dtype=jnp.int32)
    run_group = jnp.sum(
        jnp.where(run_sent[:, None] == sent_ids[None, :], sent_group[None, :], 0), axis=1
    )
    group_ids = jnp.arange(lang_count, dtype=jnp.int32)
    sends = jnp.any(run_group[:, None] == group_ids[None, :], axis=0).astype(jnp.int32)
    mine = group_ids[:, None] == lang_at
    table = lax.psum(
        jnp.concatenate(
            [jnp.where(mine, sends[None, :], 0), jnp.where(mine, blocks[:, :1], 0)], axis=1
        ),
        "lang",
    )
    before = jnp.sum(jnp.where(group_ids[:, None] < lang_at, table[:, :lang_count], 0), axis=0)
    group_live = before * capacity // BLOCK < table[:, lang_count]
    run_live = jnp.any((run_group[:, None] == group_ids[None, :]) & group_live[None, :], axis=1)

    normed = layer_norm(tokens, enc_gain).astype(jnp.bfloat16)
    columns = columns_of(normed)
    query = product(columns, query_w).astype(jnp.bfloat16)
    keyed = product(columns, key_w).astype(jnp.bfloat16)
    valued = product(columns, value_w).astype(jnp.bfloat16)
    context = attend(query, keyed, valued, sentence)
    attention = product(columns_of(context), output_w)
    hidden = (tokens.astype(jnp.float32) + attention).astype(jnp.bfloat16)
    routed = layer_norm(hidden, moe_gain).astype(jnp.bfloat16)

    dispatch = (group_ids[:, None] == run_group[None, :]).astype(jnp.bfloat16)
    runs = routed.reshape(slots_dev, capacity * width)
    outgoing = jnp.dot(dispatch, runs, preferred_element_type=jnp.float32).astype(jnp.bfloat16)
    incoming = lax.all_to_all(
        outgoing.reshape(lang_count, capacity, width), "lang", 0, 0, tiled=True
    )
    expert_shards = lax.optimization_barrier((expert_in[0], expert_out[0], *output_w))[:2]
    first, second = map(pieces_of, expert_shards)
    (result,) = expert_ffn([incoming.reshape(lang_count * capacity, width)], first, second)
    back = lax.all_to_all(result.reshape(lang_count, capacity, width), "lang", 0, 0, tiled=True)
    expert = jnp.dot(
        (dispatch * run_live[None, :].astype(jnp.bfloat16)).T,
        back.reshape(lang_count, capacity * width),
        preferred_element_type=jnp.float32,
    ).reshape(count, width)
    return (hidden.astype(jnp.float32) + expert).astype(jnp.bfloat16)


def solution(mesh):
    return jax.shard_map(
        body,
        mesh=mesh,
        in_specs=(
            P(("lang", "fsdp"), None),
            P(("lang", "fsdp")),
            P(("lang", "fsdp")),
            P(),
            P("lang", "fsdp"),
            P(),
            P("fsdp", None),
            P("fsdp", None),
            P("fsdp", None),
            P("fsdp", None),
            P(),
            P("lang", None, "fsdp"),
            P("lang", "fsdp", None),
        ),
        out_specs=P(("lang", "fsdp"), None),
        check_vma=False,
    )
```

time: 307 us -> 230 us (0.75)
  the two profiles are of different devices: /device:TPU:16 before, /device:TPU:0 now
where the time goes in v1:
time: 230 us; the launch traced here: 229 us
  blocking collectives  154 us (67%)
  Pallas kernels  25 us (11%)
  matrix products  23.9 us (10%)
  other arithmetic  8.93 us (4%)
  local copies, waits for them, and re-layouts  7.15 us (3%)
  starting transfers between devices  6.05 us (3%)
  waiting for transfers between devices  3.19 us (1%)
    psum x1, blocking collectives, body(): lax.psum(jnp.concatenate([jnp.where(mine, sends[None, :], 0), jnp.where(m...  99.3 us
    all_to_all x1, blocking collectives, body(): lax.all_to_all(outgoing.reshape(lang_count, capacity, width), 'lang', 0,...  54.7 us
    pallas_call x1, Pallas kernels, expert_ffn(): pl.pallas_call(functools.partial(expert_kernel, slots, rows, pieces, per)...  25 us
    dot_general x8, matrix products, product(): jnp.dot(c, w, preferred_element_type=jnp.float32)  16.2 us
  transfers between devices with their start and end apart: 7, of which 1 were waited for; matrix products, arithmetic and copies ran while one was open for 13% of the time, Pallas kernels for 0%

profile of v1, /device:TPU:0, one launch (start us, length us, event | category | flops | bytes accessed | tf_op | source)
XLA Modules:
  0.0 229.1 jit_solution(6760410410084107423)
XLA Ops:
  0.0 0.0 copy-start
  0.0 0.5 collective-permute-start.1
  0.5 0.1 collective-permute-start.2
  0.6 0.4 collective-permute-start
  1.1 0.1 collective-permute-start.3
  1.1 1.4 convert_reduce_fusion.1
  2.6 1.6 fusion.9
  4.2 0.0 copy-done.8
  4.2 0.1 copy.24
  4.3 0.1 reduce
  4.4 0.0 copy-done
  4.4 0.0 copy-done.5
  4.4 0.4 fusion.11
  4.9 0.2 convert_reduce_fusion.3
  5.0 0.1 convert_reduce_fusion.2
  5.1 0.0 copy-done.7
  5.1 0.0 copy-done.9
  5.1 0.0 copy-start.3
  5.2 0.2 select_reduce_fusion
  5.3 0.2 select_reduce_fusion.1
  5.5 3.5 %fusion.32 = f32[256,1024]{1,0:T(8,128)} fusion(bf16[960,1024]{1,0:T(8,128)(2,1)} %param.19, bf16[256,1920]{1,0:T(8,128)(2,1)S(1)} %fusion.11, s32[]{:T(128)S(6)} %select_n.69), kind=kOutput, calls=%fused_computation.47 | convolution fusion | flops 503316480 | bytes 3538948 | tf_op jit(solution)/shard_map/dot_general | solution.py:135
  9.0 0.0 copy-done.3
  9.0 0.8 fusion.30
  9.8 3.2 %collective-permute-done.3 = bf16[512,1920]{1,0:T(8,128)(2,1)} collective-permute-done((bf16[512,1920]{1,0:T(8,128)(2,1)}, bf16[512,1920]{1,0:T(8,128)(2,1)}, u32[]{:S(2)}, u32[]{:S(2)}) %collective-permute-start.3) | collective-permute-done | bytes 1966112 | tf_op jit(solution)/shard_map/ppermute | solution.py:122
  12.9 0.4 collective-permute-start.4
  13.3 0.1 collective-permute-start.5
  13.4 0.7 broadcast_compare_fusion
  14.2 0.0 copy-done.2
  14.2 0.8 fusion.34
  14.9 0.0 collective-permute-done
  14.9 2.3 %fusion.14 = bf16[256,1024]{1,0:T(8,128)(2,1)S(1)} fusion(f32[256,1024]{1,0:T(8,128)S(1)} %fusion.34, bf16[960,1024]{1,0:T(8,128)(2,1)} %collective-permute-done, bf16[256,1920]{1,0:T(8,128)(2,1)S(1)} %fusion.11, s32[]{:T(128)S(6)} %select_n.71), kind=kOutput, calls=%fused_computation.28 | convolution fusion | flops 503840768 | bytes 4063236 | tf_op jit(solution)/shard_map/dot_general | solution.py:135
  17.3 1.0 copy.30
  18.3 0.0 collective-permute-done.1
  18.3 2.6 %fusion.18 = bf16[32,8,8,128]{3,2,1,0:T(8,128)(2,1)S(1)} fusion(f32[256,1024]{1,0:T(8,128)} %fusion.32, bf16[960,1024]{1,0:T(8,128)(2,1)} %collective-permute-done.1, bf16[256,1920]{1,0:T(8,128)(2,1)S(1)} %fusion.11, s32[]{:T(128)S(6)} %select_n.71), kind=kOutput, calls=%fused_computation.33 | convolution fusion | flops 503840768 | bytes 4063236 | tf_op jit(solution)/shard_map/dot_general | solution.py:135
  20.8 0.0 collective-permute-done.2
  20.9 3.1 %fusion.17 = bf16[32,8,8,128]{3,2,1,0:T(8,128)(2,1)} fusion(f32[256,1024]{1,0:T(8,128)S(1)} %fusion.30, bf16[960,1024]{1,0:T(8,128)(2,1)} %collective-permute-done.2, bf16[256,1920]{1,0:T(8,128)(2,1)S(1)} %fusion.11, s32[]{:T(128)S(6)} %select_n.71), kind=kOutput, calls=%fused_computation.32 | convolution fusion | flops 503840768 | bytes 4063236 | tf_op jit(solution)/shard_map/dot_general | solution.py:135
  24.0 3.3 %fusion.74 = (f32[8,256]{1,0:T(8,128)S(1)}, f32[8,256,256]{1,2,0:T(8,128)}) fusion(pred[256,256]{0,1:T(8,128)(4,1)} %broadcast_compare_fusion, bf16[32,8,8,128]{3,2,1,0:T(8,128)(2,1)} %fusion.17, bf16[32,8,8,128]{3,2,1,0:T(8,128)(2,1)S(1)} %fusion.18), kind=kOutput, calls=%fused_computation.102 | convolution fusion | flops 136315136 | bytes 3219456 | tf_op jit(solution)/shard_map/sub | solution.py:36
  27.3 0.0 copy-done.4
  27.3 2.0 convolution_convert_fusion.1
  29.4 0.1 copy-done.1
  29.5 0.7 fusion.37
  30.2 0.0 copy-start.6
  30.2 2.4 %convert_reduce_fusion = (f32[256]{0:T(256)S(1)}, bf16[256,1920]{1,0:T(8,128)(2,1)S(1)}) fusion(f32[256,1920]{1,0:T(8,128)S(1)} %fusion.37, bf16[512,1920]{1,0:T(8,128)(2,1)} %collective-permute-done.3, bf16[256,1024]{0,1:T(8,128)(2,1)S(1)} %bitcast.67, s32[]{:T(128)S(6)} %select_n.74, bf16[256,1920]{1,0:T(8,128)(2,1)S(1)} %copy-done), kind=kOutput, calls=%fused_computation.4 | convolution fusion | flops 506265344 | bytes 6161412 | tf_op jit(solution)/shard_map/dot_general | solution.py:135
  32.7 0.4 fusion.6
  33.1 0.0 copy-done.6
  33.1 0.4 fusion.8
  33.5 0.4 reshape.176
  34.0 0.7 convolution_convert_fusion
  34.6 0.2 copy.33
  34.8 54.7 %all_to_all.10 = bf16[16,32,1920]{2,1,0:T(8,128)(2,1)} all-to-all(bf16[16,32,1920]{2,1,0:T(8,128)(2,1)S(1)} %bitcast.64), channel_id=1, replica_groups=mesh['lang'=16,'fsdp'=2] {'lang'}, dimensions={0} | all-to-all | bytes 3932160 | tf_op jit(solution)/shard_map/all_to_all | solution.py:179
  89.6 0.0 collective-permute-done.4.refs_2_
  89.6 0.0 collective-permute-done.5.refs_4_
  89.6 25.0 %shard_map.127 = bf16[512,1920]{1,0:T(8,128)(2,1)} custom-call(bf16[512,1920]{1,0:T(8,128)(2,1)} %bitcast.61, bf16[1920,2048]{1,0:T(8,128)(2,1)} %bitcast.57, bf16[1920,2048]{1,0:T(8,128)(2,1)} %collective-permute-done.4.refs_2_, bf16[2048,1920]{1,0:T(8,128)(2,1)} %bitcast.59, bf16[2048,1920]{1,0:T(8,128)(2,1)} %collective-permute-done.5.refs_4_), custom_call_target="tpu_custom_call" | custom-call | tf_op jit(solution)/shard_map/pallas_call | solution.py:81
  114.6 4.4 %all-to-all-start.1 = ((bf16[16,32,1920]{2,1,0:T(8,128)(2,1)}), bf16[16,32,1920]{2,1,0:T(8,128)(2,1)}, u32[]{:S(2)}, u32[]{:S(2)}) async-start(bf16[16,32,1920]{2,1,0:T(8,128)(2,1)} %bitcast.60), calls=%async_computation.1 | async-start | bytes 3932160 | tf_op jit(solution)/shard_map/all_to_all | solution.py:185
  119.6 0.1 fusion.52
  119.7 0.1 broadcast_select_fusion
  119.8 99.3 %psum.7 = s32[16,17]{0,1:T(8,128)S(1)} all-reduce(s32[16,17]{0,1:T(8,128)S(1)} %pad_add_fusion), channel_id=1, replica_groups=mesh['lang'=16,'fsdp'=2] {'lang'}, use_global_device_ids=true, to_apply=%region_10.11 | all-reduce | flops 272 | bytes 2176 | tf_op jit(solution)/shard_map/psum | solution.py:156
  219.1 0.1 fusion.47
  219.2 0.2 fusion.55
  219.4 0.0 all-to-all-done.1
  219.4 2.1 copy.34
  221.6 1.8 fusion.49
  223.3 3.1 %reshape.181 = f32[256,1920]{1,0:T(8,128)} reshape(f32[8,61440]{1,0:T(8,128)} %fusion.49) | data formatting | bytes 3932160 | tf_op jit(solution)/shard_map/reshape | solution.py:190
  226.5 2.7 %fusion.12 = bf16[256,1920]{1,0:T(8,128)(2,1)} fusion(f32[256,1920]{1,0:T(8,128)} %reshape.181, bf16[256,1920]{1,0:T(8,128)(2,1)S(1)} %get-tuple-element.12), kind=kLoop, calls=%fused_computation.23 | loop fusion | flops 1474560 | bytes 3932160 | tf_op jit(solution)/shard_map/convert_element_type | solution.py:191
  (20 shorter events, 0.1 us)
Async XLA Ops:
  0.0 4.4 %copy-start = (bf16[256,1920]{1,0:T(8,128)(2,1)S(1)}, bf16[256,1920]{1,0:T(8,128)(2,1)}, u32[]{:S(2)}) copy-start(bf16[256,1920]{1,0:T(8,128)(2,1)} %param.13) | copy-start | bytes 2949124
  0.0 4.2 %copy-start.8 = (s32[16]{0:T(128)S(1)}, s32[16]{0:T(128)}, u32[]{:S(2)}) copy-start(s32[16]{0:T(128)} %param.14) | copy-start | bytes 196
  0.0 4.4 %copy-start.5 = (f32[1920]{0:T(1024)S(1)}, f32[1920]{0:T(1024)}, u32[]{:S(2)}) copy-start(f32[1920]{0:T(1024)} %param.18) | copy-start | bytes 23044
  0.0 5.1 %copy-start.7 = (s32[202]{0:T(256)S(1)}, s32[202]{0:T(256)}, u32[]{:S(2)}) copy-start(s32[202]{0:T(256)} %param.16) | copy-start | bytes 2428
  0.0 5.1 %copy-start.9 = (s32[16]{0:T(128)S(1)}, s32[16]{0:T(128)}, u32[]{:S(2)}) copy-start(s32[16]{0:T(128)} %param.15) | copy-start | bytes 196
  0.0 18.2 %collective-permute-start.1 = (bf16[960,1024]{1,0:T(8,128)(2,1)}, bf16[960,1024]{1,0:T(8,128)(2,1)}, u32[]{:S(2)}, u32[]{:S(2)}) collective-permute-start(bf16[960,1024]{1,0:T(8,128)(2,1)} %param.19), channel_id=1, source_target_pairs={{0,1},{1,0},{2,3},{3,2},{4,5},{5,4},{6,7},{7,6},{8,9},{9,8},{10,11... | collective-permute-start | bytes 5898248 | tf_op jit(solution)/shard_map/ppermute | solution.py:122
  0.5 20.3 %collective-permute-start.2 = (bf16[960,1024]{1,0:T(8,128)(2,1)}, bf16[960,1024]{1,0:T(8,128)(2,1)}, u32[]{:S(2)}, u32[]{:S(2)}) collective-permute-start(bf16[960,1024]{1,0:T(8,128)(2,1)} %param.20), channel_id=1, source_target_pairs={{0,1},{1,0},{2,3},{3,2},{4,5},{5,4},{6,7},{7,6},{8,9},{9,8},{10,11... | collective-permute-start | bytes 5898248 | tf_op jit(solution)/shard_map/ppermute | solution.py:122
  0.6 14.3 %collective-permute-start = (bf16[960,1024]{1,0:T(8,128)(2,1)}, bf16[960,1024]{1,0:T(8,128)(2,1)}, u32[]{:S(2)}, u32[]{:S(2)}) collective-permute-start(bf16[960,1024]{1,0:T(8,128)(2,1)} %param.21), channel_id=1, source_target_pairs={{0,1},{1,0},{2,3},{3,2},{4,5},{5,4},{6,7},{7,6},{8,9},{9,8},{10,11... | collective-permute-start | bytes 5898248 | tf_op jit(solution)/shard_map/ppermute | solution.py:122
  1.1 11.9 %collective-permute-start.3 = (bf16[512,1920]{1,0:T(8,128)(2,1)}, bf16[512,1920]{1,0:T(8,128)(2,1)}, u32[]{:S(2)}, u32[]{:S(2)}) collective-permute-start(bf16[512,1920]{1,0:T(8,128)(2,1)} %param.22), channel_id=1, source_target_pairs={{0,1},{1,0},{2,3},{3,2},{4,5},{5,4},{6,7},{7,6},{8,9},{9,8},{10,11... | collective-permute-start | bytes 5898248 | tf_op jit(solution)/shard_map/ppermute | solution.py:122
  5.1 3.8 %copy-start.3 = (bf16[960,1024]{1,0:T(8,128)(2,1)S(1)}, bf16[960,1024]{1,0:T(8,128)(2,1)}, u32[]{:S(2)}) copy-start(bf16[960,1024]{1,0:T(8,128)(2,1)} %param.20) | copy-start | bytes 5898244
  9.0 5.2 %copy-start.2 = (bf16[960,1024]{1,0:T(8,128)(2,1)S(1)}, bf16[960,1024]{1,0:T(8,128)(2,1)}, u32[]{:S(2)}) copy-start(bf16[960,1024]{1,0:T(8,128)(2,1)} %param.21) | copy-start | bytes 5898244
  12.9 76.6 %collective-permute-start.4 = (bf16[1920,2048]{1,0:T(8,128)(2,1)}, bf16[1920,2048]{1,0:T(8,128)(2,1)}, u32[]{:S(2)}, u32[]{:S(2)}) collective-permute-start(bf16[1920,2048]{1,0:T(8,128)(2,1)} %bitcast.56), channel_id=1, source_target_pairs={{0,1},{1,0},{2,3},{3,2},{4,5},{5,4},{6,7},{7,6},{8,9},{9,8},{10,11... | collective-permute-start | bytes 23592968 | tf_op jit(solution)/shard_map/ppermute | solution.py:122
  13.3 76.3 %collective-permute-start.5 = (bf16[2048,1920]{1,0:T(8,128)(2,1)}, bf16[2048,1920]{1,0:T(8,128)(2,1)}, u32[]{:S(2)}, u32[]{:S(2)}) collective-permute-start(bf16[2048,1920]{1,0:T(8,128)(2,1)} %bitcast.58), channel_id=1, source_target_pairs={{0,1},{1,0},{2,3},{3,2},{4,5},{5,4},{6,7},{7,6},{8,9},{9,8},{10,11... | collective-permute-start | bytes 23592968 | tf_op jit(solution)/shard_map/ppermute | solution.py:122
  24.0 3.3 %copy-start.4 = (bf16[256,1024]{0,1:T(8,128)(2,1)S(1)}, bf16[256,1024]{0,1:T(8,128)(2,1)}, u32[]{:S(2)}) copy-start(bf16[256,1024]{0,1:T(8,128)(2,1)} %copy.30) | copy-start | bytes 1572868
  27.3 2.2 copy-start.1
  30.2 2.9 %copy-start.6 = (f32[1920]{0:T(1024)S(1)}, f32[1920]{0:T(1024)}, u32[]{:S(2)}) copy-start(f32[1920]{0:T(1024)} %param.23) | copy-start | bytes 23044
  114.6 104.9 %all-to-all-start.1 = ((bf16[16,32,1920]{2,1,0:T(8,128)(2,1)}), bf16[16,32,1920]{2,1,0:T(8,128)(2,1)}, u32[]{:S(2)}, u32[]{:S(2)}) async-start(bf16[16,32,1920]{2,1,0:T(8,128)(2,1)} %bitcast.60), calls=%async_computation.1 | async-start | bytes 3932160 | tf_op jit(solution)/shard_map/all_to_all | solution.py:185

commit v2 on v1

--- a/solution.py
+++ b/solution.py
@@ -9,7 +9,8 @@
 
 HDIM = 128
 BLOCK = 128
-VMEM_LIMIT = 56 * 1024 * 1024
+VMEM_LIMIT = 60 * 1024 * 1024
+FRONT_LIMIT = 24 * 1024 * 1024
 
 epsilon = 1e-05
 
@@ -21,22 +22,162 @@
     return center * lax.rsqrt(spread + epsilon) * gain
 
 
-def attend(query_rows, key_rows, value_rows, sentence):
-    count = query_rows.shape[0]
-    heads = query_rows.shape[1] // HDIM
-    query_heads = query_rows.reshape(count, heads, HDIM)
-    key_heads = key_rows.reshape(count, heads, HDIM)
-    value_heads = value_rows.reshape(count, heads, HDIM)
-    scores = jnp.einsum(
-        "qhd,khd->hqk", query_heads, key_heads, preferred_element_type=jnp.float32
-    ) / jnp.sqrt(jnp.float32(HDIM))
-    same = sentence[:, None] == sentence[None, :]
-    scores = jnp.where(same[None], scores, jnp.float32(-1e30))
-    top = jnp.max(scores, axis=-1, keepdims=True)
-    weights = jnp.exp(scores - top)
-    probs = (weights / jnp.sum(weights, axis=-1, keepdims=True)).astype(jnp.bfloat16)
-    context = jnp.einsum("hqk,khd->qhd", probs, value_heads, preferred_element_type=jnp.float32)
-    return context.astype(jnp.bfloat16).reshape(count, heads * HDIM)
+def dot(a, b):
+    return jnp.dot(a, b, preferred_element_type=jnp.float32)
+
+
+def in_vmem(count):
+    return [pl.BlockSpec(memory_space=pltpu.VMEM)] * count
+
+
+def cost(macs, *arrays):
+    size = sum(a.size * a.dtype.itemsize for a in arrays)
+    return pl.CostEstimate(flops=2 * macs, bytes_accessed=size, transcendentals=0)
+
+
+def project_kernel(pieces, at_ref, tokens, gain, *refs):
+    weights, rest, sums = refs[:3], refs[3 : 2 + pieces], refs[2 + pieces : 5 + pieces]
+    own = refs[-1]
+    part = own.shape[1]
+    normed = layer_norm(tokens[...], gain[...]).astype(jnp.bfloat16)
+    for v in range(pieces):
+
+        @pl.when(at_ref[0] == v)
+        def _():
+            for s, ref in enumerate((own, *rest)):
+                first = (v - s) % pieces * part
+                ref[...] = normed[:, first : first + part]
+
+    for weight, total in zip(weights, sums):
+        total[...] = dot(own[...], weight[...])
+
+
+def project(at, tokens, gain, weights, pieces):
+    count, width = tokens.shape
+    part, wide = weights[0].shape
+    out = pl.pallas_call(
+        functools.partial(project_kernel, pieces),
+        in_specs=[pl.BlockSpec(memory_space=pltpu.SMEM)] + in_vmem(5),
+        out_specs=in_vmem(pieces + 2),
+        out_shape=[jax.ShapeDtypeStruct((count, part), jnp.bfloat16)] * (pieces - 1)
+        + [jax.ShapeDtypeStruct((count, wide), jnp.float32)] * 3,
+        scratch_shapes=[pltpu.VMEM((count, part), jnp.bfloat16)],
+        compiler_params=pltpu.CompilerParams(vmem_limit_bytes=FRONT_LIMIT),
+        cost_estimate=cost(3 * count * part * wide, tokens, *weights),
+    )(at, tokens, gain, *weights)
+    return out[: pieces - 1], out[pieces - 1 :]
+
+
+def attend_kernel(rest_count, bias, *refs):
+    rest = refs[:rest_count]
+    sums = refs[rest_count : rest_count + 3]
+    weights = refs[rest_count + 3 : -2]
+    context, scores = refs[-2:]
+
+    def full(n):
+        total = sums[n][...]
+        for s in range(rest_count):
+            total += dot(rest[s][...], weights[n * rest_count + s][...])
+        return total.astype(jnp.bfloat16)
+
+    count, block = bias.shape
+    query, keyed = full(0), full(1)
+    heads = query.shape[1] // HDIM
+    tiles = [
+        (h, slice(h * HDIM, (h + 1) * HDIM), slice(top, top + block))
+        for h in range(heads)
+        for top in range(0, count, block)
+    ]
+    for h, head, rows in tiles:
+        product = lax.dot_general(
+            query[rows, head], keyed[rows, head], (((1,), (1,)), ((), ())),
+            preferred_element_type=jnp.float32,
+        )
+        scores[h, rows, :] = product * (HDIM**-0.5) + bias[rows, :]
+    valued = full(2)
+    for h, head, rows in tiles:
+        tile = scores[h, rows, :]
+        weight = jnp.exp(tile - jnp.max(tile, axis=-1, keepdims=True))
+        probs = (weight / jnp.sum(weight, axis=-1, keepdims=True)).astype(jnp.bfloat16)
+        context[rows, head] = dot(probs, valued[rows, head]).astype(jnp.bfloat16)
+
+
+def attend(bias, rest, sums, weights):
+    count, wide = sums[0].shape
+    flat = [w for pieces in weights for w in pieces]
+    return pl.pallas_call(
+        functools.partial(attend_kernel, len(rest)),
+        in_specs=in_vmem(4 + len(rest) + len(flat)),
+        out_specs=in_vmem(1)[0],
+        out_shape=jax.ShapeDtypeStruct((count, wide), jnp.bfloat16),
+        scratch_shapes=[pltpu.VMEM((wide // HDIM, *bias.shape), jnp.float32)],
+        compiler_params=pltpu.CompilerParams(vmem_limit_bytes=FRONT_LIMIT),
+        cost_estimate=cost(2 * count * sum(w.size for w in flat), *flat, *sums),
+    )(bias, *rest, *sums, *flat)
+
+
+def hidden_kernel(pieces, runs, slots, at_ref, run_ref, context, tokens, gain, *refs):
+    weights, hidden, outs, routed = refs[:pieces], refs[pieces], refs[pieces + 1 : -1], refs[-1]
+    part = weights[0].shape[0]
+    count = tokens.shape[0]
+    total = tokens[...].astype(jnp.float32)
+    for s in range(pieces):
+        first = lax.rem(at_ref[0] + pieces - s, pieces) * part
+        total += dot(context[:, pl.ds(pl.multiple_of(first, 128), part)], weights[s][...])
+    hidden[...] = total.astype(jnp.bfloat16)
+    rows = count // runs
+    for j in range(runs):
+        run = slice(j * rows, (j + 1) * rows)
+        normed = layer_norm(hidden[run, :], gain[...]).astype(jnp.bfloat16)
+        if slots:
+            routed[j] = normed
+        else:
+            outs[0][run, :] = normed
+    if slots:
+        routed[runs] = jnp.zeros_like(routed[runs])
+        for k in range(slots):
+            outs[k][...] = routed[run_ref[k]]
+
+
+def hidden_states(at, run_of_slot, context, tokens, gain, weights, runs, slots):
+    count, width = tokens.shape
+    rows = count // runs
+    outs = [(rows, width)] * slots if slots else [(count, width)]
+    out = pl.pallas_call(
+        functools.partial(hidden_kernel, len(weights), runs, slots),
+        in_specs=[pl.BlockSpec(memory_space=pltpu.SMEM)] * 2 + in_vmem(3 + len(weights)),
+        out_specs=in_vmem(1 + len(outs)),
+        out_shape=[
+            jax.ShapeDtypeStruct(shape, jnp.bfloat16) for shape in [tokens.shape, *outs]
+        ],
+        scratch_shapes=[pltpu.VMEM((runs + 1, rows, width), jnp.bfloat16)],
+        compiler_params=pltpu.CompilerParams(vmem_limit_bytes=FRONT_LIMIT),
+        cost_estimate=cost(context.size * width, context, tokens, *weights),
+    )(at, run_of_slot, context, tokens, gain, *weights)
+    return out[0], out[1:]
+
+
+def mix_kernel(slots, runs, run_ref, live_ref, hidden, *refs):
+    ins, mixed = refs[:slots], refs[slots]
+    rows = hidden.shape[0] // runs
+    for k in range(slots):
+
+        @pl.when(run_ref[k] < runs)
+        def _():
+            run = pl.ds(pl.multiple_of(run_ref[k] * rows, rows), rows)
+            expert = jnp.where(live_ref[k] > 0, ins[k][...].astype(jnp.float32), 0.0)
+            mixed[run, :] = (hidden[run, :].astype(jnp.float32) + expert).astype(jnp.bfloat16)
+
+
+def mix(run_of_slot, slot_live, hidden, ins, runs):
+    return pl.pallas_call(
+        functools.partial(mix_kernel, len(ins), runs),
+        in_specs=[pl.BlockSpec(memory_space=pltpu.SMEM)] * 2
+        + [pl.BlockSpec(memory_space=pltpu.VMEM)] * (1 + len(ins)),
+        out_specs=pl.BlockSpec(memory_space=pltpu.VMEM),
+        out_shape=jax.ShapeDtypeStruct(hidden.shape, jnp.bfloat16),
+        compiler_params=pltpu.CompilerParams(vmem_limit_bytes=FRONT_LIMIT),
+    )(run_of_slot, slot_live, hidden, *ins)
 
 
 def expert_kernel(slots, rows, pieces, per, *refs):
@@ -93,6 +234,7 @@
         compiler_params=pltpu.CompilerParams(
             dimension_semantics=("arbitrary",), vmem_limit_bytes=VMEM_LIMIT
         ),
+        cost_estimate=cost(2 * slots * rows * width * hidden * pieces, *first, *second),
     )(*ins, *first, *second)
 
 
@@ -116,26 +258,14 @@
     lang_at, fsdp_at = lax.axis_index("lang"), lax.axis_index("fsdp")
     slots_dev = min(32, lang_count // 2)
     capacity = count // slots_dev
-
-    def pieces_of(shard):
-        return [shard] + [
+    direct = lang_count <= 16 and lang_count & (lang_count - 1) == 0 and capacity % 16 == 0
+    fsdp_scalar = fsdp_at.astype(jnp.int32).reshape(1)
+
+    def others(shard):
+        return [
             lax.ppermute(shard, "fsdp", [(i, (i + s) % fsdp_count) for i in range(fsdp_count)])
             for s in range(1, fsdp_count)
         ]
-
-    def columns_of(rows):
-        part = rows.shape[1] // fsdp_count
-        return [
-            lax.dynamic_slice_in_dim(rows, (fsdp_at - s) % fsdp_count * part, part, 1)
-            for s in range(fsdp_count)
-        ]
-
-    def product(columns, pieces):
-        return sum(
-            jnp.dot(c, w, preferred_element_type=jnp.float32) for c, w in zip(columns, pieces)
-        )
-
-    query_w, key_w, value_w, output_w = map(pieces_of, (w_query, w_key, w_value, w_output))
 
     ends = jnp.cumsum(lengths)
     positions = jnp.arange(count, dtype=jnp.int32)
@@ -153,39 +283,85 @@
     group_ids = jnp.arange(lang_count, dtype=jnp.int32)
     sends = jnp.any(run_group[:, None] == group_ids[None, :], axis=0).astype(jnp.int32)
     mine = group_ids[:, None] == lang_at
-    table = lax.psum(
-        jnp.concatenate(
-            [jnp.where(mine, sends[None, :], 0), jnp.where(mine, blocks[:, :1], 0)], axis=1
-        ),
-        "lang",
-    )
+    table = jnp.concatenate(
+        [jnp.where(mine, sends[None, :], 0), jnp.where(mine, blocks[:, :1], 0)], axis=1
+    )
+    step = 1
+    while step < lang_count:
+        table += lax.ppermute(table, "lang", [(i, i ^ step) for i in range(lang_count)])
+        step *= 2
     before = jnp.sum(jnp.where(group_ids[:, None] < lang_at, table[:, :lang_count], 0), axis=0)
     group_live = before * capacity // BLOCK < table[:, lang_count]
-    run_live = jnp.any((run_group[:, None] == group_ids[None, :]) & group_live[None, :], axis=1)
-
-    normed = layer_norm(tokens, enc_gain).astype(jnp.bfloat16)
-    columns = columns_of(normed)
-    query = product(columns, query_w).astype(jnp.bfloat16)
-    keyed = product(columns, key_w).astype(jnp.bfloat16)
-    valued = product(columns, value_w).astype(jnp.bfloat16)
-    context = attend(query, keyed, valued, sentence)
-    attention = product(columns_of(context), output_w)
-    hidden = (tokens.astype(jnp.float32) + attention).astype(jnp.bfloat16)
-    routed = layer_norm(hidden, moe_gain).astype(jnp.bfloat16)
+    slot_group = jnp.bitwise_xor(group_ids, lang_at.astype(jnp.int32))
+    run_of_slot = slots_dev - jnp.sum(
+        jnp.where(run_group[None, :] == slot_group[:, None], slots_dev - run_ids[None, :], 0),
+        axis=1,
+    )
+    slot_live = jnp.any(
+        (slot_group[:, None] == group_ids[None, :]) & group_live[None, :], axis=1
+    ).astype(jnp.int32)
+
+    weights = (w_query, w_key, w_value)
+    later = [others(w) for w in weights]
+    rest, sums = project(fsdp_scalar, tokens, enc_gain[None, :], weights, fsdp_count)
+    block = 128 if count % 128 == 0 and 128 % capacity == 0 else count
+    keys = sentence.reshape(count // block, 1, block)
+    same = sentence.reshape(count // block, block, 1) == keys
+    bias = jnp.where(same, jnp.float32(0), jnp.float32(-1e30)).reshape(count, block)
+    bias, run_of_slot, slot_live, w_output, later = lax.optimization_barrier(
+        (bias, run_of_slot, slot_live, w_output, later)
+    )
+    output_w = [w_output, *others(w_output)]
+    context = attend(bias, rest, sums, later)
+    context, output_w, *shards = lax.optimization_barrier(
+        (context, output_w, expert_in[0], expert_out[0])
+    )
+    first, second = ([shard, *others(shard)] for shard in shards)
+    hidden, slots = hidden_states(
+        fsdp_scalar, run_of_slot, context, tokens, moe_gain[None, :], output_w, slots_dev,
+        lang_count if direct else 0,
+    )
+
+    def swap(ks, arrays):
+        return [
+            lax.ppermute(a, "lang", [(i, i ^ k) for i in range(lang_count)])
+            for k, a in zip(ks, arrays)
+        ]
+
+    if direct:
+        half, quarter = lang_count // 2, lang_count // 4
+        near = list(range(1, half))
+        far = list(range(half, half + quarter))
+        last = list(range(half + quarter, lang_count))
+
+        def after(arrays, *done):
+            return list(lax.optimization_barrier((tuple(arrays), done))[0])
+
+        far_in = swap(far, [slots[k] for k in far])
+        near_in = swap(near, [slots[k] for k in near])
+        last_in = []
+        for n, k in enumerate(last):
+            last_in += swap([k], after([slots[k]], far_in[min(n + 1, quarter - 2)]))
+        far_out = expert_ffn(after(far_in, near_in), first, second)
+        far_back = swap(far, far_out)
+        out = expert_ffn(after([slots[0], *near_in, *last_in], far_out), first, second)
+        last_back = swap(last, after(out[half:], far_back))
+        near_back = swap(near, after(out[1:half], last_back[0]))
+        back = [out[0], *near_back, *far_back, *last_back]
+        return mix(run_of_slot, slot_live, hidden, back, slots_dev)
 
     dispatch = (group_ids[:, None] == run_group[None, :]).astype(jnp.bfloat16)
-    runs = routed.reshape(slots_dev, capacity * width)
+    runs = slots[0].reshape(slots_dev, capacity * width)
     outgoing = jnp.dot(dispatch, runs, preferred_element_type=jnp.float32).astype(jnp.bfloat16)
     incoming = lax.all_to_all(
         outgoing.reshape(lang_count, capacity, width), "lang", 0, 0, tiled=True
     )
-    expert_shards = lax.optimization_barrier((expert_in[0], expert_out[0], *output_w))[:2]
-    first, second = map(pieces_of, expert_shards)
     (result,) = expert_ffn([incoming.reshape(lang_count * capacity, width)], first, second)
     back = lax.all_to_all(result.reshape(lang_count, capacity, width), "lang", 0, 0, tiled=True)
-    expert = jnp.dot(
-        (dispatch * run_live[None, :].astype(jnp.bfloat16)).T,
+    expert = lax.dot_general(
+        dispatch * group_live[:, None].astype(jnp.bfloat16),
         back.reshape(lang_count, capacity * width),
+        (((0,), (0,)), ((), ())),
         preferred_element_type=jnp.float32,
     ).reshape(count, width)
     return (hidden.astype(jnp.float32) + expert).astype(jnp.bfloat16)

time: 230 us -> 171 us (0.74)
  the two profiles are of different devices: /device:TPU:0 before, /device:TPU:16 now
where the time goes in v2:
time: 171 us; the launch traced here: 168 us
  starting transfers between devices  73.8 us (43%)
  Pallas kernels  49.1 us (29%)
  waiting for transfers between devices  27.9 us (16%)
  local copies, waits for them, and re-layouts  14 us (8%)
  other arithmetic  2.2 us (1%)
    ppermute x30, starting transfers between devices, swap(): lax.ppermute(a, 'lang', [(i, i ^ k) for i in range(lang_count)])  68.1 us
    pallas_call x2, Pallas kernels, expert_ffn(): pl.pallas_call(functools.partial(expert_kernel, slots, rows, pieces, per)...  37.4 us
    ppermute x30, waiting for transfers between devices, swap(): lax.ppermute(a, 'lang', [(i, i ^ k) for i in range(lang_count)])  17.1 us
    unnamed x56, local copies, waits for them, and re-layouts  12.5 us
    ppermute x4, waiting for transfers between devices, body(): lax.ppermute(table, 'lang', [(i, i ^ step) for i in range(lang_count)])  10.8 us
    pallas_call x1, Pallas kernels, attend(): pl.pallas_call(functools.partial(attend_kernel, len(rest)), in_specs=in_v...  4.68 us
    ppermute x4, starting transfers between devices, body(): lax.ppermute(table, 'lang', [(i, i ^ step) for i in range(lang_count)])  4.63 us
  transfers between devices with their start and end apart: 40, of which 13 were waited for; matrix products, arithmetic and copies ran while one was open for 2% of the time, Pallas kernels for 28%

profile of v2, /device:TPU:16, one launch (start us, length us, event | category | flops | bytes accessed | tf_op | source)
XLA Modules:
  0.0 168.0 jit_solution(14783711862344517637)
XLA Ops:
  0.0 0.5 collective-permute-start.5
  0.5 0.7 copy.16
  1.4 0.9 select_reduce_fusion
  2.3 0.2 convert_reduce_fusion.1
  2.5 0.2 select_reduce_fusion.2
  3.5 1.5 collective-permute-start
  5.1 2.1 %collective-permute-done = s32[16,17]{0,1:T(8,128)S(1)} collective-permute-done((s32[16,17]{0,1:T(8,128)S(1)}, s32[16,17]{0,1:T(8,128)S(1)}, u32[]{:S(2)}, u32[]{:S(2)}) %collective-permute-start) | collective-permute-done | bytes 1120 | tf_op jit(solution)/shard_map/ppermute | solution.py:291
  7.2 1.5 collective-permute-start.1
  8.8 2.2 %collective-permute-done.1 = s32[16,17]{0,1:T(8,128)S(1)} collective-permute-done((s32[16,17]{0,1:T(8,128)S(1)}, s32[16,17]{0,1:T(8,128)S(1)}, u32[]{:S(2)}, u32[]{:S(2)}) %collective-permute-start.1) | collective-permute-done | bytes 1120 | tf_op jit(solution)/shard_map/ppermute | solution.py:291
  10.9 1.6 collective-permute-start.2
  12.6 2.0 %collective-permute-done.2 = s32[16,17]{0,1:T(8,128)S(1)} collective-permute-done((s32[16,17]{0,1:T(8,128)S(1)}, s32[16,17]{0,1:T(8,128)S(1)}, u32[]{:S(2)}, u32[]{:S(2)}) %collective-permute-start.2) | collective-permute-done | bytes 1120 | tf_op jit(solution)/shard_map/ppermute | solution.py:291
  14.8 4.5 %collective-permute-done.3 = s32[16,17]{0,1:T(8,128)S(1)} collective-permute-done((s32[16,17]{0,1:T(8,128)S(1)}, s32[16,17]{0,1:T(8,128)S(1)}, u32[]{:S(2)}, u32[]{:S(2)}) %collective-permute-start.3) | collective-permute-done | bytes 1120 | tf_op jit(solution)/shard_map/ppermute | solution.py:291
  19.4 0.2 fusion.3
  19.6 1.3 copy-done.7
  20.9 0.7 broadcast_in_dim.130.gain
  21.6 1.2 copy-done
  22.8 1.5 copy-done.3
  24.4 1.5 copy-done.4
  25.9 1.5 copy-done.5
  27.5 2.7 %shard_map.127 = (bf16[256,960]{1,0:T(8,128)(2,1)S(1)}, f32[256,1024]{1,0:T(8,128)S(1)}, f32[256,1024]{1,0:T(8,128)S(1)}, f32[256,1024]{1,0:T(8,128)S(1)}) custom-call(s32[1]{0:T(128)} %bitcast.5.at_ref, bf16[256,1920]{1,0:T(8,128)(2,1)S(1)} %copy-done, f32[1,1920]{1,0:T(1,128)S(1)} %broadcast_in_dim.130.gain, bf16[960,1024]{1,0:T(8,128)(2,1)S(1)} %copy-done.3, ...), custom_call_target="tpu_custom_call" | custom-call | flops 1509949440 | bytes 6881280 | tf_op jit(solution)/shard_map/pallas_call | solution.py:58
  30.2 4.7 %shard_map.128.context = bf16[256,1024]{1,0:T(8,128)(2,1)S(1)} custom-call(f32[256,128]{1,0:T(8,128)S(1)} %fusion.bias, bf16[256,960]{1,0:T(8,128)(2,1)S(1)} %get-tuple-element.88.refs_0_, f32[256,1024]{1,0:T(8,128)S(1)} %get-tuple-element.89.refs_1_, f32[256,1024]{1,0:T(8,128)S(1)} %get-tuple-element.90.refs_2_, f32[256,1024]{1,0:T(8,128)S(1)} %get-tuple-element.91.refs_3_, ...), custom_call_target="tpu_custom_call" | custom-call | flops 3019898880 | bytes 9043968 | tf_op jit(solution)/shard_map/pallas_call | solution.py:108
  34.9 0.6 collective-permute-start.23
  35.6 2.5 %shard_map.129 = (bf16[256,1920]{1,0:T(8,128)(2,1)S(1)}, bf16[32,1920]{1,0:T(8,128)(2,1)S(1)}, bf16[32,1920]{1,0:T(8,128)(2,1)S(1)}, bf16[32,1920]{1,0:T(8,128)(...) custom-call(s32[1]{0:T(128)} %bitcast.5.at_ref, ...), custom_call_target="tpu_custom_call" | custom-call | flops 1006632960 | bytes 5439488 | tf_op jit(solution)/shard_map/pallas_call | solution.py:146
  38.1 0.6 copy-done.9
  38.7 1.5 collective-permute-start.8
  40.2 1.5 collective-permute-start.9
  41.7 0.5 collective-permute-start.10
  42.2 2.4 %collective-permute-done.8.refs_1_ = bf16[32,1920]{1,0:T(8,128)(2,1)S(1)} collective-permute-done((bf16[32,1920]{1,0:T(8,128)(2,1)S(1)}, bf16[32,1920]{1,0:T(8,128)(2,1)S(1)}, u32[]{:S(2)}, u32[]{:S(2)}) %collective-permute-start.8) | collective-permute-done | bytes 122912 | tf_op jit(solution)/shard_map/ppermute | solution.py:327
  44.6 1.6 collective-permute-start.11
  46.2 2.1 %collective-permute-done.9.refs_2_ = bf16[32,1920]{1,0:T(8,128)(2,1)S(1)} collective-permute-done((bf16[32,1920]{1,0:T(8,128)(2,1)S(1)}, bf16[32,1920]{1,0:T(8,128)(2,1)S(1)}, u32[]{:S(2)}, u32[]{:S(2)}) %collective-permute-start.9) | collective-permute-done | bytes 122912 | tf_op jit(solution)/shard_map/ppermute | solution.py:327
  48.2 0.6 collective-permute-start.12
  48.9 2.3 %collective-permute-start.13 = (bf16[32,1920]{1,0:T(8,128)(2,1)S(1)}, bf16[32,1920]{1,0:T(8,128)(2,1)S(1)}, u32[]{:S(2)}, u32[]{:S(2)}) collective-permute-start(bf16[32,1920]{1,0:T(8,128)(2,1)S(1)} %get-tuple-element.106), channel_id=1, source_target_pairs={{0,12},{2,14},{4,8},{6,10},{8,4},{10,6},{12,0},{14,2},{16,28},{18,... | collective-permute-start | bytes 368648 | tf_op jit(solution)/shard_map/ppermute | solution.py:327
  51.2 1.3 collective-permute-start.15
  52.5 2.3 %collective-permute-done.12.refs_5_ = bf16[32,1920]{1,0:T(8,128)(2,1)S(1)} collective-permute-done((bf16[32,1920]{1,0:T(8,128)(2,1)S(1)}, bf16[32,1920]{1,0:T(8,128)(2,1)S(1)}, u32[]{:S(2)}, u32[]{:S(2)}) %collective-permute-start.12) | collective-permute-done | bytes 122912 | tf_op jit(solution)/shard_map/ppermute | solution.py:327
  54.7 5.3 %collective-permute-start.17 = (bf16[32,1920]{1,0:T(8,128)(2,1)S(1)}, bf16[32,1920]{1,0:T(8,128)(2,1)S(1)}, u32[]{:S(2)}, u32[]{:S(2)}) collective-permute-start(bf16[32,1920]{1,0:T(8,128)(2,1)S(1)} %get-tuple-element.112), channel_id=1, source_target_pairs={{0,20},{2,22},{4,16},{6,18},{8,28},{10,30},{12,24},{14,26},{16,4},... | collective-permute-start | bytes 368648 | tf_op jit(solution)/shard_map/ppermute | solution.py:327
  60.0 0.8 collective-permute-start.14
  60.9 2.7 %collective-permute-start.21 = (bf16[32,1920]{1,0:T(8,128)(2,1)S(1)}, bf16[32,1920]{1,0:T(8,128)(2,1)S(1)}, u32[]{:S(2)}, u32[]{:S(2)}) collective-permute-start(bf16[32,1920]{1,0:T(8,128)(2,1)S(1)} %get-tuple-element.118), channel_id=1, source_target_pairs={{0,16},{2,18},{4,20},{6,22},{8,24},{10,26},{12,28},{14,30},{16,0},... | collective-permute-start | bytes 368648 | tf_op jit(solution)/shard_map/ppermute | solution.py:327
  63.6 2.0 %collective-permute-done.17.refs_2_ = bf16[32,1920]{1,0:T(8,128)(2,1)S(1)} collective-permute-done((bf16[32,1920]{1,0:T(8,128)(2,1)S(1)}, bf16[32,1920]{1,0:T(8,128)(2,1)S(1)}, u32[]{:S(2)}, u32[]{:S(2)}) %collective-permute-start.17) | collective-permute-done | bytes 122912 | tf_op jit(solution)/shard_map/ppermute | solution.py:327
  65.6 5.6 %collective-permute-start.22 = (bf16[32,1920]{1,0:T(8,128)(2,1)S(1)}, bf16[32,1920]{1,0:T(8,128)(2,1)S(1)}, u32[]{:S(2)}, u32[]{:S(2)}) collective-permute-start(bf16[32,1920]{1,0:T(8,128)(2,1)S(1)} %get-tuple-element.119), channel_id=1, source_target_pairs={{0,22},{2,20},{4,18},{6,16},{8,30},{10,28},{12,26},{14,24},{16,6},... | collective-permute-start | bytes 368648 | tf_op jit(solution)/shard_map/ppermute | solution.py:327
  71.2 2.0 %collective-permute-start.16 = (bf16[32,1920]{1,0:T(8,128)(2,1)S(1)}, bf16[32,1920]{1,0:T(8,128)(2,1)S(1)}, u32[]{:S(2)}, u32[]{:S(2)}) collective-permute-start(bf16[32,1920]{1,0:T(8,128)(2,1)S(1)} %get-tuple-element.110), channel_id=1, source_target_pairs={{0,24},{2,26},{4,28},{6,30},{8,16},{10,18},{12,20},{14,22},{16,8},... | collective-permute-start | bytes 368648 | tf_op jit(solution)/shard_map/ppermute | solution.py:327
  73.3 4.2 %collective-permute-start.18 = (bf16[32,1920]{1,0:T(8,128)(2,1)S(1)}, bf16[32,1920]{1,0:T(8,128)(2,1)S(1)}, u32[]{:S(2)}, u32[]{:S(2)}) collective-permute-start(bf16[32,1920]{1,0:T(8,128)(2,1)S(1)} %get-tuple-element.113), channel_id=1, source_target_pairs={{0,26},{2,24},{4,30},{6,28},{8,18},{10,16},{12,22},{14,20},{16,10}... | collective-permute-start | bytes 368648 | tf_op jit(solution)/shard_map/ppermute | solution.py:327
  77.4 1.0 collective-permute-done.22.refs_3_
  78.4 8.0 %collective-permute-start.19 = (bf16[32,1920]{1,0:T(8,128)(2,1)S(1)}, bf16[32,1920]{1,0:T(8,128)(2,1)S(1)}, u32[]{:S(2)}, u32[]{:S(2)}) collective-permute-start(bf16[32,1920]{1,0:T(8,128)(2,1)S(1)} %get-tuple-element.115), channel_id=1, source_target_pairs={{0,28},{2,30},{4,24},{6,26},{8,20},{10,22},{12,16},{14,18},{16,12}... | collective-permute-start | bytes 368648 | tf_op jit(solution)/shard_map/ppermute | solution.py:327
  86.5 3.1 %copy-done.11 = bf16[1920,2048]{1,0:T(8,128)(2,1)} copy-done((bf16[1920,2048]{1,0:T(8,128)(2,1)}, bf16[1920,2048]{1,0:T(8,128)(2,1)S(1)}, u32[]{:S(2)}) %copy-start.11) | copy-done | bytes 7864344
  89.6 16.0 %shard_map.130 = (bf16[32,1920]{1,0:T(8,128)(2,1)}, bf16[32,1920]{1,0:T(8,128)(2,1)}, bf16[32,1920]{1,0:T(8,128)(2,1)}, bf16[32,1920]{1,0:T(8,128)(2,1)}) custom-call(bf16[32,1920]{1,0:T(8,128)(2,1)} %copy-done.14, bf16[32,1920]{1,0:T(8,128)(2,1)} %copy-done.12, bf16[32,1920]{1,0:T(8,128)(2,1)} %copy-done.13, bf16[32,1920]{1,0:T(8,128)(2,1)} %copy-done.15, ...), custom_call_target="tpu_custom_call" | custom-call | flops 4026531840 | bytes 31457280 | tf_op jit(solution)/shard_map/pallas_call | solution.py:222
  105.6 2.5 %collective-permute-start.25 = (bf16[32,1920]{1,0:T(8,128)(2,1)}, bf16[32,1920]{1,0:T(8,128)(2,1)S(1)}, u32[]{:S(2)}, u32[]{:S(2)}) collective-permute-start(bf16[32,1920]{1,0:T(8,128)(2,1)} %get-tuple-element.126), channel_id=1, source_target_pairs={{0,16},{2,18},{4,20},{6,22},{8,24},{10,26},{12,28},{14,30},{16,0},... | collective-permute-start | bytes 368648 | tf_op jit(solution)/shard_map/ppermute | solution.py:327
  108.2 6.5 %collective-permute-start.27 = (bf16[32,1920]{1,0:T(8,128)(2,1)}, bf16[32,1920]{1,0:T(8,128)(2,1)S(1)}, u32[]{:S(2)}, u32[]{:S(2)}) collective-permute-start(bf16[32,1920]{1,0:T(8,128)(2,1)} %get-tuple-element.128), channel_id=1, source_target_pairs={{0,20},{2,22},{4,16},{6,18},{8,28},{10,30},{12,24},{14,26},{16,4},... | collective-permute-start | bytes 368648 | tf_op jit(solution)/shard_map/ppermute | solution.py:327
  114.8 0.6 copy-done.26
  115.4 21.4 %shard_map.131 = (bf16[32,1920]{1,0:T(8,128)(2,1)}, bf16[32,1920]{1,0:T(8,128)(2,1)}, bf16[32,1920]{1,0:T(8,128)(2,1)}, bf16[32,1920]{1,0:T(8,128)(2,1)}, bf16[3...) custom-call(bf16[32,1920]{1,0:T(8,128)(2,1)} %copy-done.9, ...), custom_call_target="tpu_custom_call" | custom-call | flops 12079595520 | bytes 31457280 | tf_op jit(solution)/shard_map/pallas_call | solution.py:222
  136.9 1.8 %collective-permute-start.29 = (bf16[32,1920]{1,0:T(8,128)(2,1)}, bf16[32,1920]{1,0:T(8,128)(2,1)S(1)}, u32[]{:S(2)}, u32[]{:S(2)}) collective-permute-start(bf16[32,1920]{1,0:T(8,128)(2,1)} %get-tuple-element.154), channel_id=1, source_target_pairs={{0,24},{2,26},{4,28},{6,30},{8,16},{10,18},{12,20},{14,22},{16,8},... | collective-permute-start | bytes 368648 | tf_op jit(solution)/shard_map/ppermute | solution.py:327
  138.6 1.3 collective-permute-start.37
  139.9 1.0 collective-permute-start.38
  140.9 1.9 %collective-permute-start.39 = (bf16[32,1920]{1,0:T(8,128)(2,1)}, bf16[32,1920]{1,0:T(8,128)(2,1)S(1)}, u32[]{:S(2)}, u32[]{:S(2)}) collective-permute-start(bf16[32,1920]{1,0:T(8,128)(2,1)} %get-tuple-element.164), channel_id=1, source_target_pairs={{0,30},{2,28},{4,26},{6,24},{8,22},{10,20},{12,18},{14,16},{16,14}... | collective-permute-start | bytes 368648 | tf_op jit(solution)/shard_map/ppermute | solution.py:327
  142.8 0.2 collective-permute-done.29.refs_12_
  142.9 3.4 %collective-permute-start.30 = (bf16[32,1920]{1,0:T(8,128)(2,1)}, bf16[32,1920]{1,0:T(8,128)(2,1)S(1)}, u32[]{:S(2)}, u32[]{:S(2)}) collective-permute-start(bf16[32,1920]{1,0:T(8,128)(2,1)} %get-tuple-element.155), channel_id=1, source_target_pairs={{0,2},{2,0},{4,6},{6,4},{8,10},{10,8},{12,14},{14,12},{16,18},{18,... | collective-permute-start | bytes 368648 | tf_op jit(solution)/shard_map/ppermute | solution.py:327
  146.3 0.1 collective-permute-start.31
  146.4 2.8 %collective-permute-done.37.refs_13_ = bf16[32,1920]{1,0:T(8,128)(2,1)S(1)} collective-permute-done((bf16[32,1920]{1,0:T(8,128)(2,1)}, bf16[32,1920]{1,0:T(8,128)(2,1)S(1)}, u32[]{:S(2)}, u32[]{:S(2)}) %collective-permute-start.37) | collective-permute-done | bytes 122912 | tf_op jit(solution)/shard_map/ppermute | solution.py:327
  149.2 4.6 %collective-permute-start.33 = (bf16[32,1920]{1,0:T(8,128)(2,1)}, bf16[32,1920]{1,0:T(8,128)(2,1)S(1)}, u32[]{:S(2)}, u32[]{:S(2)}) collective-permute-start(bf16[32,1920]{1,0:T(8,128)(2,1)} %get-tuple-element.158), channel_id=1, source_target_pairs={{0,8},{2,10},{4,12},{6,14},{8,0},{10,2},{12,4},{14,6},{16,24},{18,... | collective-permute-start | bytes 368648 | tf_op jit(solution)/shard_map/ppermute | solution.py:327
  153.8 2.9 %collective-permute-start.34 = (bf16[32,1920]{1,0:T(8,128)(2,1)}, bf16[32,1920]{1,0:T(8,128)(2,1)S(1)}, u32[]{:S(2)}, u32[]{:S(2)}) collective-permute-start(bf16[32,1920]{1,0:T(8,128)(2,1)} %get-tuple-element.159), channel_id=1, source_target_pairs={{0,10},{2,8},{4,14},{6,12},{8,2},{10,0},{12,6},{14,4},{16,26},{18,... | collective-permute-start | bytes 368648 | tf_op jit(solution)/shard_map/ppermute | solution.py:327
  156.8 4.1 %collective-permute-start.36 = (bf16[32,1920]{1,0:T(8,128)(2,1)}, bf16[32,1920]{1,0:T(8,128)(2,1)S(1)}, u32[]{:S(2)}, u32[]{:S(2)}) collective-permute-start(bf16[32,1920]{1,0:T(8,128)(2,1)} %get-tuple-element.161), channel_id=1, source_target_pairs={{0,14},{2,12},{4,10},{6,8},{8,6},{10,4},{12,2},{14,0},{16,30},{18,... | collective-permute-start | bytes 368648 | tf_op jit(solution)/shard_map/ppermute | solution.py:327
  160.9 1.9 %collective-permute-done.35.refs_6_ = bf16[32,1920]{1,0:T(8,128)(2,1)S(1)} collective-permute-done((bf16[32,1920]{1,0:T(8,128)(2,1)}, bf16[32,1920]{1,0:T(8,128)(2,1)S(1)}, u32[]{:S(2)}, u32[]{:S(2)}) %collective-permute-start.35) | collective-permute-done | bytes 122912 | tf_op jit(solution)/shard_map/ppermute | solution.py:327
  162.8 2.5 %collective-permute-done.36.refs_7_ = bf16[32,1920]{1,0:T(8,128)(2,1)S(1)} collective-permute-done((bf16[32,1920]{1,0:T(8,128)(2,1)}, bf16[32,1920]{1,0:T(8,128)(2,1)S(1)}, u32[]{:S(2)}, u32[]{:S(2)}) %collective-permute-start.36) | collective-permute-done | bytes 122912 | tf_op jit(solution)/shard_map/ppermute | solution.py:327
  165.2 0.9 copy-done.6
  166.1 1.9 %shard_map.132 = bf16[256,1920]{1,0:T(8,128)(2,1)} custom-call(s32[16]{0:T(128)S(1)} %broadcast_subtract_fusion.run_ref, s32[16]{0:T(128)S(1)} %convert_element_type.19.live_ref, bf16[256,1920]{1,0:T(8,128)(2,1)S(1)} %get-tuple-element.99.hidden, bf16[32,1920]{1,0:T(8,128)(2,1)S(1)} %copy-done.6, bf16[32,1920]{1,0:T(8,128)(2,1)S(1)} %collective-permute-done.30.refs_1_, ...), custom_call_target="tpu_custom_call" | custom-call | tf_op jit(solution)/shard_map/pallas_call | solution.py:173
  (108 shorter events, 1.1 us)
Async XLA Ops:
  0.0 19.6 %collective-permute-start.4 = (bf16[960,1024]{1,0:T(8,128)(2,1)}, bf16[960,1024]{1,0:T(8,128)(2,1)S(1)}, u32[]{:S(2)}, u32[]{:S(2)}) collective-permute-start(bf16[960,1024]{1,0:T(8,128)(2,1)} %refs_0_.1), channel_id=1, source_target_pairs={{0,1},{1,0},{2,3},{3,2},{4,5},{5,4},{6,7},{7,6},{8,9},{9,8},{10,11... | collective-permute-start | bytes 5898248 | tf_op jit(solution)/shard_map/ppermute | solution.py:266
  0.0 20.9 %collective-permute-start.5 = (bf16[960,1024]{1,0:T(8,128)(2,1)}, bf16[960,1024]{1,0:T(8,128)(2,1)}, u32[]{:S(2)}, u32[]{:S(2)}) collective-permute-start(bf16[960,1024]{1,0:T(8,128)(2,1)} %refs_1_.1), channel_id=1, source_target_pairs={{0,1},{1,0},{2,3},{3,2},{4,5},{5,4},{6,7},{7,6},{8,9},{9,8},{10,11... | collective-permute-start | bytes 5898248 | tf_op jit(solution)/shard_map/ppermute | solution.py:266
  0.5 20.4 %collective-permute-start.6 = (bf16[960,1024]{1,0:T(8,128)(2,1)}, bf16[960,1024]{1,0:T(8,128)(2,1)}, u32[]{:S(2)}, u32[]{:S(2)}) collective-permute-start(bf16[960,1024]{1,0:T(8,128)(2,1)} %refs_2_.1), channel_id=1, source_target_pairs={{0,1},{1,0},{2,3},{3,2},{4,5},{5,4},{6,7},{7,6},{8,9},{9,8},{10,11... | collective-permute-start | bytes 5898248 | tf_op jit(solution)/shard_map/ppermute | solution.py:266
  3.5 3.7 %collective-permute-start = (s32[16,17]{0,1:T(8,128)S(1)}, s32[16,17]{0,1:T(8,128)S(1)}, u32[]{:S(2)}, u32[]{:S(2)}) collective-permute-start(s32[16,17]{0,1:T(8,128)S(1)} %pad_add_fusion), channel_id=1, source_target_pairs={{0,2},{2,0},{4,6},{6,4},{8,10},{10,8},{12,14},{14,12},{16,18},{18,... | collective-permute-start | bytes 3272 | tf_op jit(solution)/shard_map/ppermute | solution.py:291
  7.2 3.7 %collective-permute-start.1 = (s32[16,17]{0,1:T(8,128)S(1)}, s32[16,17]{0,1:T(8,128)S(1)}, u32[]{:S(2)}, u32[]{:S(2)}) collective-permute-start(s32[16,17]{0,1:T(8,128)S(1)} %fusion.6), channel_id=1, source_target_pairs={{0,4},{2,6},{4,0},{6,2},{8,12},{10,14},{12,8},{14,10},{16,20},{18,... | collective-permute-start | bytes 3272 | tf_op jit(solution)/shard_map/ppermute | solution.py:291
  10.9 3.7 %collective-permute-start.2 = (s32[16,17]{0,1:T(8,128)S(1)}, s32[16,17]{0,1:T(8,128)S(1)}, u32[]{:S(2)}, u32[]{:S(2)}) collective-permute-start(s32[16,17]{0,1:T(8,128)S(1)} %add.18), channel_id=1, source_target_pairs={{0,8},{2,10},{4,12},{6,14},{8,0},{10,2},{12,4},{14,6},{16,24},{18,... | collective-permute-start | bytes 3272 | tf_op jit(solution)/shard_map/ppermute | solution.py:291
  14.6 4.6 %collective-permute-start.3 = (s32[16,17]{0,1:T(8,128)S(1)}, s32[16,17]{0,1:T(8,128)S(1)}, u32[]{:S(2)}, u32[]{:S(2)}) collective-permute-start(s32[16,17]{0,1:T(8,128)S(1)} %add.19), channel_id=1, source_target_pairs={{0,16},{2,18},{4,20},{6,22},{8,24},{10,26},{12,28},{14,30},{16,0},... | collective-permute-start | bytes 3272 | tf_op jit(solution)/shard_map/ppermute | solution.py:291
  19.6 1.3 copy-start.7
  20.9 14.0 %collective-permute-start.7 = (bf16[512,1920]{1,0:T(8,128)(2,1)}, bf16[512,1920]{1,0:T(8,128)(2,1)S(1)}, u32[]{:S(2)}, u32[]{:S(2)}) collective-permute-start(bf16[512,1920]{1,0:T(8,128)(2,1)} %refs_0_.2), channel_id=1, source_target_pairs={{0,1},{1,0},{2,3},{3,2},{4,5},{5,4},{6,7},{7,6},{8,9},{9,8},{10,11... | collective-permute-start | bytes 5898248 | tf_op jit(solution)/shard_map/ppermute | solution.py:266
  21.6 1.2 copy-start
  22.8 1.5 copy-start.3
  24.4 1.5 copy-start.4
  25.9 1.5 copy-start.5
  27.5 2.7 %copy-start.8 = (bf16[960,1024]{1,0:T(8,128)(2,1)S(1)}, bf16[960,1024]{1,0:T(8,128)(2,1)}, u32[]{:S(2)}) copy-start(bf16[960,1024]{1,0:T(8,128)(2,1)} %copy-done.7) | copy-start | bytes 5898244
  30.2 4.7 %copy-start.10 = (bf16[1,1920,2048]{2,1,0:T(8,128)(2,1)S(1)}, bf16[1,1920,2048]{2,1,0:T(8,128)(2,1)}, u32[]{:S(2)}) copy-start(bf16[1,1920,2048]{2,1,0:T(8,128)(2,1)} %param.24) | copy-start | bytes 23592964
  30.2 5.4 %copy-start.16 = (f32[1920]{0:T(1024)S(1)}, f32[1920]{0:T(1024)}, u32[]{:S(2)}) copy-start(f32[1920]{0:T(1024)} %param.23) | copy-start | bytes 23044
  30.2 5.4 %copy-start.1 = (bf16[256,1920]{1,0:T(8,128)(2,1)S(1)}, bf16[256,1920]{1,0:T(8,128)(2,1)}, u32[]{:S(2)}) copy-start(bf16[256,1920]{1,0:T(8,128)(2,1)} %tokens.3) | copy-start | bytes 2949124
  30.2 5.4 %copy-start.2 = (bf16[512,1920]{1,0:T(8,128)(2,1)S(1)}, bf16[512,1920]{1,0:T(8,128)(2,1)}, u32[]{:S(2)}) copy-start(bf16[512,1920]{1,0:T(8,128)(2,1)} %refs_0_.2) | copy-start | bytes 5898244
  34.9 51.5 %collective-permute-start.23 = (bf16[1920,2048]{1,0:T(8,128)(2,1)S(1)}, bf16[1920,2048]{1,0:T(8,128)(2,1)S(1)}, u32[]{:S(2)}, u32[]{:S(2)}) collective-permute-start(bf16[1920,2048]{1,0:T(8,128)(2,1)S(1)} %bitcast.17), channel_id=1, source_target_pairs={{0,1},{1,0},{2,3},{3,2},{4,5},{5,4},{6,7},{7,6},{8,9},{9,8},{10,11... | collective-permute-start | bytes 23592968 | tf_op jit(solution)/shard_map/ppermute | solution.py:266
  35.5 54.1 %collective-permute-start.24 = (bf16[2048,1920]{1,0:T(8,128)(2,1)}, bf16[2048,1920]{1,0:T(8,128)(2,1)}, u32[]{:S(2)}, u32[]{:S(2)}) collective-permute-start(bf16[2048,1920]{1,0:T(8,128)(2,1)} %bitcast.18), channel_id=1, source_target_pairs={{0,1},{1,0},{2,3},{3,2},{4,5},{5,4},{6,7},{7,6},{8,9},{9,8},{10,11... | collective-permute-start | bytes 23592968 | tf_op jit(solution)/shard_map/ppermute | solution.py:266
  38.7 5.8 %collective-permute-start.8 = (bf16[32,1920]{1,0:T(8,128)(2,1)S(1)}, bf16[32,1920]{1,0:T(8,128)(2,1)S(1)}, u32[]{:S(2)}, u32[]{:S(2)}) collective-permute-start(bf16[32,1920]{1,0:T(8,128)(2,1)S(1)} %get-tuple-element.101), channel_id=1, source_target_pairs={{0,2},{2,0},{4,6},{6,4},{8,10},{10,8},{12,14},{14,12},{16,18},{18,... | collective-permute-start | bytes 368648 | tf_op jit(solution)/shard_map/ppermute | solution.py:327
  40.2 8.0 %collective-permute-start.9 = (bf16[32,1920]{1,0:T(8,128)(2,1)S(1)}, bf16[32,1920]{1,0:T(8,128)(2,1)S(1)}, u32[]{:S(2)}, u32[]{:S(2)}) collective-permute-start(bf16[32,1920]{1,0:T(8,128)(2,1)S(1)} %get-tuple-element.102), channel_id=1, source_target_pairs={{0,4},{2,6},{4,0},{6,2},{8,12},{10,14},{12,8},{14,10},{16,20},{18,... | collective-permute-start | bytes 368648 | tf_op jit(solution)/shard_map/ppermute | solution.py:327
  41.7 7.1 %collective-permute-start.10 = (bf16[32,1920]{1,0:T(8,128)(2,1)S(1)}, bf16[32,1920]{1,0:T(8,128)(2,1)S(1)}, u32[]{:S(2)}, u32[]{:S(2)}) collective-permute-start(bf16[32,1920]{1,0:T(8,128)(2,1)S(1)} %get-tuple-element.103), channel_id=1, source_target_pairs={{0,6},{2,4},{4,2},{6,0},{8,14},{10,12},{12,10},{14,8},{16,22},{18,... | collective-permute-start | bytes 368648 | tf_op jit(solution)/shard_map/ppermute | solution.py:327
  44.6 61.0 %copy-start.17 = (bf16[32,1920]{1,0:T(8,128)(2,1)}, bf16[32,1920]{1,0:T(8,128)(2,1)S(1)}, u32[]{:S(2)}) copy-start(bf16[32,1920]{1,0:T(8,128)(2,1)S(1)} %collective-permute-done.8.refs_1_) | copy-start | bytes 368644
  44.6 6.6 %collective-permute-start.11 = (bf16[32,1920]{1,0:T(8,128)(2,1)S(1)}, bf16[32,1920]{1,0:T(8,128)(2,1)S(1)}, u32[]{:S(2)}, u32[]{:S(2)}) collective-permute-start(bf16[32,1920]{1,0:T(8,128)(2,1)S(1)} %get-tuple-element.104), channel_id=1, source_target_pairs={{0,8},{2,10},{4,12},{6,14},{8,0},{10,2},{12,4},{14,6},{16,24},{18,... | collective-permute-start | bytes 368648 | tf_op jit(solution)/shard_map/ppermute | solution.py:327
  48.2 57.3 %copy-start.18 = (bf16[32,1920]{1,0:T(8,128)(2,1)}, bf16[32,1920]{1,0:T(8,128)(2,1)S(1)}, u32[]{:S(2)}) copy-start(bf16[32,1920]{1,0:T(8,128)(2,1)S(1)} %collective-permute-done.9.refs_2_) | copy-start | bytes 368644
  48.2 6.5 %collective-permute-start.12 = (bf16[32,1920]{1,0:T(8,128)(2,1)S(1)}, bf16[32,1920]{1,0:T(8,128)(2,1)S(1)}, u32[]{:S(2)}, u32[]{:S(2)}) collective-permute-start(bf16[32,1920]{1,0:T(8,128)(2,1)S(1)} %get-tuple-element.105), channel_id=1, source_target_pairs={{0,10},{2,8},{4,14},{6,12},{8,2},{10,0},{12,6},{14,4},{16,26},{18,... | collective-permute-start | bytes 368648 | tf_op jit(solution)/shard_map/ppermute | solution.py:327
  48.9 56.7 %copy-start.19 = (bf16[32,1920]{1,0:T(8,128)(2,1)}, bf16[32,1920]{1,0:T(8,128)(2,1)S(1)}, u32[]{:S(2)}) copy-start(bf16[32,1920]{1,0:T(8,128)(2,1)S(1)} %collective-permute-done.10.refs_3_) | copy-start | bytes 368644
  48.9 11.2 %collective-permute-start.13 = (bf16[32,1920]{1,0:T(8,128)(2,1)S(1)}, bf16[32,1920]{1,0:T(8,128)(2,1)S(1)}, u32[]{:S(2)}, u32[]{:S(2)}) collective-permute-start(bf16[32,1920]{1,0:T(8,128)(2,1)S(1)} %get-tuple-element.106), channel_id=1, source_target_pairs={{0,12},{2,14},{4,8},{6,10},{8,4},{10,6},{12,0},{14,2},{16,28},{18,... | collective-permute-start | bytes 368648 | tf_op jit(solution)/shard_map/ppermute | solution.py:327
  51.2 54.4 %copy-start.20 = (bf16[32,1920]{1,0:T(8,128)(2,1)}, bf16[32,1920]{1,0:T(8,128)(2,1)S(1)}, u32[]{:S(2)}) copy-start(bf16[32,1920]{1,0:T(8,128)(2,1)S(1)} %collective-permute-done.11.refs_4_) | copy-start | bytes 368644
  51.2 9.7 %collective-permute-start.15 = (bf16[32,1920]{1,0:T(8,128)(2,1)S(1)}, bf16[32,1920]{1,0:T(8,128)(2,1)S(1)}, u32[]{:S(2)}, u32[]{:S(2)}) collective-permute-start(bf16[32,1920]{1,0:T(8,128)(2,1)S(1)} %get-tuple-element.109), channel_id=1, source_target_pairs={{0,18},{2,16},{4,22},{6,20},{8,26},{10,24},{12,30},{14,28},{16,2},... | collective-permute-start | bytes 368648 | tf_op jit(solution)/shard_map/ppermute | solution.py:327
  54.7 50.8 %copy-start.21 = (bf16[32,1920]{1,0:T(8,128)(2,1)}, bf16[32,1920]{1,0:T(8,128)(2,1)S(1)}, u32[]{:S(2)}) copy-start(bf16[32,1920]{1,0:T(8,128)(2,1)S(1)} %collective-permute-done.12.refs_5_) | copy-start | bytes 368644
  54.7 10.9 %collective-permute-start.17 = (bf16[32,1920]{1,0:T(8,128)(2,1)S(1)}, bf16[32,1920]{1,0:T(8,128)(2,1)S(1)}, u32[]{:S(2)}, u32[]{:S(2)}) collective-permute-start(bf16[32,1920]{1,0:T(8,128)(2,1)S(1)} %get-tuple-element.112), channel_id=1, source_target_pairs={{0,20},{2,22},{4,16},{6,18},{8,28},{10,30},{12,24},{14,26},{16,4},... | collective-permute-start | bytes 368648 | tf_op jit(solution)/shard_map/ppermute | solution.py:327
  60.0 45.6 %copy-start.22 = (bf16[32,1920]{1,0:T(8,128)(2,1)}, bf16[32,1920]{1,0:T(8,128)(2,1)S(1)}, u32[]{:S(2)}) copy-start(bf16[32,1920]{1,0:T(8,128)(2,1)S(1)} %collective-permute-done.13.refs_6_) | copy-start | bytes 368644
  60.0 11.2 %collective-permute-start.14 = (bf16[32,1920]{1,0:T(8,128)(2,1)S(1)}, bf16[32,1920]{1,0:T(8,128)(2,1)S(1)}, u32[]{:S(2)}, u32[]{:S(2)}) collective-permute-start(bf16[32,1920]{1,0:T(8,128)(2,1)S(1)} %get-tuple-element.107), channel_id=1, source_target_pairs={{0,14},{2,12},{4,10},{6,8},{8,6},{10,4},{12,2},{14,0},{16,30},{18,... | collective-permute-start | bytes 368648 | tf_op jit(solution)/shard_map/ppermute | solution.py:327
  60.9 28.6 %copy-start.12 = (bf16[32,1920]{1,0:T(8,128)(2,1)}, bf16[32,1920]{1,0:T(8,128)(2,1)S(1)}, u32[]{:S(2)}) copy-start(bf16[32,1920]{1,0:T(8,128)(2,1)S(1)} %collective-permute-done.15.refs_1_) | copy-start | bytes 368644
  60.9 12.4 %collective-permute-start.21 = (bf16[32,1920]{1,0:T(8,128)(2,1)S(1)}, bf16[32,1920]{1,0:T(8,128)(2,1)S(1)}, u32[]{:S(2)}, u32[]{:S(2)}) collective-permute-start(bf16[32,1920]{1,0:T(8,128)(2,1)S(1)} %get-tuple-element.118), channel_id=1, source_target_pairs={{0,16},{2,18},{4,20},{6,22},{8,24},{10,26},{12,28},{14,30},{16,0},... | collective-permute-start | bytes 368648 | tf_op jit(solution)/shard_map/ppermute | solution.py:327
  65.6 23.9 %copy-start.13 = (bf16[32,1920]{1,0:T(8,128)(2,1)}, bf16[32,1920]{1,0:T(8,128)(2,1)S(1)}, u32[]{:S(2)}) copy-start(bf16[32,1920]{1,0:T(8,128)(2,1)S(1)} %collective-permute-done.17.refs_2_) | copy-start | bytes 368644
  65.6 12.8 %collective-permute-start.22 = (bf16[32,1920]{1,0:T(8,128)(2,1)S(1)}, bf16[32,1920]{1,0:T(8,128)(2,1)S(1)}, u32[]{:S(2)}, u32[]{:S(2)}) collective-permute-start(bf16[32,1920]{1,0:T(8,128)(2,1)S(1)} %get-tuple-element.119), channel_id=1, source_target_pairs={{0,22},{2,20},{4,18},{6,16},{8,30},{10,28},{12,26},{14,24},{16,6},... | collective-permute-start | bytes 368648 | tf_op jit(solution)/shard_map/ppermute | solution.py:327
  71.2 34.4 %copy-start.23 = (bf16[32,1920]{1,0:T(8,128)(2,1)}, bf16[32,1920]{1,0:T(8,128)(2,1)S(1)}, u32[]{:S(2)}) copy-start(bf16[32,1920]{1,0:T(8,128)(2,1)S(1)} %collective-permute-done.14.refs_7_) | copy-start | bytes 368644
  71.2 36.9 %collective-permute-start.16 = (bf16[32,1920]{1,0:T(8,128)(2,1)S(1)}, bf16[32,1920]{1,0:T(8,128)(2,1)S(1)}, u32[]{:S(2)}, u32[]{:S(2)}) collective-permute-start(bf16[32,1920]{1,0:T(8,128)(2,1)S(1)} %get-tuple-element.110), channel_id=1, source_target_pairs={{0,24},{2,26},{4,28},{6,30},{8,16},{10,18},{12,20},{14,22},{16,8},... | collective-permute-start | bytes 368648 | tf_op jit(solution)/shard_map/ppermute | solution.py:327
  73.3 16.3 %copy-start.14 = (bf16[32,1920]{1,0:T(8,128)(2,1)}, bf16[32,1920]{1,0:T(8,128)(2,1)S(1)}, u32[]{:S(2)}) copy-start(bf16[32,1920]{1,0:T(8,128)(2,1)S(1)} %collective-permute-done.21.refs_0_) | copy-start | bytes 368644
  73.3 34.9 %collective-permute-start.18 = (bf16[32,1920]{1,0:T(8,128)(2,1)S(1)}, bf16[32,1920]{1,0:T(8,128)(2,1)S(1)}, u32[]{:S(2)}, u32[]{:S(2)}) collective-permute-start(bf16[32,1920]{1,0:T(8,128)(2,1)S(1)} %get-tuple-element.113), channel_id=1, source_target_pairs={{0,26},{2,24},{4,30},{6,28},{8,18},{10,16},{12,22},{14,20},{16,10}... | collective-permute-start | bytes 368648 | tf_op jit(solution)/shard_map/ppermute | solution.py:327
  78.4 11.1 %copy-start.15 = (bf16[32,1920]{1,0:T(8,128)(2,1)}, bf16[32,1920]{1,0:T(8,128)(2,1)S(1)}, u32[]{:S(2)}) copy-start(bf16[32,1920]{1,0:T(8,128)(2,1)S(1)} %collective-permute-done.22.refs_3_) | copy-start | bytes 368644
  78.4 36.3 %collective-permute-start.19 = (bf16[32,1920]{1,0:T(8,128)(2,1)S(1)}, bf16[32,1920]{1,0:T(8,128)(2,1)S(1)}, u32[]{:S(2)}, u32[]{:S(2)}) collective-permute-start(bf16[32,1920]{1,0:T(8,128)(2,1)S(1)} %get-tuple-element.115), channel_id=1, source_target_pairs={{0,28},{2,30},{4,24},{6,26},{8,20},{10,22},{12,16},{14,18},{16,12}... | collective-permute-start | bytes 368648 | tf_op jit(solution)/shard_map/ppermute | solution.py:327
  86.5 3.1 %copy-start.11 = (bf16[1920,2048]{1,0:T(8,128)(2,1)}, bf16[1920,2048]{1,0:T(8,128)(2,1)S(1)}, u32[]{:S(2)}) copy-start(bf16[1920,2048]{1,0:T(8,128)(2,1)S(1)} %collective-permute-done.23.refs_5_.refs_13_) | copy-start | bytes 23592964
  86.5 28.3 %collective-permute-start.20 = (bf16[32,1920]{1,0:T(8,128)(2,1)S(1)}, bf16[32,1920]{1,0:T(8,128)(2,1)S(1)}, u32[]{:S(2)}, u32[]{:S(2)}) collective-permute-start(bf16[32,1920]{1,0:T(8,128)(2,1)S(1)} %get-tuple-element.117), channel_id=1, source_target_pairs={{0,30},{2,28},{4,26},{6,24},{8,22},{10,20},{12,18},{14,16},{16,14}... | collective-permute-start | bytes 368648 | tf_op jit(solution)/shard_map/ppermute | solution.py:327
  105.6 31.2 %collective-permute-start.25 = (bf16[32,1920]{1,0:T(8,128)(2,1)}, bf16[32,1920]{1,0:T(8,128)(2,1)S(1)}, u32[]{:S(2)}, u32[]{:S(2)}) collective-permute-start(bf16[32,1920]{1,0:T(8,128)(2,1)} %get-tuple-element.126), channel_id=1, source_target_pairs={{0,16},{2,18},{4,20},{6,22},{8,24},{10,26},{12,28},{14,30},{16,0},... | collective-permute-start | bytes 368648 | tf_op jit(solution)/shard_map/ppermute | solution.py:327
  108.2 6.6 %copy-start.24 = (bf16[32,1920]{1,0:T(8,128)(2,1)}, bf16[32,1920]{1,0:T(8,128)(2,1)S(1)}, u32[]{:S(2)}) copy-start(bf16[32,1920]{1,0:T(8,128)(2,1)S(1)} %collective-permute-done.16.refs_8_) | copy-start | bytes 368644
  108.2 28.7 %collective-permute-start.26 = (bf16[32,1920]{1,0:T(8,128)(2,1)}, bf16[32,1920]{1,0:T(8,128)(2,1)S(1)}, u32[]{:S(2)}, u32[]{:S(2)}) collective-permute-start(bf16[32,1920]{1,0:T(8,128)(2,1)} %get-tuple-element.127), channel_id=1, source_target_pairs={{0,18},{2,16},{4,22},{6,20},{8,26},{10,24},{12,30},{14,28},{16,2},... | collective-permute-start | bytes 368648 | tf_op jit(solution)/shard_map/ppermute | solution.py:327
  108.2 6.6 %copy-start.25 = (bf16[32,1920]{1,0:T(8,128)(2,1)}, bf16[32,1920]{1,0:T(8,128)(2,1)S(1)}, u32[]{:S(2)}) copy-start(bf16[32,1920]{1,0:T(8,128)(2,1)S(1)} %collective-permute-done.18.refs_9_) | copy-start | bytes 368644
  108.2 28.7 %collective-permute-start.27 = (bf16[32,1920]{1,0:T(8,128)(2,1)}, bf16[32,1920]{1,0:T(8,128)(2,1)S(1)}, u32[]{:S(2)}, u32[]{:S(2)}) collective-permute-start(bf16[32,1920]{1,0:T(8,128)(2,1)} %get-tuple-element.128), channel_id=1, source_target_pairs={{0,20},{2,22},{4,16},{6,18},{8,28},{10,30},{12,24},{14,26},{16,4},... | collective-permute-start | bytes 368648 | tf_op jit(solution)/shard_map/ppermute | solution.py:327
  114.7 22.1 %collective-permute-start.28 = (bf16[32,1920]{1,0:T(8,128)(2,1)}, bf16[32,1920]{1,0:T(8,128)(2,1)S(1)}, u32[]{:S(2)}, u32[]{:S(2)}) collective-permute-start(bf16[32,1920]{1,0:T(8,128)(2,1)} %get-tuple-element.129), channel_id=1, source_target_pairs={{0,22},{2,20},{4,18},{6,16},{8,30},{10,28},{12,26},{14,24},{16,6},... | collective-permute-start | bytes 368648 | tf_op jit(solution)/shard_map/ppermute | solution.py:327
  136.9 6.1 %collective-permute-start.29 = (bf16[32,1920]{1,0:T(8,128)(2,1)}, bf16[32,1920]{1,0:T(8,128)(2,1)S(1)}, u32[]{:S(2)}, u32[]{:S(2)}) collective-permute-start(bf16[32,1920]{1,0:T(8,128)(2,1)} %get-tuple-element.154), channel_id=1, source_target_pairs={{0,24},{2,26},{4,28},{6,30},{8,16},{10,18},{12,20},{14,22},{16,8},... | collective-permute-start | bytes 368648 | tf_op jit(solution)/shard_map/ppermute | solution.py:327
  138.6 10.6 %collective-permute-start.37 = (bf16[32,1920]{1,0:T(8,128)(2,1)}, bf16[32,1920]{1,0:T(8,128)(2,1)S(1)}, u32[]{:S(2)}, u32[]{:S(2)}) collective-permute-start(bf16[32,1920]{1,0:T(8,128)(2,1)} %get-tuple-element.162), channel_id=1, source_target_pairs={{0,26},{2,24},{4,30},{6,28},{8,18},{10,16},{12,22},{14,20},{16,10}... | collective-permute-start | bytes 368648 | tf_op jit(solution)/shard_map/ppermute | solution.py:327
  139.9 9.3 %collective-permute-start.38 = (bf16[32,1920]{1,0:T(8,128)(2,1)}, bf16[32,1920]{1,0:T(8,128)(2,1)S(1)}, u32[]{:S(2)}, u32[]{:S(2)}) collective-permute-start(bf16[32,1920]{1,0:T(8,128)(2,1)} %get-tuple-element.163), channel_id=1, source_target_pairs={{0,28},{2,30},{4,24},{6,26},{8,20},{10,22},{12,16},{14,18},{16,12}... | collective-permute-start | bytes 368648 | tf_op jit(solution)/shard_map/ppermute | solution.py:327
  140.9 13.0 %collective-permute-start.39 = (bf16[32,1920]{1,0:T(8,128)(2,1)}, bf16[32,1920]{1,0:T(8,128)(2,1)S(1)}, u32[]{:S(2)}, u32[]{:S(2)}) collective-permute-start(bf16[32,1920]{1,0:T(8,128)(2,1)} %get-tuple-element.164), channel_id=1, source_target_pairs={{0,30},{2,28},{4,26},{6,24},{8,22},{10,20},{12,18},{14,16},{16,14}... | collective-permute-start | bytes 368648 | tf_op jit(solution)/shard_map/ppermute | solution.py:327
  142.9 13.8 %collective-permute-start.30 = (bf16[32,1920]{1,0:T(8,128)(2,1)}, bf16[32,1920]{1,0:T(8,128)(2,1)S(1)}, u32[]{:S(2)}, u32[]{:S(2)}) collective-permute-start(bf16[32,1920]{1,0:T(8,128)(2,1)} %get-tuple-element.155), channel_id=1, source_target_pairs={{0,2},{2,0},{4,6},{6,4},{8,10},{10,8},{12,14},{14,12},{16,18},{18,... | collective-permute-start | bytes 368648 | tf_op jit(solution)/shard_map/ppermute | solution.py:327
  146.3 10.5 %collective-permute-start.31 = (bf16[32,1920]{1,0:T(8,128)(2,1)}, bf16[32,1920]{1,0:T(8,128)(2,1)S(1)}, u32[]{:S(2)}, u32[]{:S(2)}) collective-permute-start(bf16[32,1920]{1,0:T(8,128)(2,1)} %get-tuple-element.156), channel_id=1, source_target_pairs={{0,4},{2,6},{4,0},{6,2},{8,12},{10,14},{12,8},{14,10},{16,20},{18,... | collective-permute-start | bytes 368648 | tf_op jit(solution)/shard_map/ppermute | solution.py:327
  149.2 11.6 %collective-permute-start.32 = (bf16[32,1920]{1,0:T(8,128)(2,1)}, bf16[32,1920]{1,0:T(8,128)(2,1)S(1)}, u32[]{:S(2)}, u32[]{:S(2)}) collective-permute-start(bf16[32,1920]{1,0:T(8,128)(2,1)} %get-tuple-element.157), channel_id=1, source_target_pairs={{0,6},{2,4},{4,2},{6,0},{8,14},{10,12},{12,10},{14,8},{16,22},{18,... | collective-permute-start | bytes 368648 | tf_op jit(solution)/shard_map/ppermute | solution.py:327
  149.2 11.6 %collective-permute-start.33 = (bf16[32,1920]{1,0:T(8,128)(2,1)}, bf16[32,1920]{1,0:T(8,128)(2,1)S(1)}, u32[]{:S(2)}, u32[]{:S(2)}) collective-permute-start(bf16[32,1920]{1,0:T(8,128)(2,1)} %get-tuple-element.158), channel_id=1, source_target_pairs={{0,8},{2,10},{4,12},{6,14},{8,0},{10,2},{12,4},{14,6},{16,24},{18,... | collective-permute-start | bytes 368648 | tf_op jit(solution)/shard_map/ppermute | solution.py:327
  153.8 7.0 %collective-permute-start.34 = (bf16[32,1920]{1,0:T(8,128)(2,1)}, bf16[32,1920]{1,0:T(8,128)(2,1)S(1)}, u32[]{:S(2)}, u32[]{:S(2)}) collective-permute-start(bf16[32,1920]{1,0:T(8,128)(2,1)} %get-tuple-element.159), channel_id=1, source_target_pairs={{0,10},{2,8},{4,14},{6,12},{8,2},{10,0},{12,6},{14,4},{16,26},{18,... | collective-permute-start | bytes 368648 | tf_op jit(solution)/shard_map/ppermute | solution.py:327
  156.8 6.0 %collective-permute-start.35 = (bf16[32,1920]{1,0:T(8,128)(2,1)}, bf16[32,1920]{1,0:T(8,128)(2,1)S(1)}, u32[]{:S(2)}, u32[]{:S(2)}) collective-permute-start(bf16[32,1920]{1,0:T(8,128)(2,1)} %get-tuple-element.160), channel_id=1, source_target_pairs={{0,12},{2,14},{4,8},{6,10},{8,4},{10,6},{12,0},{14,2},{16,28},{18,... | collective-permute-start | bytes 368648 | tf_op jit(solution)/shard_map/ppermute | solution.py:327
  156.8 8.5 %collective-permute-start.36 = (bf16[32,1920]{1,0:T(8,128)(2,1)}, bf16[32,1920]{1,0:T(8,128)(2,1)S(1)}, u32[]{:S(2)}, u32[]{:S(2)}) collective-permute-start(bf16[32,1920]{1,0:T(8,128)(2,1)} %get-tuple-element.161), channel_id=1, source_target_pairs={{0,14},{2,12},{4,10},{6,8},{8,6},{10,4},{12,2},{14,0},{16,30},{18,... | collective-permute-start | bytes 368648 | tf_op jit(solution)/shard_map/ppermute | solution.py:327
  (4 other events, 2.9 us)

commit v3 on v2

--- a/solution.py
+++ b/solution.py
@@ -9,8 +9,10 @@
 
 HDIM = 128
 BLOCK = 128
-VMEM_LIMIT = 60 * 1024 * 1024
+VMEM_LIMIT = 30 * 1024 * 1024
 FRONT_LIMIT = 24 * 1024 * 1024
+
+EMPTY = 1024.0
 
 epsilon = 1e-05
 
@@ -37,8 +39,13 @@
 
 def project_kernel(pieces, at_ref, tokens, gain, *refs):
     weights, rest, sums = refs[:3], refs[3 : 2 + pieces], refs[2 + pieces : 5 + pieces]
-    own = refs[-1]
+    own, held, arrived = refs[-3:]
     part = own.shape[1]
+    copies = [
+        pltpu.make_async_copy(weight, held.at[n], arrived.at[n]) for n, weight in enumerate(weights)
+    ]
+    for copy in copies:
+        copy.start()
     normed = layer_norm(tokens[...], gain[...]).astype(jnp.bfloat16)
     for v in range(pieces):
 
@@ -48,8 +55,9 @@
                 first = (v - s) % pieces * part
                 ref[...] = normed[:, first : first + part]
 
-    for weight, total in zip(weights, sums):
-        total[...] = dot(own[...], weight[...])
+    for n, total in enumerate(sums):
+        copies[n].wait()
+        total[...] = dot(own[...], held[n])
 
 
 def project(at, tokens, gain, weights, pieces):
@@ -57,11 +65,17 @@
     part, wide = weights[0].shape
     out = pl.pallas_call(
         functools.partial(project_kernel, pieces),
-        in_specs=[pl.BlockSpec(memory_space=pltpu.SMEM)] + in_vmem(5),
+        in_specs=[pl.BlockSpec(memory_space=pltpu.SMEM)]
+        + in_vmem(2)
+        + [pl.BlockSpec(memory_space=pltpu.HBM)] * 3,
         out_specs=in_vmem(pieces + 2),
         out_shape=[jax.ShapeDtypeStruct((count, part), jnp.bfloat16)] * (pieces - 1)
         + [jax.ShapeDtypeStruct((count, wide), jnp.float32)] * 3,
-        scratch_shapes=[pltpu.VMEM((count, part), jnp.bfloat16)],
+        scratch_shapes=[
+            pltpu.VMEM((count, part), jnp.bfloat16),
+            pltpu.VMEM((3, part, wide), jnp.bfloat16),
+            pltpu.SemaphoreType.DMA((3,)),
+        ],
         compiler_params=pltpu.CompilerParams(vmem_limit_bytes=FRONT_LIMIT),
         cost_estimate=cost(3 * count * part * wide, tokens, *weights),
     )(at, tokens, gain, *weights)
@@ -134,15 +148,20 @@
         else:
             outs[0][run, :] = normed
     if slots:
-        routed[runs] = jnp.zeros_like(routed[runs])
+        routed[runs] = jnp.full_like(routed[runs], EMPTY)
+        near = outs[0].shape[0]
         for k in range(slots):
-            outs[k][...] = routed[run_ref[k]]
+            if k < near:
+                outs[0][k] = routed[run_ref[k]]
+            else:
+                outs[1 + k - near][...] = routed[run_ref[k]]
 
 
 def hidden_states(at, run_of_slot, context, tokens, gain, weights, runs, slots):
     count, width = tokens.shape
     rows = count // runs
-    outs = [(rows, width)] * slots if slots else [(count, width)]
+    near = slots // 2
+    outs = [(near, rows, width)] + [(rows, width)] * near if slots else [(count, width)]
     out = pl.pallas_call(
         functools.partial(hidden_kernel, len(weights), runs, slots),
         in_specs=[pl.BlockSpec(memory_space=pltpu.SMEM)] * 2 + in_vmem(3 + len(weights)),
@@ -157,85 +176,124 @@
     return out[0], out[1:]
 
 
-def mix_kernel(slots, runs, run_ref, live_ref, hidden, *refs):
-    ins, mixed = refs[:slots], refs[slots]
+def mix_kernel(runs, run_ref, hidden, near, *refs):
+    far, mixed = refs[:-1], refs[-1]
     rows = hidden.shape[0] // runs
-    for k in range(slots):
+    half = near.shape[0]
+    for k in range(half + len(far)):
 
         @pl.when(run_ref[k] < runs)
         def _():
             run = pl.ds(pl.multiple_of(run_ref[k] * rows, rows), rows)
-            expert = jnp.where(live_ref[k] > 0, ins[k][...].astype(jnp.float32), 0.0)
-            mixed[run, :] = (hidden[run, :].astype(jnp.float32) + expert).astype(jnp.bfloat16)
-
-
-def mix(run_of_slot, slot_live, hidden, ins, runs):
+            expert = near[k] if k < half else far[k - half][...]
+            total = hidden[run, :].astype(jnp.float32) + expert.astype(jnp.float32)
+            mixed[run, :] = total.astype(jnp.bfloat16)
+
+
+def mix(run_of_slot, hidden, near, far, runs):
     return pl.pallas_call(
-        functools.partial(mix_kernel, len(ins), runs),
-        in_specs=[pl.BlockSpec(memory_space=pltpu.SMEM)] * 2
-        + [pl.BlockSpec(memory_space=pltpu.VMEM)] * (1 + len(ins)),
-        out_specs=pl.BlockSpec(memory_space=pltpu.VMEM),
+        functools.partial(mix_kernel, runs),
+        in_specs=[pl.BlockSpec(memory_space=pltpu.SMEM)] + in_vmem(2 + len(far)),
+        out_specs=in_vmem(1)[0],
         out_shape=jax.ShapeDtypeStruct(hidden.shape, jnp.bfloat16),
         compiler_params=pltpu.CompilerParams(vmem_limit_bytes=FRONT_LIMIT),
-    )(run_of_slot, slot_live, hidden, *ins)
-
-
-def expert_kernel(slots, rows, pieces, per, *refs):
-    ins = refs[:slots]
-    first = refs[slots : slots + pieces]
-    second = refs[slots + pieces : slots + 2 * pieces]
-    outs = refs[slots + 2 * pieces : 2 * slots + 2 * pieces]
-    packed, total = refs[2 * slots + 2 * pieces :]
+    )(run_of_slot, hidden, near, *far)
+
+
+def live_kernel(first, at_ref, blocks_ref, near, *refs):
+    count = (len(refs) - 1 - 2 * first)
+    far, results, outs, live = refs[:count], refs[count : count + first], refs[-1 - first : -1], refs[-1]
+    half, rows = near.shape[:2]
+    me = at_ref[0]
+    heads = [near[k, :16, :128] for k in range(half)] + [ref[:16, :128] for ref in far]
+    full = [(jnp.max(head.astype(jnp.float32)) < EMPTY / 2).astype(jnp.int32) for head in heads]
+    source = [me // half * half + k for k in range(half)]
+    source += [jnp.bitwise_xor(me, half + k) for k in range(len(far))]
+    for k in range(half + len(far)):
+        before = sum(jnp.where(s < source[k], f, 0) for s, f in zip(source, full))
+        live[k] = (before * rows // BLOCK < blocks_ref[0, 0]).astype(jnp.int32)
+    for k in range(first):
+        kept = live[half + k] > 0
+        outs[k][...] = jnp.where(kept, results[k][...], jnp.zeros_like(results[k]))
+
+
+def live_rows(at, blocks, near, far, results):
+    first = len(results)
+    smem = pl.BlockSpec(memory_space=pltpu.SMEM)
+    out = pl.pallas_call(
+        functools.partial(live_kernel, first),
+        in_specs=[smem] * 2 + in_vmem(1 + len(far) + first),
+        out_specs=in_vmem(first) + [smem],
+        out_shape=[jax.ShapeDtypeStruct(r.shape, r.dtype) for r in results]
+        + [jax.ShapeDtypeStruct((near.shape[0] + len(far),), jnp.int32)],
+        compiler_params=pltpu.CompilerParams(vmem_limit_bytes=FRONT_LIMIT),
+    )(at, blocks, near, *far, *results)
+    return out[:first], out[first]
+
+
+def expert_kernel(sizes, pieces, per, slots, live, *refs):
+    count = len(sizes)
+    ins, outs = refs[:count], refs[count + 2 * pieces : 2 * count + 2 * pieces]
+    first, second = refs[count : count + pieces], refs[count + pieces : count + 2 * pieces]
+    packed, total = refs[-2:]
     step = pl.program_id(0)
+    tops = [sum(sizes[:n]) for n in range(count)]
 
     @pl.when(step == 0)
     def _():
-        for s in range(slots):
-            packed[s * rows : (s + 1) * rows, :] = ins[s][...]
+        for top, size, ref in zip(tops, sizes, ins):
+            packed[top : top + size, :] = ref[...]
         total[...] = jnp.zeros_like(total)
 
     for p in range(pieces):
 
         @pl.when(step // per == p)
         def _():
-            inner = jnp.dot(packed[...], first[p][...], preferred_element_type=jnp.float32)
-            inner = jnp.maximum(inner, 0.0).astype(jnp.bfloat16)
-            total[...] += jnp.dot(inner, second[p][...], preferred_element_type=jnp.float32)
+            inner = jnp.maximum(dot(packed[...], first[p][...]), 0.0).astype(jnp.bfloat16)
+            total[...] += dot(inner, second[p][...])
 
     @pl.when(step == pieces * per - 1)
     def _():
-        for s in range(slots):
-            outs[s][...] = total[s * rows : (s + 1) * rows, :].astype(jnp.bfloat16)
-
-
-def expert_ffn(ins, first, second):
-    slots, pieces = len(ins), len(first)
-    rows, width = ins[0].shape
-    hidden = first[0].shape[1]
+        for n, (top, size, ref) in enumerate(zip(tops, sizes, outs)):
+            rows = size // max(1, len(slots[n]))
+            for m, slot in enumerate(slots[n]):
+                part = slice(top + m * rows, top + (m + 1) * rows)
+                kept = jnp.where(live[slot] > 0, total[part, :], 0.0)
+                ref[m * rows : (m + 1) * rows, :] = kept.astype(jnp.bfloat16)
+            if not slots[n]:
+                ref[...] = total[top : top + size, :].astype(jnp.bfloat16)
+
+
+def expert_ffn(ins, first, second, live=None, slots=None):
+    pieces, (width, hidden) = len(first), first[0].shape
+    sizes = [a.shape[0] for a in ins]
+    rows = sum(sizes)
     chunk = 512 if hidden % 512 == 0 else hidden
     per = hidden // chunk
+    if live is None:
+        live, slots = jnp.zeros((1,), jnp.int32), [[]] * len(ins)
 
     def at(p, i):
         return jnp.clip(i - p * per, 0, per - 1)
 
-    whole = pl.BlockSpec((rows, width), lambda i: (0, 0))
     return pl.pallas_call(
-        functools.partial(expert_kernel, slots, rows, pieces, per),
+        functools.partial(expert_kernel, sizes, pieces, per, slots),
         grid=(pieces * per,),
-        in_specs=[whole] * slots
+        in_specs=[pl.BlockSpec(memory_space=pltpu.SMEM)]
+        + in_vmem(len(ins))
         + [pl.BlockSpec((width, chunk), lambda i, p=p: (0, at(p, i))) for p in range(pieces)]
         + [pl.BlockSpec((chunk, width), lambda i, p=p: (at(p, i), 0)) for p in range(pieces)],
-        out_specs=[whole] * slots,
-        out_shape=[jax.ShapeDtypeStruct((rows, width), jnp.bfloat16)] * slots,
+        out_specs=in_vmem(len(ins)),
+        out_shape=[jax.ShapeDtypeStruct(a.shape, jnp.bfloat16) for a in ins],
         scratch_shapes=[
-            pltpu.VMEM((slots * rows, width), jnp.bfloat16),
-            pltpu.VMEM((slots * rows, width), jnp.float32),
+            pltpu.VMEM((rows, width), jnp.bfloat16),
+            pltpu.VMEM((rows, width), jnp.float32),
         ],
         compiler_params=pltpu.CompilerParams(
             dimension_semantics=("arbitrary",), vmem_limit_bytes=VMEM_LIMIT
         ),
-        cost_estimate=cost(2 * slots * rows * width * hidden * pieces, *first, *second),
-    )(*ins, *first, *second)
+        cost_estimate=cost(2 * rows * width * hidden * pieces, *first, *second),
+    )(live, *ins, *first, *second)
 
 
 def body(
@@ -260,6 +318,7 @@
     capacity = count // slots_dev
     direct = lang_count <= 16 and lang_count & (lang_count - 1) == 0 and capacity % 16 == 0
     fsdp_scalar = fsdp_at.astype(jnp.int32).reshape(1)
+    lang_scalar = lang_at.astype(jnp.int32).reshape(1)
 
     def others(shard):
         return [
@@ -281,37 +340,25 @@
         jnp.where(run_sent[:, None] == sent_ids[None, :], sent_group[None, :], 0), axis=1
     )
     group_ids = jnp.arange(lang_count, dtype=jnp.int32)
-    sends = jnp.any(run_group[:, None] == group_ids[None, :], axis=0).astype(jnp.int32)
-    mine = group_ids[:, None] == lang_at
-    table = jnp.concatenate(
-        [jnp.where(mine, sends[None, :], 0), jnp.where(mine, blocks[:, :1], 0)], axis=1
-    )
-    step = 1
-    while step < lang_count:
-        table += lax.ppermute(table, "lang", [(i, i ^ step) for i in range(lang_count)])
-        step *= 2
-    before = jnp.sum(jnp.where(group_ids[:, None] < lang_at, table[:, :lang_count], 0), axis=0)
-    group_live = before * capacity // BLOCK < table[:, lang_count]
-    slot_group = jnp.bitwise_xor(group_ids, lang_at.astype(jnp.int32))
+    half = lang_count // 2
+    slot_group = jnp.where(
+        group_ids < half,
+        lang_at // half * half + group_ids,
+        jnp.bitwise_xor(group_ids, lang_at.astype(jnp.int32)),
+    )
     run_of_slot = slots_dev - jnp.sum(
         jnp.where(run_group[None, :] == slot_group[:, None], slots_dev - run_ids[None, :], 0),
         axis=1,
     )
-    slot_live = jnp.any(
-        (slot_group[:, None] == group_ids[None, :]) & group_live[None, :], axis=1
-    ).astype(jnp.int32)
-
     weights = (w_query, w_key, w_value)
     later = [others(w) for w in weights]
+    output_w = [w_output, *others(w_output)]
     rest, sums = project(fsdp_scalar, tokens, enc_gain[None, :], weights, fsdp_count)
     block = 128 if count % 128 == 0 and 128 % capacity == 0 else count
     keys = sentence.reshape(count // block, 1, block)
     same = sentence.reshape(count // block, block, 1) == keys
     bias = jnp.where(same, jnp.float32(0), jnp.float32(-1e30)).reshape(count, block)
-    bias, run_of_slot, slot_live, w_output, later = lax.optimization_barrier(
-        (bias, run_of_slot, slot_live, w_output, later)
-    )
-    output_w = [w_output, *others(w_output)]
+    bias, run_of_slot, later = lax.optimization_barrier((bias, run_of_slot, later))
     context = attend(bias, rest, sums, later)
     context, output_w, *shards = lax.optimization_barrier(
         (context, output_w, expert_in[0], expert_out[0])
@@ -329,37 +376,47 @@
         ]
 
     if direct:
-        half, quarter = lang_count // 2, lang_count // 4
-        near = list(range(1, half))
-        far = list(range(half, half + quarter))
-        last = list(range(half + quarter, lang_count))
+
+        def within(array):
+            halves = [list(range(top, top + half)) for top in (0, half)]
+            return lax.all_to_all(
+                array, "lang", 0, 0, axis_index_groups=halves, tiled=True
+            )
 
         def after(arrays, *done):
             return list(lax.optimization_barrier((tuple(arrays), done))[0])
 
-        far_in = swap(far, [slots[k] for k in far])
-        near_in = swap(near, [slots[k] for k in near])
-        last_in = []
-        for n, k in enumerate(last):
-            last_in += swap([k], after([slots[k]], far_in[min(n + 1, quarter - 2)]))
-        far_out = expert_ffn(after(far_in, near_in), first, second)
+        quarter = half // 2
+        far, last = range(half, half + quarter), range(half + quarter, lang_count)
+        near_in = within(slots[0])
+        far_in = swap(far, slots[1 : 1 + quarter])
+        last_in = swap(last, after(slots[1 + quarter :], *far_in[:3]))
+        far_out = expert_ffn(far_in, first, second)
+        far_out, live = live_rows(lang_scalar, blocks, near_in, [*far_in, *last_in], far_out)
+        ins = after([near_in.reshape(half * capacity, width), *last_in], far_out)
         far_back = swap(far, far_out)
-        out = expert_ffn(after([slots[0], *near_in, *last_in], far_out), first, second)
-        last_back = swap(last, after(out[half:], far_back))
-        near_back = swap(near, after(out[1:half], last_back[0]))
-        back = [out[0], *near_back, *far_back, *last_back]
-        return mix(run_of_slot, slot_live, hidden, back, slots_dev)
+        held = [list(range(half)), *[[k] for k in last]]
+        near_out, *last_out = expert_ffn(ins, first, second, live, held)
+        near_out, *last_out = after([near_out, *last_out], far_back)
+        last_back = swap(last, last_out)
+        near_back = within(near_out.reshape(half, capacity, width))
+        return mix(run_of_slot, hidden, near_back, far_back + last_back, slots_dev)
 
     dispatch = (group_ids[:, None] == run_group[None, :]).astype(jnp.bfloat16)
     runs = slots[0].reshape(slots_dev, capacity * width)
     outgoing = jnp.dot(dispatch, runs, preferred_element_type=jnp.float32).astype(jnp.bfloat16)
+    used = jnp.any(dispatch > 0, axis=1, keepdims=True)
+    outgoing = jnp.where(used, outgoing, jnp.bfloat16(EMPTY))
     incoming = lax.all_to_all(
         outgoing.reshape(lang_count, capacity, width), "lang", 0, 0, tiled=True
     )
+    full = (incoming[:, 0, 0] < EMPTY / 2).astype(jnp.int32)
+    live = (jnp.cumsum(full) - full) * capacity // BLOCK < blocks[0, 0]
     (result,) = expert_ffn([incoming.reshape(lang_count * capacity, width)], first, second)
-    back = lax.all_to_all(result.reshape(lang_count, capacity, width), "lang", 0, 0, tiled=True)
+    result = jnp.where(live[:, None, None], result.reshape(lang_count, capacity, width), 0)
+    back = lax.all_to_all(result.astype(jnp.bfloat16), "lang", 0, 0, tiled=True)
     expert = lax.dot_general(
-        dispatch * group_live[:, None].astype(jnp.bfloat16),
+        dispatch,
         back.reshape(lang_count, capacity * width),
         (((0,), (0,)), ((), ())),
         preferred_element_type=jnp.float32,

time: 171 us -> 146 us (0.85)
  the two profiles are of different devices: /device:TPU:16 before, /device:TPU:0 now
where the time goes in v3:
time: 146 us; the launch traced here: 145 us
  Pallas kernels  51.5 us (35%)
  starting transfers between devices  51 us (35%)
  waiting for transfers between devices  32.7 us (22%)
  local copies, waits for them, and re-layouts  7.3 us (5%)
  other arithmetic  1.68 us (1%)
    ppermute x16, starting transfers between devices, swap(): lax.ppermute(a, 'lang', [(i, i ^ k) for i in range(lang_count)])  39.7 us
    pallas_call x2, Pallas kernels, expert_ffn(): pl.pallas_call(functools.partial(expert_kernel, sizes, pieces, per, slots...  35.8 us
    ppermute x16, waiting for transfers between devices, swap(): lax.ppermute(a, 'lang', [(i, i ^ k) for i in range(lang_count)])  32.6 us
    all_to_all x2, starting transfers between devices, within(): lax.all_to_all(array, 'lang', 0, 0, axis_index_groups=halves, tiled=True)  9.74 us
    unnamed x14, local copies, waits for them, and re-layouts  5.86 us
    pallas_call x1, Pallas kernels, attend(): pl.pallas_call(functools.partial(attend_kernel, len(rest)), in_specs=in_v...  5.29 us
    pallas_call x1, Pallas kernels, project(): pl.pallas_call(functools.partial(project_kernel, pieces), in_specs=[pl.Bl...  3.89 us
    pallas_call x1, Pallas kernels, hidden_states(): pl.pallas_call(functools.partial(hidden_kernel, len(weights), runs, slots...  3.55 us
  transfers between devices with their start and end apart: 24, of which 6 were waited for; matrix products, arithmetic and copies ran while one was open for 2% of the time, Pallas kernels for 33%

profile of v3, /device:TPU:0, one launch (start us, length us, event | category | flops | bytes accessed | tf_op | source)
XLA Modules:
  0.0 145.1 jit_solution(13204273696643637725)
XLA Ops:
  0.0 0.5 collective-permute-start
  0.5 0.1 collective-permute-start.1
  0.5 0.5 collective-permute-start.2
  1.0 0.1 collective-permute-start.3
  1.0 0.7 broadcast_in_dim.71.gain
  1.7 0.7 copy.16
  2.5 0.1 reduce
  2.6 0.1 convert_reduce_fusion
  2.7 0.1 fusion.bias
  2.9 0.2 convert_reduce_fusion.1
  3.0 0.9 select_reduce_fusion
  3.9 0.2 select_reduce_fusion.2
  4.1 0.1 select_reduce_fusion.1
  4.2 1.2 copy-done
  5.4 1.5 %copy-done.3 = bf16[960,1024]{1,0:T(8,128)(2,1)S(1)} copy-done((bf16[960,1024]{1,0:T(8,128)(2,1)S(1)}, bf16[960,1024]{1,0:T(8,128)(2,1)}, u32[]{:S(2)}) %copy-start.3) | copy-done | bytes 1966104
  6.9 1.5 %copy-done.4 = bf16[960,1024]{1,0:T(8,128)(2,1)S(1)} copy-done((bf16[960,1024]{1,0:T(8,128)(2,1)S(1)}, bf16[960,1024]{1,0:T(8,128)(2,1)}, u32[]{:S(2)}) %copy-start.4) | copy-done | bytes 1966104
  8.5 1.5 %copy-done.5 = bf16[960,1024]{1,0:T(8,128)(2,1)S(1)} copy-done((bf16[960,1024]{1,0:T(8,128)(2,1)S(1)}, bf16[960,1024]{1,0:T(8,128)(2,1)}, u32[]{:S(2)}) %copy-start.5) | copy-done | bytes 1966104
  10.0 3.9 %shard_map.127 = (bf16[256,960]{1,0:T(8,128)(2,1)S(1)}, f32[256,1024]{1,0:T(8,128)S(1)}, f32[256,1024]{1,0:T(8,128)S(1)}, f32[256,1024]{1,0:T(8,128)S(1)}) custom-call(s32[1]{0:T(128)} %bitcast.3.at_ref, bf16[256,1920]{1,0:T(8,128)(2,1)S(1)} %copy-done, f32[1,1920]{1,0:T(1,128)S(1)} %broadcast_in_dim.71.gain, bf16[960,1024]{1,0:T(8,128)(2,1)S(1)} %copy-done.3, ...), custom_call_target="tpu_custom_call" | custom-call | flops 1509949440 | bytes 6881280 | tf_op jit(solution)/shard_map/pallas_call | solution.py:66
  14.0 0.0 collective-permute-done.2.refs_6_
  14.0 0.0 copy-start.6
  14.0 0.0 copy-start.1
  14.0 0.0 copy-start.2
  14.0 5.3 %shard_map.128.context = bf16[256,1024]{1,0:T(8,128)(2,1)S(1)} custom-call(f32[256,128]{1,0:T(8,128)S(1)} %fusion.bias, bf16[256,960]{1,0:T(8,128)(2,1)S(1)} %get-tuple-element.59.refs_0_, f32[256,1024]{1,0:T(8,128)S(1)} %get-tuple-element.60.refs_1_, f32[256,1024]{1,0:T(8,128)S(1)} %get-tuple-element.61.refs_2_, f32[256,1024]{1,0:T(8,128)S(1)} %get-tuple-element.62.refs_3_, ...), custom_call_target="tpu_custom_call" | custom-call | flops 3019898880 | bytes 9043968 | tf_op jit(solution)/shard_map/pallas_call | solution.py:122
  19.3 0.0 collective-permute-done.3.refs_1_
  19.3 0.5 collective-permute-start.12
  19.8 0.1 collective-permute-start.13
  19.9 3.6 %shard_map.129 = (bf16[256,1920]{1,0:T(8,128)(2,1)S(1)}, bf16[8,32,1920]{2,1,0:T(8,128)(2,1)}, bf16[32,1920]{1,0:T(8,128)(2,1)S(1)}, bf16[32,1920]{1,0:T(8,128)(...) custom-call(s32[1]{0:T(128)} %bitcast.3.at_ref, ...), custom_call_target="tpu_custom_call" | custom-call | flops 1006632960 | bytes 5439488 | tf_op jit(solution)/shard_map/pallas_call | solution.py:165
  23.5 6.2 %all-to-all-start = ((bf16[8,32,1920]{2,1,0:T(8,128)(2,1)}), bf16[8,32,1920]{2,1,0:T(8,128)(2,1)S(1)}, u32[]{:S(2)}, u32[]{:S(2)}) async-start(bf16[8,32,1920]{2,1,0:T(8,128)(2,1)} %get-tuple-element.70), calls=%async_computation | async-start | bytes 1966080 | tf_op jit(solution)/shard_map/all_to_all | solution.py:382
  29.7 2.6 %collective-permute-start.4 = (bf16[32,1920]{1,0:T(8,128)(2,1)S(1)}, bf16[32,1920]{1,0:T(8,128)(2,1)S(1)}, u32[]{:S(2)}, u32[]{:S(2)}) collective-permute-start(bf16[32,1920]{1,0:T(8,128)(2,1)S(1)} %get-tuple-element.71), channel_id=1, source_target_pairs={{0,16},{2,18},{4,20},{6,22},{8,24},{10,26},{12,28},{14,30},{16,0},... | collective-permute-start | bytes 368648 | tf_op jit(solution)/shard_map/ppermute | solution.py:374
  32.2 1.8 %collective-permute-start.5 = (bf16[32,1920]{1,0:T(8,128)(2,1)S(1)}, bf16[32,1920]{1,0:T(8,128)(2,1)S(1)}, u32[]{:S(2)}, u32[]{:S(2)}) collective-permute-start(bf16[32,1920]{1,0:T(8,128)(2,1)S(1)} %get-tuple-element.72), channel_id=1, source_target_pairs={{0,18},{2,16},{4,22},{6,20},{8,26},{10,24},{12,30},{14,28},{16,2},... | collective-permute-start | bytes 368648 | tf_op jit(solution)/shard_map/ppermute | solution.py:374
  34.0 3.5 %collective-permute-start.6 = (bf16[32,1920]{1,0:T(8,128)(2,1)S(1)}, bf16[32,1920]{1,0:T(8,128)(2,1)S(1)}, u32[]{:S(2)}, u32[]{:S(2)}) collective-permute-start(bf16[32,1920]{1,0:T(8,128)(2,1)S(1)} %get-tuple-element.73), channel_id=1, source_target_pairs={{0,20},{2,22},{4,16},{6,18},{8,28},{10,30},{12,24},{14,26},{16,4},... | collective-permute-start | bytes 368648 | tf_op jit(solution)/shard_map/ppermute | solution.py:374
  37.5 6.6 %collective-permute-done.4.refs_0_ = bf16[32,1920]{1,0:T(8,128)(2,1)S(1)} collective-permute-done((bf16[32,1920]{1,0:T(8,128)(2,1)S(1)}, bf16[32,1920]{1,0:T(8,128)(2,1)S(1)}, u32[]{:S(2)}, u32[]{:S(2)}) %collective-permute-start.4) | collective-permute-done | bytes 122912 | tf_op jit(solution)/shard_map/ppermute | solution.py:374
  44.1 5.8 %collective-permute-start.7 = (bf16[32,1920]{1,0:T(8,128)(2,1)S(1)}, bf16[32,1920]{1,0:T(8,128)(2,1)S(1)}, u32[]{:S(2)}, u32[]{:S(2)}) collective-permute-start(bf16[32,1920]{1,0:T(8,128)(2,1)S(1)} %get-tuple-element.74), channel_id=1, source_target_pairs={{0,22},{2,20},{4,18},{6,16},{8,30},{10,28},{12,26},{14,24},{16,6},... | collective-permute-start | bytes 368648 | tf_op jit(solution)/shard_map/ppermute | solution.py:374
  50.5 0.0 collective-permute-done.5.refs_1_
  50.6 3.7 %collective-permute-start.8 = (bf16[32,1920]{1,0:T(8,128)(2,1)}, bf16[32,1920]{1,0:T(8,128)(2,1)S(1)}, u32[]{:S(2)}, u32[]{:S(2)}) collective-permute-start(bf16[32,1920]{1,0:T(8,128)(2,1)} %get-tuple-element.79), channel_id=1, source_target_pairs={{0,24},{2,26},{4,28},{6,30},{8,16},{10,18},{12,20},{14,22},{16,8},... | collective-permute-start | bytes 368648 | tf_op jit(solution)/shard_map/ppermute | solution.py:374
  54.3 0.4 collective-permute-start.9
  54.7 10.5 %collective-permute-done.7.refs_3_ = bf16[32,1920]{1,0:T(8,128)(2,1)S(1)} collective-permute-done((bf16[32,1920]{1,0:T(8,128)(2,1)S(1)}, bf16[32,1920]{1,0:T(8,128)(2,1)S(1)}, u32[]{:S(2)}, u32[]{:S(2)}) %collective-permute-start.7) | collective-permute-done | bytes 122912 | tf_op jit(solution)/shard_map/ppermute | solution.py:374
  65.3 0.2 collective-permute-start.10
  65.5 0.0 collective-permute-done.12.refs_5_.refs_6_
  65.5 4.4 %collective-permute-start.11 = (bf16[32,1920]{1,0:T(8,128)(2,1)}, bf16[32,1920]{1,0:T(8,128)(2,1)S(1)}, u32[]{:S(2)}, u32[]{:S(2)}) collective-permute-start(bf16[32,1920]{1,0:T(8,128)(2,1)} %get-tuple-element.82), channel_id=1, source_target_pairs={{0,30},{2,28},{4,26},{6,24},{8,22},{10,20},{12,18},{14,16},{16,14}... | collective-permute-start | bytes 368648 | tf_op jit(solution)/shard_map/ppermute | solution.py:374
  69.9 0.0 collective-permute-done.13.refs_7_.refs_8_
  69.9 14.9 %shard_map.130 = (bf16[32,1920]{1,0:T(8,128)(2,1)S(1)}, bf16[32,1920]{1,0:T(8,128)(2,1)S(1)}, bf16[32,1920]{1,0:T(8,128)(2,1)S(1)}, bf16[32,1920]{1,0:T(8,128)(2,1)S(1)}) custom-call(s32[1]{0:T(128)} %constant.38.clone.1.live, bf16[32,1920]{1,0:T(8,128)(2,1)S(1)} %collective-permute-done.4.refs_0_, bf16[32,1920]{1,0:T(8,128)(2,1)S(1)} %collective-permute-done.5.refs_1_, ...), custom_call_target="tpu_custom_call" | custom-call | flops 4026531840 | bytes 31457280 | tf_op jit(solution)/shard_map/pallas_call | solution.py:279
  84.9 0.0 collective-permute-done.8.refs_4_.refs_1_
  84.9 0.0 collective-permute-done.9.refs_5_.refs_2_
  84.9 0.0 collective-permute-done.11.refs_7_.refs_4_
  84.9 0.0 all-to-all-done.near
  84.9 1.2 shard_map.131
  86.1 0.1 collective-permute-start.14
  86.2 3.9 %collective-permute-start.15 = (bf16[32,1920]{1,0:T(8,128)(2,1)S(1)}, bf16[32,1920]{1,0:T(8,128)(2,1)S(1)}, u32[]{:S(2)}, u32[]{:S(2)}) collective-permute-start(bf16[32,1920]{1,0:T(8,128)(2,1)S(1)} %get-tuple-element.91), channel_id=1, source_target_pairs={{0,18},{2,16},{4,22},{6,20},{8,26},{10,24},{12,30},{14,28},{16,2},... | collective-permute-start | bytes 368648 | tf_op jit(solution)/shard_map/ppermute | solution.py:374
  90.1 0.1 collective-permute-start.16
  90.2 3.7 %collective-permute-start.17 = (bf16[32,1920]{1,0:T(8,128)(2,1)S(1)}, bf16[32,1920]{1,0:T(8,128)(2,1)S(1)}, u32[]{:S(2)}, u32[]{:S(2)}) collective-permute-start(bf16[32,1920]{1,0:T(8,128)(2,1)S(1)} %get-tuple-element.93), channel_id=1, source_target_pairs={{0,22},{2,20},{4,18},{6,16},{8,30},{10,28},{12,26},{14,24},{16,6},... | collective-permute-start | bytes 368648 | tf_op jit(solution)/shard_map/ppermute | solution.py:374
  93.8 20.8 %shard_map.132 = (bf16[256,1920]{1,0:T(8,128)(2,1)}, bf16[32,1920]{1,0:T(8,128)(2,1)}, bf16[32,1920]{1,0:T(8,128)(2,1)}, bf16[32,1920]{1,0:T(8,128)(2,1)S(1)}, bf16[32,1920]{1,0:T(8,128)(2,1)S(1)}) custom-call(s32[16]{0:T(128)S(1)} %get-tuple-element.89.live, bf16[256,1920]{1,0:T(8,128)(2,1)S(1)} %bitcast.12, ...), custom_call_target="tpu_custom_call" | custom-call | flops 12079595520 | bytes 31457280 | tf_op jit(solution)/shard_map/pallas_call | solution.py:279
  114.6 0.0 collective-permute-done.14.refs_0_
  114.6 0.0 collective-permute-done.15.refs_1_
  114.7 3.6 %all-to-all-start.1 = ((bf16[8,32,1920]{2,1,0:T(8,128)(2,1)}), bf16[8,32,1920]{2,1,0:T(8,128)(2,1)S(1)}, u32[]{:S(2)}, u32[]{:S(2)}) async-start(bf16[8,32,1920]{2,1,0:T(8,128)(2,1)} %bitcast.8), calls=%async_computation.1 | async-start | bytes 1966080 | tf_op jit(solution)/shard_map/all_to_all | solution.py:382
  118.3 1.5 %collective-permute-start.18 = (bf16[32,1920]{1,0:T(8,128)(2,1)}, bf16[32,1920]{1,0:T(8,128)(2,1)S(1)}, u32[]{:S(2)}, u32[]{:S(2)}) collective-permute-start(bf16[32,1920]{1,0:T(8,128)(2,1)} %get-tuple-element.105), channel_id=1, source_target_pairs={{0,24},{2,26},{4,28},{6,30},{8,16},{10,18},{12,20},{14,22},{16,8},... | collective-permute-start | bytes 368648 | tf_op jit(solution)/shard_map/ppermute | solution.py:374
  119.7 3.7 %collective-permute-start.19 = (bf16[32,1920]{1,0:T(8,128)(2,1)}, bf16[32,1920]{1,0:T(8,128)(2,1)S(1)}, u32[]{:S(2)}, u32[]{:S(2)}) collective-permute-start(bf16[32,1920]{1,0:T(8,128)(2,1)} %get-tuple-element.106), channel_id=1, source_target_pairs={{0,26},{2,24},{4,30},{6,28},{8,18},{10,16},{12,22},{14,20},{16,10}... | collective-permute-start | bytes 368648 | tf_op jit(solution)/shard_map/ppermute | solution.py:374
  123.4 1.9 %collective-permute-start.20 = (bf16[32,1920]{1,0:T(8,128)(2,1)S(1)}, bf16[32,1920]{1,0:T(8,128)(2,1)S(1)}, u32[]{:S(2)}, u32[]{:S(2)}) collective-permute-start(bf16[32,1920]{1,0:T(8,128)(2,1)S(1)} %get-tuple-element.107), channel_id=1, source_target_pairs={{0,28},{2,30},{4,24},{6,26},{8,20},{10,22},{12,16},{14,18},{16,12}... | collective-permute-start | bytes 368648 | tf_op jit(solution)/shard_map/ppermute | solution.py:374
  125.4 2.4 %collective-permute-start.21 = (bf16[32,1920]{1,0:T(8,128)(2,1)S(1)}, bf16[32,1920]{1,0:T(8,128)(2,1)S(1)}, u32[]{:S(2)}, u32[]{:S(2)}) collective-permute-start(bf16[32,1920]{1,0:T(8,128)(2,1)S(1)} %get-tuple-element.108), channel_id=1, source_target_pairs={{0,30},{2,28},{4,26},{6,24},{8,22},{10,20},{12,18},{14,16},{16,14}... | collective-permute-start | bytes 368648 | tf_op jit(solution)/shard_map/ppermute | solution.py:374
  127.8 7.6 %collective-permute-done.18.refs_4_ = bf16[32,1920]{1,0:T(8,128)(2,1)S(1)} collective-permute-done((bf16[32,1920]{1,0:T(8,128)(2,1)}, bf16[32,1920]{1,0:T(8,128)(2,1)S(1)}, u32[]{:S(2)}, u32[]{:S(2)}) %collective-permute-start.18) | collective-permute-done | bytes 122912 | tf_op jit(solution)/shard_map/ppermute | solution.py:374
  135.4 4.1 %collective-permute-done.19.refs_5_ = bf16[32,1920]{1,0:T(8,128)(2,1)S(1)} collective-permute-done((bf16[32,1920]{1,0:T(8,128)(2,1)}, bf16[32,1920]{1,0:T(8,128)(2,1)S(1)}, u32[]{:S(2)}, u32[]{:S(2)}) %collective-permute-start.19) | collective-permute-done | bytes 122912 | tf_op jit(solution)/shard_map/ppermute | solution.py:374
  139.5 1.5 %collective-permute-done.20.refs_6_ = bf16[32,1920]{1,0:T(8,128)(2,1)S(1)} collective-permute-done((bf16[32,1920]{1,0:T(8,128)(2,1)S(1)}, bf16[32,1920]{1,0:T(8,128)(2,1)S(1)}, u32[]{:S(2)}, u32[]{:S(2)}) %collective-permute-start.20) | collective-permute-done | bytes 122912 | tf_op jit(solution)/shard_map/ppermute | solution.py:374
  141.0 2.3 %collective-permute-done.21.refs_7_ = bf16[32,1920]{1,0:T(8,128)(2,1)S(1)} collective-permute-done((bf16[32,1920]{1,0:T(8,128)(2,1)S(1)}, bf16[32,1920]{1,0:T(8,128)(2,1)S(1)}, u32[]{:S(2)}, u32[]{:S(2)}) %collective-permute-start.21) | collective-permute-done | bytes 122912 | tf_op jit(solution)/shard_map/ppermute | solution.py:374
  143.3 1.9 %shard_map.133 = bf16[256,1920]{1,0:T(8,128)(2,1)} custom-call(s32[16]{0:T(128)S(1)} %broadcast_subtract_fusion.run_ref, bf16[256,1920]{1,0:T(8,128)(2,1)S(1)} %get-tuple-element.69.hidden, bf16[8,32,1920]{2,1,0:T(8,128)(2,1)S(1)} %all-to-all-done.1.near, bf16[32,1920]{1,0:T(8,128)(2,1)S(1)} %collective-permute-done.14.refs_0_, ...), custom_call_target="tpu_custom_call" | custom-call | tf_op jit(solution)/shard_map/pallas_call | solution.py:194
  (20 shorter events, 0.1 us)
Async XLA Ops:
  0.0 13.9 %collective-permute-start = (bf16[960,1024]{1,0:T(8,128)(2,1)}, bf16[960,1024]{1,0:T(8,128)(2,1)}, u32[]{:S(2)}, u32[]{:S(2)}) collective-permute-start(bf16[960,1024]{1,0:T(8,128)(2,1)} %refs_0_.1), channel_id=1, source_target_pairs={{0,1},{1,0},{2,3},{3,2},{4,5},{5,4},{6,7},{7,6},{8,9},{9,8},{10,11... | collective-permute-start | bytes 5898248 | tf_op jit(solution)/shard_map/ppermute | solution.py:325
  0.5 13.5 %collective-permute-start.1 = (bf16[960,1024]{1,0:T(8,128)(2,1)}, bf16[960,1024]{1,0:T(8,128)(2,1)}, u32[]{:S(2)}, u32[]{:S(2)}) collective-permute-start(bf16[960,1024]{1,0:T(8,128)(2,1)} %refs_1_.1), channel_id=1, source_target_pairs={{0,1},{1,0},{2,3},{3,2},{4,5},{5,4},{6,7},{7,6},{8,9},{9,8},{10,11... | collective-permute-start | bytes 5898248 | tf_op jit(solution)/shard_map/ppermute | solution.py:325
  0.5 13.5 %collective-permute-start.2 = (bf16[960,1024]{1,0:T(8,128)(2,1)}, bf16[960,1024]{1,0:T(8,128)(2,1)}, u32[]{:S(2)}, u32[]{:S(2)}) collective-permute-start(bf16[960,1024]{1,0:T(8,128)(2,1)} %refs_2_.1), channel_id=1, source_target_pairs={{0,1},{1,0},{2,3},{3,2},{4,5},{5,4},{6,7},{7,6},{8,9},{9,8},{10,11... | collective-permute-start | bytes 5898248 | tf_op jit(solution)/shard_map/ppermute | solution.py:325
  1.0 18.3 %collective-permute-start.3 = (bf16[512,1920]{1,0:T(8,128)(2,1)}, bf16[512,1920]{1,0:T(8,128)(2,1)S(1)}, u32[]{:S(2)}, u32[]{:S(2)}) collective-permute-start(bf16[512,1920]{1,0:T(8,128)(2,1)} %refs_0_.2), channel_id=1, source_target_pairs={{0,1},{1,0},{2,3},{3,2},{4,5},{5,4},{6,7},{7,6},{8,9},{9,8},{10,11... | collective-permute-start | bytes 5898248 | tf_op jit(solution)/shard_map/ppermute | solution.py:325
  4.2 1.2 copy-start
  5.4 1.5 %copy-start.3 = (bf16[960,1024]{1,0:T(8,128)(2,1)S(1)}, bf16[960,1024]{1,0:T(8,128)(2,1)}, u32[]{:S(2)}) copy-start(bf16[960,1024]{1,0:T(8,128)(2,1)} %refs_0_.1) | copy-start | bytes 5898244
  6.9 1.5 %copy-start.4 = (bf16[960,1024]{1,0:T(8,128)(2,1)S(1)}, bf16[960,1024]{1,0:T(8,128)(2,1)}, u32[]{:S(2)}) copy-start(bf16[960,1024]{1,0:T(8,128)(2,1)} %refs_1_.1) | copy-start | bytes 5898244
  8.5 1.5 %copy-start.5 = (bf16[960,1024]{1,0:T(8,128)(2,1)S(1)}, bf16[960,1024]{1,0:T(8,128)(2,1)}, u32[]{:S(2)}) copy-start(bf16[960,1024]{1,0:T(8,128)(2,1)} %refs_2_.1) | copy-start | bytes 5898244
  14.0 5.9 %copy-start.6 = (f32[1920]{0:T(1024)S(1)}, f32[1920]{0:T(1024)}, u32[]{:S(2)}) copy-start(f32[1920]{0:T(1024)} %param.23) | copy-start | bytes 23044
  14.0 5.9 %copy-start.1 = (bf16[256,1920]{1,0:T(8,128)(2,1)S(1)}, bf16[256,1920]{1,0:T(8,128)(2,1)}, u32[]{:S(2)}) copy-start(bf16[256,1920]{1,0:T(8,128)(2,1)} %tokens.3) | copy-start | bytes 2949124
  14.0 5.9 %copy-start.2 = (bf16[512,1920]{1,0:T(8,128)(2,1)S(1)}, bf16[512,1920]{1,0:T(8,128)(2,1)}, u32[]{:S(2)}) copy-start(bf16[512,1920]{1,0:T(8,128)(2,1)} %refs_0_.2) | copy-start | bytes 5898244
  19.3 46.2 %collective-permute-start.12 = (bf16[1920,2048]{1,0:T(8,128)(2,1)}, bf16[1920,2048]{1,0:T(8,128)(2,1)}, u32[]{:S(2)}, u32[]{:S(2)}) collective-permute-start(bf16[1920,2048]{1,0:T(8,128)(2,1)} %bitcast.4.refs_4_.refs_5_), channel_id=1, source_target_pairs={{0,1},{1,0},{2,3},{3,2},{4,5},{5,4},{6,7},{7,6},{8,9},{9,8},{10,11... | collective-permute-start | bytes 23592968 | tf_op jit(solution)/shard_map/ppermute | solution.py:325
  19.8 50.1 %collective-permute-start.13 = (bf16[2048,1920]{1,0:T(8,128)(2,1)}, bf16[2048,1920]{1,0:T(8,128)(2,1)}, u32[]{:S(2)}, u32[]{:S(2)}) collective-permute-start(bf16[2048,1920]{1,0:T(8,128)(2,1)} %bitcast.5.refs_6_.refs_7_), channel_id=1, source_target_pairs={{0,1},{1,0},{2,3},{3,2},{4,5},{5,4},{6,7},{7,6},{8,9},{9,8},{10,11... | collective-permute-start | bytes 23592968 | tf_op jit(solution)/shard_map/ppermute | solution.py:325
  23.5 61.4 %all-to-all-start = ((bf16[8,32,1920]{2,1,0:T(8,128)(2,1)}), bf16[8,32,1920]{2,1,0:T(8,128)(2,1)S(1)}, u32[]{:S(2)}, u32[]{:S(2)}) async-start(bf16[8,32,1920]{2,1,0:T(8,128)(2,1)} %get-tuple-element.70), calls=%async_computation | async-start | bytes 1966080 | tf_op jit(solution)/shard_map/all_to_all | solution.py:382
  29.7 14.4 %collective-permute-start.4 = (bf16[32,1920]{1,0:T(8,128)(2,1)S(1)}, bf16[32,1920]{1,0:T(8,128)(2,1)S(1)}, u32[]{:S(2)}, u32[]{:S(2)}) collective-permute-start(bf16[32,1920]{1,0:T(8,128)(2,1)S(1)} %get-tuple-element.71), channel_id=1, source_target_pairs={{0,16},{2,18},{4,20},{6,22},{8,24},{10,26},{12,28},{14,30},{16,0},... | collective-permute-start | bytes 368648 | tf_op jit(solution)/shard_map/ppermute | solution.py:374
  32.2 18.3 %collective-permute-start.5 = (bf16[32,1920]{1,0:T(8,128)(2,1)S(1)}, bf16[32,1920]{1,0:T(8,128)(2,1)S(1)}, u32[]{:S(2)}, u32[]{:S(2)}) collective-permute-start(bf16[32,1920]{1,0:T(8,128)(2,1)S(1)} %get-tuple-element.72), channel_id=1, source_target_pairs={{0,18},{2,16},{4,22},{6,20},{8,26},{10,24},{12,30},{14,28},{16,2},... | collective-permute-start | bytes 368648 | tf_op jit(solution)/shard_map/ppermute | solution.py:374
  34.0 16.5 %collective-permute-start.6 = (bf16[32,1920]{1,0:T(8,128)(2,1)S(1)}, bf16[32,1920]{1,0:T(8,128)(2,1)S(1)}, u32[]{:S(2)}, u32[]{:S(2)}) collective-permute-start(bf16[32,1920]{1,0:T(8,128)(2,1)S(1)} %get-tuple-element.73), channel_id=1, source_target_pairs={{0,20},{2,22},{4,16},{6,18},{8,28},{10,30},{12,24},{14,26},{16,4},... | collective-permute-start | bytes 368648 | tf_op jit(solution)/shard_map/ppermute | solution.py:374
  44.1 21.2 %collective-permute-start.7 = (bf16[32,1920]{1,0:T(8,128)(2,1)S(1)}, bf16[32,1920]{1,0:T(8,128)(2,1)S(1)}, u32[]{:S(2)}, u32[]{:S(2)}) collective-permute-start(bf16[32,1920]{1,0:T(8,128)(2,1)S(1)} %get-tuple-element.74), channel_id=1, source_target_pairs={{0,22},{2,20},{4,18},{6,16},{8,30},{10,28},{12,26},{14,24},{16,6},... | collective-permute-start | bytes 368648 | tf_op jit(solution)/shard_map/ppermute | solution.py:374
  50.6 34.3 %collective-permute-start.8 = (bf16[32,1920]{1,0:T(8,128)(2,1)}, bf16[32,1920]{1,0:T(8,128)(2,1)S(1)}, u32[]{:S(2)}, u32[]{:S(2)}) collective-permute-start(bf16[32,1920]{1,0:T(8,128)(2,1)} %get-tuple-element.79), channel_id=1, source_target_pairs={{0,24},{2,26},{4,28},{6,30},{8,16},{10,18},{12,20},{14,22},{16,8},... | collective-permute-start | bytes 368648 | tf_op jit(solution)/shard_map/ppermute | solution.py:374
  54.3 30.6 %collective-permute-start.9 = (bf16[32,1920]{1,0:T(8,128)(2,1)}, bf16[32,1920]{1,0:T(8,128)(2,1)S(1)}, u32[]{:S(2)}, u32[]{:S(2)}) collective-permute-start(bf16[32,1920]{1,0:T(8,128)(2,1)} %get-tuple-element.80), channel_id=1, source_target_pairs={{0,26},{2,24},{4,30},{6,28},{8,18},{10,16},{12,22},{14,20},{16,10}... | collective-permute-start | bytes 368648 | tf_op jit(solution)/shard_map/ppermute | solution.py:374
  65.3 19.6 %collective-permute-start.10 = (bf16[32,1920]{1,0:T(8,128)(2,1)}, bf16[32,1920]{1,0:T(8,128)(2,1)S(1)}, u32[]{:S(2)}, u32[]{:S(2)}) collective-permute-start(bf16[32,1920]{1,0:T(8,128)(2,1)} %get-tuple-element.81), channel_id=1, source_target_pairs={{0,28},{2,30},{4,24},{6,26},{8,20},{10,22},{12,16},{14,18},{16,12}... | collective-permute-start | bytes 368648 | tf_op jit(solution)/shard_map/ppermute | solution.py:374
  65.5 19.4 %collective-permute-start.11 = (bf16[32,1920]{1,0:T(8,128)(2,1)}, bf16[32,1920]{1,0:T(8,128)(2,1)S(1)}, u32[]{:S(2)}, u32[]{:S(2)}) collective-permute-start(bf16[32,1920]{1,0:T(8,128)(2,1)} %get-tuple-element.82), channel_id=1, source_target_pairs={{0,30},{2,28},{4,26},{6,24},{8,22},{10,20},{12,18},{14,16},{16,14}... | collective-permute-start | bytes 368648 | tf_op jit(solution)/shard_map/ppermute | solution.py:374
  86.1 28.5 %collective-permute-start.14 = (bf16[32,1920]{1,0:T(8,128)(2,1)S(1)}, bf16[32,1920]{1,0:T(8,128)(2,1)S(1)}, u32[]{:S(2)}, u32[]{:S(2)}) collective-permute-start(bf16[32,1920]{1,0:T(8,128)(2,1)S(1)} %get-tuple-element.90), channel_id=1, source_target_pairs={{0,16},{2,18},{4,20},{6,22},{8,24},{10,26},{12,28},{14,30},{16,0},... | collective-permute-start | bytes 368648 | tf_op jit(solution)/shard_map/ppermute | solution.py:374
  86.2 28.5 %collective-permute-start.15 = (bf16[32,1920]{1,0:T(8,128)(2,1)S(1)}, bf16[32,1920]{1,0:T(8,128)(2,1)S(1)}, u32[]{:S(2)}, u32[]{:S(2)}) collective-permute-start(bf16[32,1920]{1,0:T(8,128)(2,1)S(1)} %get-tuple-element.91), channel_id=1, source_target_pairs={{0,18},{2,16},{4,22},{6,20},{8,26},{10,24},{12,30},{14,28},{16,2},... | collective-permute-start | bytes 368648 | tf_op jit(solution)/shard_map/ppermute | solution.py:374
  90.1 24.6 %collective-permute-start.16 = (bf16[32,1920]{1,0:T(8,128)(2,1)S(1)}, bf16[32,1920]{1,0:T(8,128)(2,1)S(1)}, u32[]{:S(2)}, u32[]{:S(2)}) collective-permute-start(bf16[32,1920]{1,0:T(8,128)(2,1)S(1)} %get-tuple-element.92), channel_id=1, source_target_pairs={{0,20},{2,22},{4,16},{6,18},{8,28},{10,30},{12,24},{14,26},{16,4},... | collective-permute-start | bytes 368648 | tf_op jit(solution)/shard_map/ppermute | solution.py:374
  90.2 24.5 %collective-permute-start.17 = (bf16[32,1920]{1,0:T(8,128)(2,1)S(1)}, bf16[32,1920]{1,0:T(8,128)(2,1)S(1)}, u32[]{:S(2)}, u32[]{:S(2)}) collective-permute-start(bf16[32,1920]{1,0:T(8,128)(2,1)S(1)} %get-tuple-element.93), channel_id=1, source_target_pairs={{0,22},{2,20},{4,18},{6,16},{8,30},{10,28},{12,26},{14,24},{16,6},... | collective-permute-start | bytes 368648 | tf_op jit(solution)/shard_map/ppermute | solution.py:374
  114.7 28.6 %all-to-all-start.1 = ((bf16[8,32,1920]{2,1,0:T(8,128)(2,1)}), bf16[8,32,1920]{2,1,0:T(8,128)(2,1)S(1)}, u32[]{:S(2)}, u32[]{:S(2)}) async-start(bf16[8,32,1920]{2,1,0:T(8,128)(2,1)} %bitcast.8), calls=%async_computation.1 | async-start | bytes 1966080 | tf_op jit(solution)/shard_map/all_to_all | solution.py:382
  118.3 17.1 %collective-permute-start.18 = (bf16[32,1920]{1,0:T(8,128)(2,1)}, bf16[32,1920]{1,0:T(8,128)(2,1)S(1)}, u32[]{:S(2)}, u32[]{:S(2)}) collective-permute-start(bf16[32,1920]{1,0:T(8,128)(2,1)} %get-tuple-element.105), channel_id=1, source_target_pairs={{0,24},{2,26},{4,28},{6,30},{8,16},{10,18},{12,20},{14,22},{16,8},... | collective-permute-start | bytes 368648 | tf_op jit(solution)/shard_map/ppermute | solution.py:374
  119.7 19.7 %collective-permute-start.19 = (bf16[32,1920]{1,0:T(8,128)(2,1)}, bf16[32,1920]{1,0:T(8,128)(2,1)S(1)}, u32[]{:S(2)}, u32[]{:S(2)}) collective-permute-start(bf16[32,1920]{1,0:T(8,128)(2,1)} %get-tuple-element.106), channel_id=1, source_target_pairs={{0,26},{2,24},{4,30},{6,28},{8,18},{10,16},{12,22},{14,20},{16,10}... | collective-permute-start | bytes 368648 | tf_op jit(solution)/shard_map/ppermute | solution.py:374
  123.4 17.5 %collective-permute-start.20 = (bf16[32,1920]{1,0:T(8,128)(2,1)S(1)}, bf16[32,1920]{1,0:T(8,128)(2,1)S(1)}, u32[]{:S(2)}, u32[]{:S(2)}) collective-permute-start(bf16[32,1920]{1,0:T(8,128)(2,1)S(1)} %get-tuple-element.107), channel_id=1, source_target_pairs={{0,28},{2,30},{4,24},{6,26},{8,20},{10,22},{12,16},{14,18},{16,12}... | collective-permute-start | bytes 368648 | tf_op jit(solution)/shard_map/ppermute | solution.py:374
  125.4 17.9 %collective-permute-start.21 = (bf16[32,1920]{1,0:T(8,128)(2,1)S(1)}, bf16[32,1920]{1,0:T(8,128)(2,1)S(1)}, u32[]{:S(2)}, u32[]{:S(2)}) collective-permute-start(bf16[32,1920]{1,0:T(8,128)(2,1)S(1)} %get-tuple-element.108), channel_id=1, source_target_pairs={{0,30},{2,28},{4,26},{6,24},{8,22},{10,20},{12,18},{14,16},{16,14}... | collective-permute-start | bytes 368648 | tf_op jit(solution)/shard_map/ppermute | solution.py:374

commit v4 on v3

--- a/solution.py
+++ b/solution.py
@@ -9,7 +9,7 @@
 
 HDIM = 128
 BLOCK = 128
-VMEM_LIMIT = 30 * 1024 * 1024
+VMEM_LIMIT = 42 * 1024 * 1024
 FRONT_LIMIT = 24 * 1024 * 1024
 
 EMPTY = 1024.0
@@ -39,13 +39,8 @@
 
 def project_kernel(pieces, at_ref, tokens, gain, *refs):
     weights, rest, sums = refs[:3], refs[3 : 2 + pieces], refs[2 + pieces : 5 + pieces]
-    own, held, arrived = refs[-3:]
+    own = refs[-1]
     part = own.shape[1]
-    copies = [
-        pltpu.make_async_copy(weight, held.at[n], arrived.at[n]) for n, weight in enumerate(weights)
-    ]
-    for copy in copies:
-        copy.start()
     normed = layer_norm(tokens[...], gain[...]).astype(jnp.bfloat16)
     for v in range(pieces):
 
@@ -55,9 +50,8 @@
                 first = (v - s) % pieces * part
                 ref[...] = normed[:, first : first + part]
 
-    for n, total in enumerate(sums):
-        copies[n].wait()
-        total[...] = dot(own[...], held[n])
+    for weight, total in zip(weights, sums):
+        total[...] = dot(own[...], weight[...])
 
 
 def project(at, tokens, gain, weights, pieces):
@@ -66,16 +60,11 @@
     out = pl.pallas_call(
         functools.partial(project_kernel, pieces),
         in_specs=[pl.BlockSpec(memory_space=pltpu.SMEM)]
-        + in_vmem(2)
-        + [pl.BlockSpec(memory_space=pltpu.HBM)] * 3,
+        + in_vmem(5),
         out_specs=in_vmem(pieces + 2),
         out_shape=[jax.ShapeDtypeStruct((count, part), jnp.bfloat16)] * (pieces - 1)
         + [jax.ShapeDtypeStruct((count, wide), jnp.float32)] * 3,
-        scratch_shapes=[
-            pltpu.VMEM((count, part), jnp.bfloat16),
-            pltpu.VMEM((3, part, wide), jnp.bfloat16),
-            pltpu.SemaphoreType.DMA((3,)),
-        ],
+        scratch_shapes=[pltpu.VMEM((count, part), jnp.bfloat16)],
         compiler_params=pltpu.CompilerParams(vmem_limit_bytes=FRONT_LIMIT),
         cost_estimate=cost(3 * count * part * wide, tokens, *weights),
     )(at, tokens, gain, *weights)
@@ -201,7 +190,7 @@
 
 
 def live_kernel(first, at_ref, blocks_ref, near, *refs):
-    count = (len(refs) - 1 - 2 * first)
+    count = len(refs) - 1 - 2 * first
     far, results, outs, live = refs[:count], refs[count : count + first], refs[-1 - first : -1], refs[-1]
     half, rows = near.shape[:2]
     me = at_ref[0]
@@ -212,8 +201,12 @@
     for k in range(half + len(far)):
         before = sum(jnp.where(s < source[k], f, 0) for s, f in zip(source, full))
         live[k] = (before * rows // BLOCK < blocks_ref[0, 0]).astype(jnp.int32)
-    for k in range(first):
-        kept = live[half + k] > 0
+    for k in range(half):
+        part = slice(k * rows, (k + 1) * rows)
+        kept = live[k] > 0
+        outs[0][k] = jnp.where(kept, results[0][part, :], jnp.zeros_like(outs[0][k]))
+    for k in range(1, first):
+        kept = live[half + k - 1] > 0
         outs[k][...] = jnp.where(kept, results[k][...], jnp.zeros_like(results[k]))
 
 
@@ -224,7 +217,7 @@
         functools.partial(live_kernel, first),
         in_specs=[smem] * 2 + in_vmem(1 + len(far) + first),
         out_specs=in_vmem(first) + [smem],
-        out_shape=[jax.ShapeDtypeStruct(r.shape, r.dtype) for r in results]
+        out_shape=[jax.ShapeDtypeStruct(r.shape, r.dtype) for r in (near, *results[1:])]
         + [jax.ShapeDtypeStruct((near.shape[0] + len(far),), jnp.int32)],
         compiler_params=pltpu.CompilerParams(vmem_limit_bytes=FRONT_LIMIT),
     )(at, blocks, near, *far, *results)
@@ -268,7 +261,8 @@
     pieces, (width, hidden) = len(first), first[0].shape
     sizes = [a.shape[0] for a in ins]
     rows = sum(sizes)
-    chunk = 512 if hidden % 512 == 0 else hidden
+    chunk = 1024 if rows <= 256 else 512
+    chunk = chunk if hidden % chunk == 0 else hidden
     per = hidden // chunk
     if live is None:
         live, slots = jnp.zeros((1,), jnp.int32), [[]] * len(ins)
@@ -386,20 +380,22 @@
         def after(arrays, *done):
             return list(lax.optimization_barrier((tuple(arrays), done))[0])
 
-        quarter = half // 2
+        quarter = half * 3 // 8
         far, last = range(half, half + quarter), range(half + quarter, lang_count)
+        far_in = swap(far, slots[1 : 1 + quarter])
         near_in = within(slots[0])
-        far_in = swap(far, slots[1 : 1 + quarter])
-        last_in = swap(last, after(slots[1 + quarter :], *far_in[:3]))
-        far_out = expert_ffn(far_in, first, second)
-        far_out, live = live_rows(lang_scalar, blocks, near_in, [*far_in, *last_in], far_out)
-        ins = after([near_in.reshape(half * capacity, width), *last_in], far_out)
+        last_in = []
+        for n, k in enumerate(last):
+            done = far_in[min(n, quarter - 1)]
+            last_in += swap([k], after([slots[1 + quarter + n]], done))
+        ins = [near_in.reshape(half * capacity, width), *far_in]
+        out = expert_ffn(ins, first, second)
+        (near_out, *far_out), live = live_rows(lang_scalar, blocks, near_in, [*far_in, *last_in], out)
+        last_in = after(last_in, far_out)
         far_back = swap(far, far_out)
-        held = [list(range(half)), *[[k] for k in last]]
-        near_out, *last_out = expert_ffn(ins, first, second, live, held)
-        near_out, *last_out = after([near_out, *last_out], far_back)
-        last_back = swap(last, last_out)
-        near_back = within(near_out.reshape(half, capacity, width))
+        near_back = within(near_out)
+        last_out = expert_ffn(last_in, first, second, live, [[k] for k in last])
+        last_back = swap(last, after(last_out, far_back))
         return mix(run_of_slot, hidden, near_back, far_back + last_back, slots_dev)
 
     dispatch = (group_ids[:, None] == run_group[None, :]).astype(jnp.bfloat16)

time: 146 us -> 136 us (0.932)
  the two profiles are of different devices: /device:TPU:0 before, /device:TPU:16 now
where the time goes in v4:
time: 136 us
  Pallas kernels  48.1 us (35%)
  starting transfers between devices  40.3 us (30%)
  waiting for transfers between devices  35.5 us (26%)
  local copies, waits for them, and re-layouts  9.22 us (7%)
  other arithmetic  1.68 us (1%)
    ppermute x16, waiting for transfers between devices, swap(): lax.ppermute(a, 'lang', [(i, i ^ k) for i in range(lang_count)])  35.5 us
    pallas_call x2, Pallas kernels, expert_ffn(): pl.pallas_call(functools.partial(expert_kernel, sizes, pieces, per, slots...  33.5 us
    ppermute x16, starting transfers between devices, swap(): lax.ppermute(a, 'lang', [(i, i ^ k) for i in range(lang_count)])  30.1 us
    all_to_all x2, starting transfers between devices, within(): lax.all_to_all(array, 'lang', 0, 0, axis_index_groups=halves, tiled=True)  8.62 us
    unnamed x26, local copies, waits for them, and re-layouts  7.78 us
    pallas_call x1, Pallas kernels, attend(): pl.pallas_call(functools.partial(attend_kernel, len(rest)), in_specs=in_v...  5.28 us
    pallas_call x1, Pallas kernels, hidden_states(): pl.pallas_call(functools.partial(hidden_kernel, len(weights), runs, slots...  3.44 us
  transfers between devices with their start and end apart: 24, of which 9 were waited for; matrix products, arithmetic and copies ran while one was open for 2% of the time, Pallas kernels for 33%

profile of v4, /device:TPU:16, one launch (start us, length us, event | category | flops | bytes accessed | tf_op | source)
XLA Modules:
  0.0 135.7 jit_solution(6601411120959653118)
XLA Ops:
  0.0 0.5 collective-permute-start.1
  0.5 0.0 collective-permute-start.2
  0.5 0.5 collective-permute-start.3
  1.0 0.7 broadcast_in_dim.71.gain
  1.7 0.7 copy.16
  2.5 0.1 reduce
  2.6 0.1 convert_reduce_fusion
  2.7 0.1 fusion.bias
  2.9 0.2 convert_reduce_fusion.1
  3.0 0.9 select_reduce_fusion
  3.9 0.2 select_reduce_fusion.2
  4.1 0.1 select_reduce_fusion.1
  4.2 1.2 copy-done
  5.4 1.5 %copy-done.3 = bf16[960,1024]{1,0:T(8,128)(2,1)S(1)} copy-done((bf16[960,1024]{1,0:T(8,128)(2,1)S(1)}, bf16[960,1024]{1,0:T(8,128)(2,1)}, u32[]{:S(2)}) %copy-start.3) | copy-done | bytes 1966104
  6.9 1.5 %copy-done.4 = bf16[960,1024]{1,0:T(8,128)(2,1)S(1)} copy-done((bf16[960,1024]{1,0:T(8,128)(2,1)S(1)}, bf16[960,1024]{1,0:T(8,128)(2,1)}, u32[]{:S(2)}) %copy-start.4) | copy-done | bytes 1966104
  8.5 1.5 %copy-done.5 = bf16[960,1024]{1,0:T(8,128)(2,1)S(1)} copy-done((bf16[960,1024]{1,0:T(8,128)(2,1)S(1)}, bf16[960,1024]{1,0:T(8,128)(2,1)}, u32[]{:S(2)}) %copy-start.5) | copy-done | bytes 1966104
  10.0 2.7 %shard_map.127 = (bf16[256,960]{1,0:T(8,128)(2,1)S(1)}, f32[256,1024]{1,0:T(8,128)S(1)}, f32[256,1024]{1,0:T(8,128)S(1)}, f32[256,1024]{1,0:T(8,128)S(1)}) custom-call(s32[1]{0:T(128)} %bitcast.3.at_ref, bf16[256,1920]{1,0:T(8,128)(2,1)S(1)} %copy-done, f32[1,1920]{1,0:T(1,128)S(1)} %broadcast_in_dim.71.gain, bf16[960,1024]{1,0:T(8,128)(2,1)S(1)} %copy-done.3, ...), custom_call_target="tpu_custom_call" | custom-call | flops 1509949440 | bytes 6881280 | tf_op jit(solution)/shard_map/pallas_call | solution.py:60
  12.7 0.0 collective-permute-done.refs_4_
  12.7 0.0 collective-permute-done.1.refs_5_
  12.7 0.0 collective-permute-done.2.refs_6_
  12.8 0.0 copy-start.2
  12.8 5.3 %shard_map.128.context = bf16[256,1024]{1,0:T(8,128)(2,1)S(1)} custom-call(f32[256,128]{1,0:T(8,128)S(1)} %fusion.bias, bf16[256,960]{1,0:T(8,128)(2,1)S(1)} %get-tuple-element.60.refs_0_, f32[256,1024]{1,0:T(8,128)S(1)} %get-tuple-element.61.refs_1_, f32[256,1024]{1,0:T(8,128)S(1)} %get-tuple-element.62.refs_2_, f32[256,1024]{1,0:T(8,128)S(1)} %get-tuple-element.63.refs_3_, ...), custom_call_target="tpu_custom_call" | custom-call | flops 3019898880 | bytes 9043968 | tf_op jit(solution)/shard_map/pallas_call | solution.py:111
  18.1 0.2 collective-permute-start.12
  18.3 0.4 collective-permute-start.13
  18.7 3.4 %shard_map.129 = (bf16[256,1920]{1,0:T(8,128)(2,1)S(1)}, bf16[8,32,1920]{2,1,0:T(8,128)(2,1)}, bf16[32,1920]{1,0:T(8,128)(2,1)S(1)}, bf16[32,1920]{1,0:T(8,128)(...) custom-call(s32[1]{0:T(128)} %bitcast.3.at_ref, ...), custom_call_target="tpu_custom_call" | custom-call | flops 1006632960 | bytes 5439488 | tf_op jit(solution)/shard_map/pallas_call | solution.py:154
  22.1 0.6 copy-done.6
  22.8 0.6 copy-done.8
  23.4 0.6 copy-done.10
  24.0 4.9 %all-to-all-start = ((bf16[8,32,1920]{2,1,0:T(8,128)(2,1)}), bf16[8,32,1920]{2,1,0:T(8,128)(2,1)S(1)}, u32[]{:S(2)}, u32[]{:S(2)}) async-start(bf16[8,32,1920]{2,1,0:T(8,128)(2,1)} %get-tuple-element.71), calls=%async_computation | async-start | bytes 1966080 | tf_op jit(solution)/shard_map/all_to_all | solution.py:376
  28.9 0.4 collective-permute-start.4
  29.3 4.0 %collective-permute-start.5 = (bf16[32,1920]{1,0:T(8,128)(2,1)S(1)}, bf16[32,1920]{1,0:T(8,128)(2,1)S(1)}, u32[]{:S(2)}, u32[]{:S(2)}) collective-permute-start(bf16[32,1920]{1,0:T(8,128)(2,1)S(1)} %copy-done.9), channel_id=1, source_target_pairs={{0,18},{2,16},{4,22},{6,20},{8,26},{10,24},{12,30},{14,28},{16,2},... | collective-permute-start | bytes 368648 | tf_op jit(solution)/shard_map/ppermute | solution.py:368
  33.3 1.2 collective-permute-start.6
  35.2 9.0 %collective-permute-done.4.refs_1_.refs_0_ = bf16[32,1920]{1,0:T(8,128)(2,1)S(1)} collective-permute-done((bf16[32,1920]{1,0:T(8,128)(2,1)S(1)}, bf16[32,1920]{1,0:T(8,128)(2,1)S(1)}, u32[]{:S(2)}, u32[]{:S(2)}) %collective-permute-start.4) | collective-permute-done | bytes 122912 | tf_op jit(solution)/shard_map/ppermute | solution.py:368
  44.2 2.0 %collective-permute-start.7 = (bf16[32,1920]{1,0:T(8,128)(2,1)}, bf16[32,1920]{1,0:T(8,128)(2,1)S(1)}, u32[]{:S(2)}, u32[]{:S(2)}) collective-permute-start(bf16[32,1920]{1,0:T(8,128)(2,1)} %get-tuple-element.76), channel_id=1, source_target_pairs={{0,22},{2,20},{4,18},{6,16},{8,30},{10,28},{12,26},{14,24},{16,6},... | collective-permute-start | bytes 368648 | tf_op jit(solution)/shard_map/ppermute | solution.py:368
  46.2 2.3 %collective-permute-done.5.refs_2_.refs_1_ = bf16[32,1920]{1,0:T(8,128)(2,1)S(1)} collective-permute-done((bf16[32,1920]{1,0:T(8,128)(2,1)S(1)}, bf16[32,1920]{1,0:T(8,128)(2,1)S(1)}, u32[]{:S(2)}, u32[]{:S(2)}) %collective-permute-start.5) | collective-permute-done | bytes 122912 | tf_op jit(solution)/shard_map/ppermute | solution.py:368
  48.4 2.7 %collective-permute-start.8 = (bf16[32,1920]{1,0:T(8,128)(2,1)S(1)}, bf16[32,1920]{1,0:T(8,128)(2,1)S(1)}, u32[]{:S(2)}, u32[]{:S(2)}) collective-permute-start(bf16[32,1920]{1,0:T(8,128)(2,1)S(1)} %get-tuple-element.78), channel_id=1, source_target_pairs={{0,24},{2,26},{4,28},{6,30},{8,16},{10,18},{12,20},{14,22},{16,8},... | collective-permute-start | bytes 368648 | tf_op jit(solution)/shard_map/ppermute | solution.py:368
  51.1 0.0 collective-permute-done.6.refs_3_.refs_2_
  51.1 3.7 %collective-permute-start.9 = (bf16[32,1920]{1,0:T(8,128)(2,1)S(1)}, bf16[32,1920]{1,0:T(8,128)(2,1)S(1)}, u32[]{:S(2)}, u32[]{:S(2)}) collective-permute-start(bf16[32,1920]{1,0:T(8,128)(2,1)S(1)} %get-tuple-element.80), channel_id=1, source_target_pairs={{0,26},{2,24},{4,30},{6,28},{8,18},{10,16},{12,22},{14,20},{16,10}... | collective-permute-start | bytes 368648 | tf_op jit(solution)/shard_map/ppermute | solution.py:368
  54.8 0.0 collective-permute-start.10
  54.8 0.0 collective-permute-done.13.refs_7_.refs_8_
  54.8 2.7 %collective-permute-start.11 = (bf16[32,1920]{1,0:T(8,128)(2,1)S(1)}, bf16[32,1920]{1,0:T(8,128)(2,1)S(1)}, u32[]{:S(2)}, u32[]{:S(2)}) collective-permute-start(bf16[32,1920]{1,0:T(8,128)(2,1)S(1)} %get-tuple-element.84), channel_id=1, source_target_pairs={{0,30},{2,28},{4,26},{6,24},{8,22},{10,20},{12,18},{14,16},{16,14}... | collective-permute-start | bytes 368648 | tf_op jit(solution)/shard_map/ppermute | solution.py:368
  57.4 0.0 all-to-all-done.near
  57.5 19.1 %shard_map.130 = (bf16[256,1920]{1,0:T(8,128)(2,1)S(1)}, bf16[32,1920]{1,0:T(8,128)(2,1)S(1)}, bf16[32,1920]{1,0:T(8,128)(2,1)S(1)}, bf16[32,1920]{1,0:T(8,128)(2,1)S(1)}) custom-call(s32[1]{0:T(128)} %constant.38.clone.1.live, bf16[256,1920]{1,0:T(8,128)(2,1)S(1)} %bitcast.11, bf16[32,1920]{1,0:T(8,128)(2,1)S(1)} %collective-permute-done.4.refs_1_.refs_0_, ...), custom_call_target="tpu_custom_call" | custom-call | flops 11072962560 | bytes 31457280 | tf_op jit(solution)/shard_map/pallas_call | solution.py:273
  76.6 0.0 collective-permute-done.8.refs_4_.refs_1_
  76.6 0.4 collective-permute-done.11.refs_7_.refs_4_
  77.1 1.4 shard_map.131
  78.4 3.7 %all-to-all-start.1 = ((bf16[8,32,1920]{2,1,0:T(8,128)(2,1)}), bf16[8,32,1920]{2,1,0:T(8,128)(2,1)S(1)}, u32[]{:S(2)}, u32[]{:S(2)}) async-start(bf16[8,32,1920]{2,1,0:T(8,128)(2,1)} %get-tuple-element.91), calls=%async_computation.1 | async-start | bytes 1966080 | tf_op jit(solution)/shard_map/all_to_all | solution.py:376
  82.2 1.7 %collective-permute-start.14 = (bf16[32,1920]{1,0:T(8,128)(2,1)S(1)}, bf16[32,1920]{1,0:T(8,128)(2,1)S(1)}, u32[]{:S(2)}, u32[]{:S(2)}) collective-permute-start(bf16[32,1920]{1,0:T(8,128)(2,1)S(1)} %get-tuple-element.92), channel_id=1, source_target_pairs={{0,16},{2,18},{4,20},{6,22},{8,24},{10,26},{12,28},{14,30},{16,0},... | collective-permute-start | bytes 368648 | tf_op jit(solution)/shard_map/ppermute | solution.py:368
  83.9 2.7 %collective-permute-start.15 = (bf16[32,1920]{1,0:T(8,128)(2,1)S(1)}, bf16[32,1920]{1,0:T(8,128)(2,1)S(1)}, u32[]{:S(2)}, u32[]{:S(2)}) collective-permute-start(bf16[32,1920]{1,0:T(8,128)(2,1)S(1)} %get-tuple-element.93), channel_id=1, source_target_pairs={{0,18},{2,16},{4,22},{6,20},{8,26},{10,24},{12,30},{14,28},{16,2},... | collective-permute-start | bytes 368648 | tf_op jit(solution)/shard_map/ppermute | solution.py:368
  86.5 2.6 %collective-permute-start.16 = (bf16[32,1920]{1,0:T(8,128)(2,1)S(1)}, bf16[32,1920]{1,0:T(8,128)(2,1)S(1)}, u32[]{:S(2)}, u32[]{:S(2)}) collective-permute-start(bf16[32,1920]{1,0:T(8,128)(2,1)S(1)} %get-tuple-element.94), channel_id=1, source_target_pairs={{0,20},{2,22},{4,16},{6,18},{8,28},{10,30},{12,24},{14,26},{16,4},... | collective-permute-start | bytes 368648 | tf_op jit(solution)/shard_map/ppermute | solution.py:368
  89.2 14.3 %shard_map.132 = (bf16[32,1920]{1,0:T(8,128)(2,1)S(1)}, bf16[32,1920]{1,0:T(8,128)(2,1)S(1)}, bf16[32,1920]{1,0:T(8,128)(2,1)S(1)}, bf16[32,1920]{1,0:T(8,128)(2,1)S(1)}, bf16[32,1920]{1,0:T(8,128)(2,1)S(1)}) custom-call(s32[16]{0:T(128)S(1)} %get-tuple-element.95.live, bf16[32,1920]{1,0:T(8,128)(2,1)S(1)} %collective-permute-done.7.refs_3_.refs_0_, ...), custom_call_target="tpu_custom_call" | custom-call | flops 5033164800 | bytes 31457280 | tf_op jit(solution)/shard_map/pallas_call | solution.py:273
  103.5 0.0 collective-permute-done.14.refs_0_
  103.5 0.7 collective-permute-done.16.refs_2_
  104.3 0.4 collective-permute-start.17
  104.7 2.3 %collective-permute-start.18 = (bf16[32,1920]{1,0:T(8,128)(2,1)S(1)}, bf16[32,1920]{1,0:T(8,128)(2,1)S(1)}, u32[]{:S(2)}, u32[]{:S(2)}) collective-permute-start(bf16[32,1920]{1,0:T(8,128)(2,1)S(1)} %get-tuple-element.107), channel_id=1, source_target_pairs={{0,24},{2,26},{4,28},{6,30},{8,16},{10,18},{12,20},{14,22},{16,8},... | collective-permute-start | bytes 368648 | tf_op jit(solution)/shard_map/ppermute | solution.py:368
  107.0 0.7 collective-permute-start.19
  107.7 2.6 %collective-permute-start.20 = (bf16[32,1920]{1,0:T(8,128)(2,1)S(1)}, bf16[32,1920]{1,0:T(8,128)(2,1)S(1)}, u32[]{:S(2)}, u32[]{:S(2)}) collective-permute-start(bf16[32,1920]{1,0:T(8,128)(2,1)S(1)} %get-tuple-element.109), channel_id=1, source_target_pairs={{0,28},{2,30},{4,24},{6,26},{8,20},{10,22},{12,16},{14,18},{16,12}... | collective-permute-start | bytes 368648 | tf_op jit(solution)/shard_map/ppermute | solution.py:368
  110.4 0.5 collective-permute-start.21
  110.8 10.6 %collective-permute-done.17.refs_3_ = bf16[32,1920]{1,0:T(8,128)(2,1)S(1)} collective-permute-done((bf16[32,1920]{1,0:T(8,128)(2,1)S(1)}, bf16[32,1920]{1,0:T(8,128)(2,1)S(1)}, u32[]{:S(2)}, u32[]{:S(2)}) %collective-permute-start.17) | collective-permute-done | bytes 122912 | tf_op jit(solution)/shard_map/ppermute | solution.py:368
  121.4 4.7 %collective-permute-done.18.refs_4_ = bf16[32,1920]{1,0:T(8,128)(2,1)S(1)} collective-permute-done((bf16[32,1920]{1,0:T(8,128)(2,1)S(1)}, bf16[32,1920]{1,0:T(8,128)(2,1)S(1)}, u32[]{:S(2)}, u32[]{:S(2)}) %collective-permute-start.18) | collective-permute-done | bytes 122912 | tf_op jit(solution)/shard_map/ppermute | solution.py:368
  126.1 2.7 %collective-permute-done.19.refs_5_ = bf16[32,1920]{1,0:T(8,128)(2,1)S(1)} collective-permute-done((bf16[32,1920]{1,0:T(8,128)(2,1)S(1)}, bf16[32,1920]{1,0:T(8,128)(2,1)S(1)}, u32[]{:S(2)}, u32[]{:S(2)}) %collective-permute-start.19) | collective-permute-done | bytes 122912 | tf_op jit(solution)/shard_map/ppermute | solution.py:368
  128.8 3.2 %collective-permute-done.20.refs_6_ = bf16[32,1920]{1,0:T(8,128)(2,1)S(1)} collective-permute-done((bf16[32,1920]{1,0:T(8,128)(2,1)S(1)}, bf16[32,1920]{1,0:T(8,128)(2,1)S(1)}, u32[]{:S(2)}, u32[]{:S(2)}) %collective-permute-start.20) | collective-permute-done | bytes 122912 | tf_op jit(solution)/shard_map/ppermute | solution.py:368
  132.0 1.8 %collective-permute-done.21.refs_7_ = bf16[32,1920]{1,0:T(8,128)(2,1)S(1)} collective-permute-done((bf16[32,1920]{1,0:T(8,128)(2,1)S(1)}, bf16[32,1920]{1,0:T(8,128)(2,1)S(1)}, u32[]{:S(2)}, u32[]{:S(2)}) %collective-permute-start.21) | collective-permute-done | bytes 122912 | tf_op jit(solution)/shard_map/ppermute | solution.py:368
  133.9 1.9 %shard_map.133 = bf16[256,1920]{1,0:T(8,128)(2,1)} custom-call(s32[16]{0:T(128)S(1)} %broadcast_subtract_fusion.run_ref, bf16[256,1920]{1,0:T(8,128)(2,1)S(1)} %get-tuple-element.70.hidden, bf16[8,32,1920]{2,1,0:T(8,128)(2,1)S(1)} %all-to-all-done.1.near, bf16[32,1920]{1,0:T(8,128)(2,1)S(1)} %collective-permute-done.14.refs_0_, ...), custom_call_target="tpu_custom_call" | custom-call | tf_op jit(solution)/shard_map/pallas_call | solution.py:183
  (32 shorter events, 0.1 us)
Async XLA Ops:
  0.0 12.7 %collective-permute-start = (bf16[960,1024]{1,0:T(8,128)(2,1)}, bf16[960,1024]{1,0:T(8,128)(2,1)}, u32[]{:S(2)}, u32[]{:S(2)}) collective-permute-start(bf16[960,1024]{1,0:T(8,128)(2,1)} %refs_0_.1), channel_id=1, source_target_pairs={{0,1},{1,0},{2,3},{3,2},{4,5},{5,4},{6,7},{7,6},{8,9},{9,8},{10,11... | collective-permute-start | bytes 5898248 | tf_op jit(solution)/shard_map/ppermute | solution.py:319
  0.0 12.7 %collective-permute-start.1 = (bf16[960,1024]{1,0:T(8,128)(2,1)}, bf16[960,1024]{1,0:T(8,128)(2,1)}, u32[]{:S(2)}, u32[]{:S(2)}) collective-permute-start(bf16[960,1024]{1,0:T(8,128)(2,1)} %refs_1_.1), channel_id=1, source_target_pairs={{0,1},{1,0},{2,3},{3,2},{4,5},{5,4},{6,7},{7,6},{8,9},{9,8},{10,11... | collective-permute-start | bytes 5898248 | tf_op jit(solution)/shard_map/ppermute | solution.py:319
  0.5 12.2 %collective-permute-start.2 = (bf16[960,1024]{1,0:T(8,128)(2,1)}, bf16[960,1024]{1,0:T(8,128)(2,1)}, u32[]{:S(2)}, u32[]{:S(2)}) collective-permute-start(bf16[960,1024]{1,0:T(8,128)(2,1)} %refs_2_.1), channel_id=1, source_target_pairs={{0,1},{1,0},{2,3},{3,2},{4,5},{5,4},{6,7},{7,6},{8,9},{9,8},{10,11... | collective-permute-start | bytes 5898248 | tf_op jit(solution)/shard_map/ppermute | solution.py:319
  0.5 17.6 %collective-permute-start.3 = (bf16[512,1920]{1,0:T(8,128)(2,1)}, bf16[512,1920]{1,0:T(8,128)(2,1)S(1)}, u32[]{:S(2)}, u32[]{:S(2)}) collective-permute-start(bf16[512,1920]{1,0:T(8,128)(2,1)} %refs_0_.2), channel_id=1, source_target_pairs={{0,1},{1,0},{2,3},{3,2},{4,5},{5,4},{6,7},{7,6},{8,9},{9,8},{10,11... | collective-permute-start | bytes 5898248 | tf_op jit(solution)/shard_map/ppermute | solution.py:319
  4.2 1.2 copy-start
  5.4 1.5 %copy-start.3 = (bf16[960,1024]{1,0:T(8,128)(2,1)S(1)}, bf16[960,1024]{1,0:T(8,128)(2,1)}, u32[]{:S(2)}) copy-start(bf16[960,1024]{1,0:T(8,128)(2,1)} %refs_0_.1) | copy-start | bytes 5898244
  6.9 1.5 %copy-start.4 = (bf16[960,1024]{1,0:T(8,128)(2,1)S(1)}, bf16[960,1024]{1,0:T(8,128)(2,1)}, u32[]{:S(2)}) copy-start(bf16[960,1024]{1,0:T(8,128)(2,1)} %refs_1_.1) | copy-start | bytes 5898244
  8.5 1.5 %copy-start.5 = (bf16[960,1024]{1,0:T(8,128)(2,1)S(1)}, bf16[960,1024]{1,0:T(8,128)(2,1)}, u32[]{:S(2)}) copy-start(bf16[960,1024]{1,0:T(8,128)(2,1)} %refs_2_.1) | copy-start | bytes 5898244
  12.8 5.9 %copy-start.12 = (f32[1920]{0:T(1024)S(1)}, f32[1920]{0:T(1024)}, u32[]{:S(2)}) copy-start(f32[1920]{0:T(1024)} %param.23) | copy-start | bytes 23044
  12.8 5.9 %copy-start.1 = (bf16[256,1920]{1,0:T(8,128)(2,1)S(1)}, bf16[256,1920]{1,0:T(8,128)(2,1)}, u32[]{:S(2)}) copy-start(bf16[256,1920]{1,0:T(8,128)(2,1)} %tokens.3) | copy-start | bytes 2949124
  12.8 5.9 %copy-start.2 = (bf16[512,1920]{1,0:T(8,128)(2,1)S(1)}, bf16[512,1920]{1,0:T(8,128)(2,1)}, u32[]{:S(2)}) copy-start(bf16[512,1920]{1,0:T(8,128)(2,1)} %refs_0_.2) | copy-start | bytes 5898244
  18.1 36.7 %collective-permute-start.12 = (bf16[1920,2048]{1,0:T(8,128)(2,1)}, bf16[1920,2048]{1,0:T(8,128)(2,1)}, u32[]{:S(2)}, u32[]{:S(2)}) collective-permute-start(bf16[1920,2048]{1,0:T(8,128)(2,1)} %bitcast.4.refs_4_.refs_5_), channel_id=1, source_target_pairs={{0,1},{1,0},{2,3},{3,2},{4,5},{5,4},{6,7},{7,6},{8,9},{9,8},{10,11... | collective-permute-start | bytes 23592968 | tf_op jit(solution)/shard_map/ppermute | solution.py:319
  18.3 36.5 %collective-permute-start.13 = (bf16[2048,1920]{1,0:T(8,128)(2,1)}, bf16[2048,1920]{1,0:T(8,128)(2,1)}, u32[]{:S(2)}, u32[]{:S(2)}) collective-permute-start(bf16[2048,1920]{1,0:T(8,128)(2,1)} %bitcast.5.refs_6_.refs_7_), channel_id=1, source_target_pairs={{0,1},{1,0},{2,3},{3,2},{4,5},{5,4},{6,7},{7,6},{8,9},{9,8},{10,11... | collective-permute-start | bytes 23592968 | tf_op jit(solution)/shard_map/ppermute | solution.py:319
  22.1 0.6 copy-start.6
  22.8 0.7 copy-start.8
  23.4 0.6 copy-start.10
  24.0 4.9 %copy-start.11 = (bf16[32,1920]{1,0:T(8,128)(2,1)S(1)}, bf16[32,1920]{1,0:T(8,128)(2,1)}, u32[]{:S(2)}) copy-start(bf16[32,1920]{1,0:T(8,128)(2,1)} %copy-done.10) | copy-start | bytes 368644
  24.0 5.3 %copy-start.9 = (bf16[32,1920]{1,0:T(8,128)(2,1)S(1)}, bf16[32,1920]{1,0:T(8,128)(2,1)}, u32[]{:S(2)}) copy-start(bf16[32,1920]{1,0:T(8,128)(2,1)} %copy-done.8) | copy-start | bytes 368644
  24.0 9.3 %copy-start.7 = (bf16[32,1920]{1,0:T(8,128)(2,1)S(1)}, bf16[32,1920]{1,0:T(8,128)(2,1)}, u32[]{:S(2)}) copy-start(bf16[32,1920]{1,0:T(8,128)(2,1)} %copy-done.6) | copy-start | bytes 368644
  24.0 33.4 %all-to-all-start = ((bf16[8,32,1920]{2,1,0:T(8,128)(2,1)}), bf16[8,32,1920]{2,1,0:T(8,128)(2,1)S(1)}, u32[]{:S(2)}, u32[]{:S(2)}) async-start(bf16[8,32,1920]{2,1,0:T(8,128)(2,1)} %get-tuple-element.71), calls=%async_computation | async-start | bytes 1966080 | tf_op jit(solution)/shard_map/all_to_all | solution.py:376
  28.9 15.3 %collective-permute-start.4 = (bf16[32,1920]{1,0:T(8,128)(2,1)S(1)}, bf16[32,1920]{1,0:T(8,128)(2,1)S(1)}, u32[]{:S(2)}, u32[]{:S(2)}) collective-permute-start(bf16[32,1920]{1,0:T(8,128)(2,1)S(1)} %copy-done.11), channel_id=1, source_target_pairs={{0,16},{2,18},{4,20},{6,22},{8,24},{10,26},{12,28},{14,30},{16,0},... | collective-permute-start | bytes 368648 | tf_op jit(solution)/shard_map/ppermute | solution.py:368
  29.3 19.1 %collective-permute-start.5 = (bf16[32,1920]{1,0:T(8,128)(2,1)S(1)}, bf16[32,1920]{1,0:T(8,128)(2,1)S(1)}, u32[]{:S(2)}, u32[]{:S(2)}) collective-permute-start(bf16[32,1920]{1,0:T(8,128)(2,1)S(1)} %copy-done.9), channel_id=1, source_target_pairs={{0,18},{2,16},{4,22},{6,20},{8,26},{10,24},{12,30},{14,28},{16,2},... | collective-permute-start | bytes 368648 | tf_op jit(solution)/shard_map/ppermute | solution.py:368
  33.3 17.8 %collective-permute-start.6 = (bf16[32,1920]{1,0:T(8,128)(2,1)S(1)}, bf16[32,1920]{1,0:T(8,128)(2,1)S(1)}, u32[]{:S(2)}, u32[]{:S(2)}) collective-permute-start(bf16[32,1920]{1,0:T(8,128)(2,1)S(1)} %copy-done.7), channel_id=1, source_target_pairs={{0,20},{2,22},{4,16},{6,18},{8,28},{10,30},{12,24},{14,26},{16,4},... | collective-permute-start | bytes 368648 | tf_op jit(solution)/shard_map/ppermute | solution.py:368
  44.2 32.4 %collective-permute-start.7 = (bf16[32,1920]{1,0:T(8,128)(2,1)}, bf16[32,1920]{1,0:T(8,128)(2,1)S(1)}, u32[]{:S(2)}, u32[]{:S(2)}) collective-permute-start(bf16[32,1920]{1,0:T(8,128)(2,1)} %get-tuple-element.76), channel_id=1, source_target_pairs={{0,22},{2,20},{4,18},{6,16},{8,30},{10,28},{12,26},{14,24},{16,6},... | collective-permute-start | bytes 368648 | tf_op jit(solution)/shard_map/ppermute | solution.py:368
  48.4 28.2 %collective-permute-start.8 = (bf16[32,1920]{1,0:T(8,128)(2,1)S(1)}, bf16[32,1920]{1,0:T(8,128)(2,1)S(1)}, u32[]{:S(2)}, u32[]{:S(2)}) collective-permute-start(bf16[32,1920]{1,0:T(8,128)(2,1)S(1)} %get-tuple-element.78), channel_id=1, source_target_pairs={{0,24},{2,26},{4,28},{6,30},{8,16},{10,18},{12,20},{14,22},{16,8},... | collective-permute-start | bytes 368648 | tf_op jit(solution)/shard_map/ppermute | solution.py:368
  51.1 25.5 %collective-permute-start.9 = (bf16[32,1920]{1,0:T(8,128)(2,1)S(1)}, bf16[32,1920]{1,0:T(8,128)(2,1)S(1)}, u32[]{:S(2)}, u32[]{:S(2)}) collective-permute-start(bf16[32,1920]{1,0:T(8,128)(2,1)S(1)} %get-tuple-element.80), channel_id=1, source_target_pairs={{0,26},{2,24},{4,30},{6,28},{8,18},{10,16},{12,22},{14,20},{16,10}... | collective-permute-start | bytes 368648 | tf_op jit(solution)/shard_map/ppermute | solution.py:368
  54.8 21.9 %collective-permute-start.10 = (bf16[32,1920]{1,0:T(8,128)(2,1)S(1)}, bf16[32,1920]{1,0:T(8,128)(2,1)S(1)}, u32[]{:S(2)}, u32[]{:S(2)}) collective-permute-start(bf16[32,1920]{1,0:T(8,128)(2,1)S(1)} %get-tuple-element.82), channel_id=1, source_target_pairs={{0,28},{2,30},{4,24},{6,26},{8,20},{10,22},{12,16},{14,18},{16,12}... | collective-permute-start | bytes 368648 | tf_op jit(solution)/shard_map/ppermute | solution.py:368
  54.8 22.3 %collective-permute-start.11 = (bf16[32,1920]{1,0:T(8,128)(2,1)S(1)}, bf16[32,1920]{1,0:T(8,128)(2,1)S(1)}, u32[]{:S(2)}, u32[]{:S(2)}) collective-permute-start(bf16[32,1920]{1,0:T(8,128)(2,1)S(1)} %get-tuple-element.84), channel_id=1, source_target_pairs={{0,30},{2,28},{4,26},{6,24},{8,22},{10,20},{12,18},{14,16},{16,14}... | collective-permute-start | bytes 368648 | tf_op jit(solution)/shard_map/ppermute | solution.py:368
  78.4 55.4 %all-to-all-start.1 = ((bf16[8,32,1920]{2,1,0:T(8,128)(2,1)}), bf16[8,32,1920]{2,1,0:T(8,128)(2,1)S(1)}, u32[]{:S(2)}, u32[]{:S(2)}) async-start(bf16[8,32,1920]{2,1,0:T(8,128)(2,1)} %get-tuple-element.91), calls=%async_computation.1 | async-start | bytes 1966080 | tf_op jit(solution)/shard_map/all_to_all | solution.py:376
  82.2 21.3 %collective-permute-start.14 = (bf16[32,1920]{1,0:T(8,128)(2,1)S(1)}, bf16[32,1920]{1,0:T(8,128)(2,1)S(1)}, u32[]{:S(2)}, u32[]{:S(2)}) collective-permute-start(bf16[32,1920]{1,0:T(8,128)(2,1)S(1)} %get-tuple-element.92), channel_id=1, source_target_pairs={{0,16},{2,18},{4,20},{6,22},{8,24},{10,26},{12,28},{14,30},{16,0},... | collective-permute-start | bytes 368648 | tf_op jit(solution)/shard_map/ppermute | solution.py:368
  83.9 19.7 %collective-permute-start.15 = (bf16[32,1920]{1,0:T(8,128)(2,1)S(1)}, bf16[32,1920]{1,0:T(8,128)(2,1)S(1)}, u32[]{:S(2)}, u32[]{:S(2)}) collective-permute-start(bf16[32,1920]{1,0:T(8,128)(2,1)S(1)} %get-tuple-element.93), channel_id=1, source_target_pairs={{0,18},{2,16},{4,22},{6,20},{8,26},{10,24},{12,30},{14,28},{16,2},... | collective-permute-start | bytes 368648 | tf_op jit(solution)/shard_map/ppermute | solution.py:368
  86.5 17.7 %collective-permute-start.16 = (bf16[32,1920]{1,0:T(8,128)(2,1)S(1)}, bf16[32,1920]{1,0:T(8,128)(2,1)S(1)}, u32[]{:S(2)}, u32[]{:S(2)}) collective-permute-start(bf16[32,1920]{1,0:T(8,128)(2,1)S(1)} %get-tuple-element.94), channel_id=1, source_target_pairs={{0,20},{2,22},{4,16},{6,18},{8,28},{10,30},{12,24},{14,26},{16,4},... | collective-permute-start | bytes 368648 | tf_op jit(solution)/shard_map/ppermute | solution.py:368
  104.3 17.1 %collective-permute-start.17 = (bf16[32,1920]{1,0:T(8,128)(2,1)S(1)}, bf16[32,1920]{1,0:T(8,128)(2,1)S(1)}, u32[]{:S(2)}, u32[]{:S(2)}) collective-permute-start(bf16[32,1920]{1,0:T(8,128)(2,1)S(1)} %get-tuple-element.106), channel_id=1, source_target_pairs={{0,22},{2,20},{4,18},{6,16},{8,30},{10,28},{12,26},{14,24},{16,6},... | collective-permute-start | bytes 368648 | tf_op jit(solution)/shard_map/ppermute | solution.py:368
  104.7 21.4 %collective-permute-start.18 = (bf16[32,1920]{1,0:T(8,128)(2,1)S(1)}, bf16[32,1920]{1,0:T(8,128)(2,1)S(1)}, u32[]{:S(2)}, u32[]{:S(2)}) collective-permute-start(bf16[32,1920]{1,0:T(8,128)(2,1)S(1)} %get-tuple-element.107), channel_id=1, source_target_pairs={{0,24},{2,26},{4,28},{6,30},{8,16},{10,18},{12,20},{14,22},{16,8},... | collective-permute-start | bytes 368648 | tf_op jit(solution)/shard_map/ppermute | solution.py:368
  107.0 21.8 %collective-permute-start.19 = (bf16[32,1920]{1,0:T(8,128)(2,1)S(1)}, bf16[32,1920]{1,0:T(8,128)(2,1)S(1)}, u32[]{:S(2)}, u32[]{:S(2)}) collective-permute-start(bf16[32,1920]{1,0:T(8,128)(2,1)S(1)} %get-tuple-element.108), channel_id=1, source_target_pairs={{0,26},{2,24},{4,30},{6,28},{8,18},{10,16},{12,22},{14,20},{16,10}... | collective-permute-start | bytes 368648 | tf_op jit(solution)/shard_map/ppermute | solution.py:368
  107.7 24.3 %collective-permute-start.20 = (bf16[32,1920]{1,0:T(8,128)(2,1)S(1)}, bf16[32,1920]{1,0:T(8,128)(2,1)S(1)}, u32[]{:S(2)}, u32[]{:S(2)}) collective-permute-start(bf16[32,1920]{1,0:T(8,128)(2,1)S(1)} %get-tuple-element.109), channel_id=1, source_target_pairs={{0,28},{2,30},{4,24},{6,26},{8,20},{10,22},{12,16},{14,18},{16,12}... | collective-permute-start | bytes 368648 | tf_op jit(solution)/shard_map/ppermute | solution.py:368
  110.4 23.5 %collective-permute-start.21 = (bf16[32,1920]{1,0:T(8,128)(2,1)S(1)}, bf16[32,1920]{1,0:T(8,128)(2,1)S(1)}, u32[]{:S(2)}, u32[]{:S(2)}) collective-permute-start(bf16[32,1920]{1,0:T(8,128)(2,1)S(1)} %get-tuple-element.110), channel_id=1, source_target_pairs={{0,30},{2,28},{4,26},{6,24},{8,22},{10,20},{12,18},{14,16},{16,14}... | collective-permute-start | bytes 368648 | tf_op jit(solution)/shard_map/ppermute | solution.py:368

commit v5 on v4

--- a/solution.py
+++ b/solution.py
@@ -32,6 +32,27 @@
     return [pl.BlockSpec(memory_space=pltpu.VMEM)] * count
 
 
+def hbm(array):
+    return pltpu.with_memory_space_constraint(array, pltpu.HBM)
+
+
+def vmem(array):
+    return pltpu.with_memory_space_constraint(array, pltpu.VMEM)
+
+
+def in_hbm(count):
+    return [pl.BlockSpec(memory_space=pltpu.HBM)] * count
+
+
+def fetch(refs, held, arrived):
+    copies = [
+        pltpu.make_async_copy(ref, held.at[n], arrived.at[n]) for n, ref in enumerate(refs)
+    ]
+    for copy in copies:
+        copy.start()
+    return copies
+
+
 def cost(macs, *arrays):
     size = sum(a.size * a.dtype.itemsize for a in arrays)
     return pl.CostEstimate(flops=2 * macs, bytes_accessed=size, transcendentals=0)
@@ -39,8 +60,9 @@
 
 def project_kernel(pieces, at_ref, tokens, gain, *refs):
     weights, rest, sums = refs[:3], refs[3 : 2 + pieces], refs[2 + pieces : 5 + pieces]
-    own = refs[-1]
+    own, held, arrived = refs[-3:]
     part = own.shape[1]
+    copies = fetch(weights, held, arrived)
     normed = layer_norm(tokens[...], gain[...]).astype(jnp.bfloat16)
     for v in range(pieces):
 
@@ -50,8 +72,9 @@
                 first = (v - s) % pieces * part
                 ref[...] = normed[:, first : first + part]
 
-    for weight, total in zip(weights, sums):
-        total[...] = dot(own[...], weight[...])
+    for n, total in enumerate(sums):
+        copies[n].wait()
+        total[...] = dot(own[...], held[n])
 
 
 def project(at, tokens, gain, weights, pieces):
@@ -59,28 +82,33 @@
     part, wide = weights[0].shape
     out = pl.pallas_call(
         functools.partial(project_kernel, pieces),
-        in_specs=[pl.BlockSpec(memory_space=pltpu.SMEM)]
-        + in_vmem(5),
+        in_specs=[pl.BlockSpec(memory_space=pltpu.SMEM)] + in_vmem(2) + in_hbm(3),
         out_specs=in_vmem(pieces + 2),
-        out_shape=[jax.ShapeDtypeStruct((count, part), jnp.bfloat16)] * (pieces - 1)
-        + [jax.ShapeDtypeStruct((count, wide), jnp.float32)] * 3,
-        scratch_shapes=[pltpu.VMEM((count, part), jnp.bfloat16)],
+        out_shape=[pltpu.VMEM((count, part), jnp.bfloat16)] * (pieces - 1)
+        + [pltpu.VMEM((count, wide), jnp.float32)] * 3,
+        scratch_shapes=[
+            pltpu.VMEM((count, part), jnp.bfloat16),
+            pltpu.VMEM((3, part, wide), jnp.bfloat16),
+            pltpu.SemaphoreType.DMA((3,)),
+        ],
         compiler_params=pltpu.CompilerParams(vmem_limit_bytes=FRONT_LIMIT),
         cost_estimate=cost(3 * count * part * wide, tokens, *weights),
-    )(at, tokens, gain, *weights)
+    )(at, tokens, gain, *map(hbm, weights))
     return out[: pieces - 1], out[pieces - 1 :]
 
 
 def attend_kernel(rest_count, bias, *refs):
     rest = refs[:rest_count]
     sums = refs[rest_count : rest_count + 3]
-    weights = refs[rest_count + 3 : -2]
-    context, scores = refs[-2:]
+    weights = refs[rest_count + 3 : -4]
+    context, scores, held, arrived = refs[-4:]
+    copies = fetch(weights, held, arrived)
 
     def full(n):
         total = sums[n][...]
         for s in range(rest_count):
-            total += dot(rest[s][...], weights[n * rest_count + s][...])
+            copies[n * rest_count + s].wait()
+            total += dot(rest[s][...], held[n * rest_count + s])
         return total.astype(jnp.bfloat16)
 
     count, block = bias.shape
@@ -101,7 +129,7 @@
     for h, head, rows in tiles:
         tile = scores[h, rows, :]
         weight = jnp.exp(tile - jnp.max(tile, axis=-1, keepdims=True))
-        probs = (weight / jnp.sum(weight, axis=-1, keepdims=True)).astype(jnp.bfloat16)
+        probs = (weight * (1.0 / jnp.sum(weight, axis=-1, keepdims=True))).astype(jnp.bfloat16)
         context[rows, head] = dot(probs, valued[rows, head]).astype(jnp.bfloat16)
 
 
@@ -110,23 +138,30 @@
     flat = [w for pieces in weights for w in pieces]
     return pl.pallas_call(
         functools.partial(attend_kernel, len(rest)),
-        in_specs=in_vmem(4 + len(rest) + len(flat)),
+        in_specs=in_vmem(4 + len(rest)) + in_hbm(len(flat)),
         out_specs=in_vmem(1)[0],
-        out_shape=jax.ShapeDtypeStruct((count, wide), jnp.bfloat16),
-        scratch_shapes=[pltpu.VMEM((wide // HDIM, *bias.shape), jnp.float32)],
+        out_shape=pltpu.VMEM((count, wide), jnp.bfloat16),
+        scratch_shapes=[
+            pltpu.VMEM((wide // HDIM, *bias.shape), jnp.float32),
+            pltpu.VMEM((len(flat), *flat[0].shape), jnp.bfloat16),
+            pltpu.SemaphoreType.DMA((len(flat),)),
+        ],
         compiler_params=pltpu.CompilerParams(vmem_limit_bytes=FRONT_LIMIT),
         cost_estimate=cost(2 * count * sum(w.size for w in flat), *flat, *sums),
-    )(bias, *rest, *sums, *flat)
+    )(bias, *map(vmem, (*rest, *sums)), *map(hbm, flat))
 
 
 def hidden_kernel(pieces, runs, slots, at_ref, run_ref, context, tokens, gain, *refs):
-    weights, hidden, outs, routed = refs[:pieces], refs[pieces], refs[pieces + 1 : -1], refs[-1]
+    weights, hidden, outs = refs[:pieces], refs[pieces], refs[pieces + 1 : -3]
+    routed, held, arrived = refs[-3:]
+    copies = fetch(weights, held, arrived)
     part = weights[0].shape[0]
     count = tokens.shape[0]
     total = tokens[...].astype(jnp.float32)
     for s in range(pieces):
         first = lax.rem(at_ref[0] + pieces - s, pieces) * part
-        total += dot(context[:, pl.ds(pl.multiple_of(first, 128), part)], weights[s][...])
+        copies[s].wait()
+        total += dot(context[:, pl.ds(pl.multiple_of(first, 128), part)], held[s])
     hidden[...] = total.astype(jnp.bfloat16)
     rows = count // runs
     for j in range(runs):
@@ -149,19 +184,24 @@
 def hidden_states(at, run_of_slot, context, tokens, gain, weights, runs, slots):
     count, width = tokens.shape
     rows = count // runs
+    part = weights[0].shape[0]
     near = slots // 2
     outs = [(near, rows, width)] + [(rows, width)] * near if slots else [(count, width)]
     out = pl.pallas_call(
         functools.partial(hidden_kernel, len(weights), runs, slots),
-        in_specs=[pl.BlockSpec(memory_space=pltpu.SMEM)] * 2 + in_vmem(3 + len(weights)),
+        in_specs=[pl.BlockSpec(memory_space=pltpu.SMEM)] * 2 + in_vmem(3) + in_hbm(len(weights)),
         out_specs=in_vmem(1 + len(outs)),
         out_shape=[
             jax.ShapeDtypeStruct(shape, jnp.bfloat16) for shape in [tokens.shape, *outs]
         ],
-        scratch_shapes=[pltpu.VMEM((runs + 1, rows, width), jnp.bfloat16)],
+        scratch_shapes=[
+            pltpu.VMEM((runs + 1, rows, width), jnp.bfloat16),
+            pltpu.VMEM((len(weights), part, width), jnp.bfloat16),
+            pltpu.SemaphoreType.DMA((len(weights),)),
+        ],
         compiler_params=pltpu.CompilerParams(vmem_limit_bytes=FRONT_LIMIT),
         cost_estimate=cost(context.size * width, context, tokens, *weights),
-    )(at, run_of_slot, context, tokens, gain, *weights)
+    )(at, run_of_slot, vmem(context), tokens, gain, *map(hbm, weights))
     return out[0], out[1:]
 
 
@@ -287,7 +327,7 @@
             dimension_semantics=("arbitrary",), vmem_limit_bytes=VMEM_LIMIT
         ),
         cost_estimate=cost(2 * rows * width * hidden * pieces, *first, *second),
-    )(live, *ins, *first, *second)
+    )(live, *ins, *map(hbm, first), *map(hbm, second))
 
 
 def body(

time: 136 us -> 132 us (0.971)
  local copies, waits for them, and re-layouts: 9.22 us -> 2.65 us
  Pallas kernels: 48.1 us -> 50.3 us
    unnamed x26 -> x6, local copies, waits for them, and re-layouts: 7.78 us -> 1.21 us
    pallas_call x1, Pallas kernels: 3.44 us -> 5.17 us  [hidden_states(): pl.pallas_call(functools.partial(hidden_kernel, len(weights), runs, slots...]
  transfers between devices with their start and end apart: 24 -> 24, of which waited for: 9 -> 10; matrix products, arithmetic and copies ran while one was open for 2% -> 2% of each run, Pallas kernels for 33% -> 36%
where the time goes in v5:
time: 132 us
  Pallas kernels  50.3 us (38%)
  starting transfers between devices  40.2 us (30%)
  waiting for transfers between devices  36.4 us (28%)
  local copies, waits for them, and re-layouts  2.65 us (2%)
  other arithmetic  1.68 us (1%)
    ppermute x16, waiting for transfers between devices, swap(): lax.ppermute(a, 'lang', [(i, i ^ k) for i in range(lang_count)])  35.6 us
    pallas_call x2, Pallas kernels, expert_ffn(): pl.pallas_call(functools.partial(expert_kernel, sizes, pieces, per, slots...  33.5 us
    ppermute x16, starting transfers between devices, swap(): lax.ppermute(a, 'lang', [(i, i ^ k) for i in range(lang_count)])  30.1 us
    all_to_all x2, starting transfers between devices, within(): lax.all_to_all(array, 'lang', 0, 0, axis_index_groups=halves, tiled=True)  8.5 us
    pallas_call x1, Pallas kernels, hidden_states(): pl.pallas_call(functools.partial(hidden_kernel, len(weights), runs, slots...  5.17 us
    pallas_call x1, Pallas kernels, attend(): pl.pallas_call(functools.partial(attend_kernel, len(rest)), in_specs=in_v...  4.7 us
    pallas_call x1, Pallas kernels, project(): pl.pallas_call(functools.partial(project_kernel, pieces), in_specs=[pl.Bl...  3.7 us
  transfers between devices with their start and end apart: 24, of which 10 were waited for; matrix products, arithmetic and copies ran while one was open for 2% of the time, Pallas kernels for 36%

profile of v5, /device:TPU:16, one launch (start us, length us, event | category | flops | bytes accessed | tf_op | source)
XLA Modules:
  0.0 132.1 jit_solution(16605021531749942311)
XLA Ops:
  0.0 0.0 collective-permute-start
  0.0 0.5 collective-permute-start.1
  0.5 0.0 collective-permute-start.2
  0.5 0.5 collective-permute-start.3
  1.0 0.7 broadcast_in_dim.71.gain
  1.7 0.7 copy.16
  2.5 0.1 reduce
  2.6 0.1 convert_reduce_fusion
  2.7 0.1 fusion.bias
  2.9 0.2 convert_reduce_fusion.1
  3.0 0.9 select_reduce_fusion
  3.9 0.2 select_reduce_fusion.2
  4.1 0.1 select_reduce_fusion.1
  4.2 1.2 copy-done
  5.4 3.7 %shard_map.127 = (bf16[256,960]{1,0:T(8,128)(2,1)S(1)}, f32[256,1024]{1,0:T(8,128)S(1)}, f32[256,1024]{1,0:T(8,128)S(1)}, f32[256,1024]{1,0:T(8,128)S(1)}) custom-call(s32[1]{0:T(128)} %bitcast.3.at_ref, bf16[256,1920]{1,0:T(8,128)(2,1)S(1)} %copy-done, f32[1,1920]{1,0:T(1,128)S(1)} %broadcast_in_dim.71.gain, bf16[960,1024]{1,0:T(8,128)(2,1)} %refs_0_.1, ...), custom_call_target="tpu_custom_call" | custom-call | flops 1509949440 | bytes 6881280 | tf_op jit(solution)/shard_map/pallas_call | solution.py:83
  9.1 0.0 collective-permute-done.refs_4_
  9.1 0.0 collective-permute-done.1.refs_5_
  9.1 0.8 collective-permute-done.2.refs_6_
  9.9 4.7 %shard_map.128.context = bf16[256,1024]{1,0:T(8,128)(2,1)S(1)} custom-call(f32[256,128]{1,0:T(8,128)S(1)} %fusion.bias, bf16[256,960]{1,0:T(8,128)(2,1)S(1)} %get-tuple-element.60.refs_0_, f32[256,1024]{1,0:T(8,128)S(1)} %get-tuple-element.61.refs_1_, f32[256,1024]{1,0:T(8,128)S(1)} %get-tuple-element.62.refs_2_, f32[256,1024]{1,0:T(8,128)S(1)} %get-tuple-element.63.refs_3_, ...), custom_call_target="tpu_custom_call" | custom-call | flops 3019898880 | bytes 9043968 | tf_op jit(solution)/shard_map/pallas_call | solution.py:139
  14.7 0.0 collective-permute-done.3.refs_1_
  14.7 0.2 collective-permute-start.12
  14.9 0.4 collective-permute-start.13
  15.3 5.2 %shard_map.129 = (bf16[256,1920]{1,0:T(8,128)(2,1)S(1)}, bf16[8,32,1920]{2,1,0:T(8,128)(2,1)}, bf16[32,1920]{1,0:T(8,128)(2,1)S(1)}, bf16[32,1920]{1,0:T(8,128)(...) custom-call(s32[1]{0:T(128)} %bitcast.3.at_ref, ...), custom_call_target="tpu_custom_call" | custom-call | flops 1006632960 | bytes 5439488 | tf_op jit(solution)/shard_map/pallas_call | solution.py:190
  20.4 4.8 %all-to-all-start = ((bf16[8,32,1920]{2,1,0:T(8,128)(2,1)}), bf16[8,32,1920]{2,1,0:T(8,128)(2,1)S(1)}, u32[]{:S(2)}, u32[]{:S(2)}) async-start(bf16[8,32,1920]{2,1,0:T(8,128)(2,1)} %get-tuple-element.71), calls=%async_computation | async-start | bytes 1966080 | tf_op jit(solution)/shard_map/all_to_all | solution.py:416
  25.2 0.3 collective-permute-start.4
  25.5 4.0 %collective-permute-start.5 = (bf16[32,1920]{1,0:T(8,128)(2,1)S(1)}, bf16[32,1920]{1,0:T(8,128)(2,1)S(1)}, u32[]{:S(2)}, u32[]{:S(2)}) collective-permute-start(bf16[32,1920]{1,0:T(8,128)(2,1)S(1)} %get-tuple-element.73), channel_id=1, source_target_pairs={{0,18},{2,16},{4,22},{6,20},{8,26},{10,24},{12,30},{14,28},{16,2},... | collective-permute-start | bytes 368648 | tf_op jit(solution)/shard_map/ppermute | solution.py:408
  29.6 1.2 collective-permute-start.6
  31.5 9.0 %collective-permute-done.4.refs_1_.refs_0_ = bf16[32,1920]{1,0:T(8,128)(2,1)S(1)} collective-permute-done((bf16[32,1920]{1,0:T(8,128)(2,1)S(1)}, bf16[32,1920]{1,0:T(8,128)(2,1)S(1)}, u32[]{:S(2)}, u32[]{:S(2)}) %collective-permute-start.4) | collective-permute-done | bytes 122912 | tf_op jit(solution)/shard_map/ppermute | solution.py:408
  40.5 2.0 %collective-permute-start.7 = (bf16[32,1920]{1,0:T(8,128)(2,1)}, bf16[32,1920]{1,0:T(8,128)(2,1)S(1)}, u32[]{:S(2)}, u32[]{:S(2)}) collective-permute-start(bf16[32,1920]{1,0:T(8,128)(2,1)} %get-tuple-element.76), channel_id=1, source_target_pairs={{0,22},{2,20},{4,18},{6,16},{8,30},{10,28},{12,26},{14,24},{16,6},... | collective-permute-start | bytes 368648 | tf_op jit(solution)/shard_map/ppermute | solution.py:408
  42.5 2.3 %collective-permute-done.5.refs_2_.refs_1_ = bf16[32,1920]{1,0:T(8,128)(2,1)S(1)} collective-permute-done((bf16[32,1920]{1,0:T(8,128)(2,1)S(1)}, bf16[32,1920]{1,0:T(8,128)(2,1)S(1)}, u32[]{:S(2)}, u32[]{:S(2)}) %collective-permute-start.5) | collective-permute-done | bytes 122912 | tf_op jit(solution)/shard_map/ppermute | solution.py:408
  44.8 2.7 %collective-permute-start.8 = (bf16[32,1920]{1,0:T(8,128)(2,1)S(1)}, bf16[32,1920]{1,0:T(8,128)(2,1)S(1)}, u32[]{:S(2)}, u32[]{:S(2)}) collective-permute-start(bf16[32,1920]{1,0:T(8,128)(2,1)S(1)} %get-tuple-element.78), channel_id=1, source_target_pairs={{0,24},{2,26},{4,28},{6,30},{8,16},{10,18},{12,20},{14,22},{16,8},... | collective-permute-start | bytes 368648 | tf_op jit(solution)/shard_map/ppermute | solution.py:408
  47.4 0.0 collective-permute-done.6.refs_3_.refs_2_
  47.4 3.7 %collective-permute-start.9 = (bf16[32,1920]{1,0:T(8,128)(2,1)S(1)}, bf16[32,1920]{1,0:T(8,128)(2,1)S(1)}, u32[]{:S(2)}, u32[]{:S(2)}) collective-permute-start(bf16[32,1920]{1,0:T(8,128)(2,1)S(1)} %get-tuple-element.80), channel_id=1, source_target_pairs={{0,26},{2,24},{4,30},{6,28},{8,18},{10,16},{12,22},{14,20},{16,10}... | collective-permute-start | bytes 368648 | tf_op jit(solution)/shard_map/ppermute | solution.py:408
  51.2 0.0 collective-permute-done.12.refs_5_.refs_6_
  51.2 0.0 collective-permute-start.10
  51.2 0.0 collective-permute-done.13.refs_7_.refs_8_
  51.2 2.5 %collective-permute-start.11 = (bf16[32,1920]{1,0:T(8,128)(2,1)S(1)}, bf16[32,1920]{1,0:T(8,128)(2,1)S(1)}, u32[]{:S(2)}, u32[]{:S(2)}) collective-permute-start(bf16[32,1920]{1,0:T(8,128)(2,1)S(1)} %get-tuple-element.84), channel_id=1, source_target_pairs={{0,30},{2,28},{4,26},{6,24},{8,22},{10,20},{12,18},{14,16},{16,14}... | collective-permute-start | bytes 368648 | tf_op jit(solution)/shard_map/ppermute | solution.py:408
  53.7 0.0 all-to-all-done.near
  53.7 19.1 %shard_map.130 = (bf16[256,1920]{1,0:T(8,128)(2,1)S(1)}, bf16[32,1920]{1,0:T(8,128)(2,1)S(1)}, bf16[32,1920]{1,0:T(8,128)(2,1)S(1)}, bf16[32,1920]{1,0:T(8,128)(2,1)S(1)}) custom-call(s32[1]{0:T(128)} %constant.38.clone.1.live, bf16[256,1920]{1,0:T(8,128)(2,1)S(1)} %bitcast.11, bf16[32,1920]{1,0:T(8,128)(2,1)S(1)} %collective-permute-done.4.refs_1_.refs_0_, ...), custom_call_target="tpu_custom_call" | custom-call | flops 11072962560 | bytes 31457280 | tf_op jit(solution)/shard_map/pallas_call | solution.py:313
  72.9 0.0 collective-permute-done.7.refs_3_.refs_0_
  72.9 0.0 collective-permute-done.8.refs_4_.refs_1_
  72.9 0.0 collective-permute-done.9.refs_5_.refs_2_
  72.9 0.0 collective-permute-done.10.refs_6_.refs_3_
  72.9 0.5 collective-permute-done.11.refs_7_.refs_4_
  73.4 1.4 %shard_map.131 = (bf16[8,32,1920]{2,1,0:T(8,128)(2,1)}, bf16[32,1920]{1,0:T(8,128)(2,1)S(1)}, bf16[32,1920]{1,0:T(8,128)(2,1)S(1)}, bf16[32,1920]{1,0:T(8,128)(2,1)S(1)}, s32[16]{0:T(128)S(1)}) custom-call(s32[1]{0:T(128)} %bitcast.6.at_ref, s32[1,1]{1,0:T(1,128)S(6)} %copy.17.blocks_ref, bf16[8,32,1920]{2,1,0:T(8,128)(2,1)S(1)} %all-to-all-done.near, ...), custom_call_target="tpu_custom_call" | custom-call | tf_op jit(solution)/shard_map/pallas_call | solution.py:256
  74.8 3.7 %all-to-all-start.1 = ((bf16[8,32,1920]{2,1,0:T(8,128)(2,1)}), bf16[8,32,1920]{2,1,0:T(8,128)(2,1)S(1)}, u32[]{:S(2)}, u32[]{:S(2)}) async-start(bf16[8,32,1920]{2,1,0:T(8,128)(2,1)} %get-tuple-element.91), calls=%async_computation.1 | async-start | bytes 1966080 | tf_op jit(solution)/shard_map/all_to_all | solution.py:416
  78.5 1.7 %collective-permute-start.14 = (bf16[32,1920]{1,0:T(8,128)(2,1)S(1)}, bf16[32,1920]{1,0:T(8,128)(2,1)S(1)}, u32[]{:S(2)}, u32[]{:S(2)}) collective-permute-start(bf16[32,1920]{1,0:T(8,128)(2,1)S(1)} %get-tuple-element.92), channel_id=1, source_target_pairs={{0,16},{2,18},{4,20},{6,22},{8,24},{10,26},{12,28},{14,30},{16,0},... | collective-permute-start | bytes 368648 | tf_op jit(solution)/shard_map/ppermute | solution.py:408
  80.3 2.6 %collective-permute-start.15 = (bf16[32,1920]{1,0:T(8,128)(2,1)S(1)}, bf16[32,1920]{1,0:T(8,128)(2,1)S(1)}, u32[]{:S(2)}, u32[]{:S(2)}) collective-permute-start(bf16[32,1920]{1,0:T(8,128)(2,1)S(1)} %get-tuple-element.93), channel_id=1, source_target_pairs={{0,18},{2,16},{4,22},{6,20},{8,26},{10,24},{12,30},{14,28},{16,2},... | collective-permute-start | bytes 368648 | tf_op jit(solution)/shard_map/ppermute | solution.py:408
  82.9 2.7 %collective-permute-start.16 = (bf16[32,1920]{1,0:T(8,128)(2,1)S(1)}, bf16[32,1920]{1,0:T(8,128)(2,1)S(1)}, u32[]{:S(2)}, u32[]{:S(2)}) collective-permute-start(bf16[32,1920]{1,0:T(8,128)(2,1)S(1)} %get-tuple-element.94), channel_id=1, source_target_pairs={{0,20},{2,22},{4,16},{6,18},{8,28},{10,30},{12,24},{14,26},{16,4},... | collective-permute-start | bytes 368648 | tf_op jit(solution)/shard_map/ppermute | solution.py:408
  85.5 14.3 %shard_map.132 = (bf16[32,1920]{1,0:T(8,128)(2,1)S(1)}, bf16[32,1920]{1,0:T(8,128)(2,1)S(1)}, bf16[32,1920]{1,0:T(8,128)(2,1)S(1)}, bf16[32,1920]{1,0:T(8,128)(2,1)S(1)}, bf16[32,1920]{1,0:T(8,128)(2,1)S(1)}) custom-call(s32[16]{0:T(128)S(1)} %get-tuple-element.95.live, bf16[32,1920]{1,0:T(8,128)(2,1)S(1)} %collective-permute-done.7.refs_3_.refs_0_, ...), custom_call_target="tpu_custom_call" | custom-call | flops 5033164800 | bytes 31457280 | tf_op jit(solution)/shard_map/pallas_call | solution.py:313
  99.9 0.0 collective-permute-done.15.refs_1_
  99.9 0.7 collective-permute-done.16.refs_2_
  100.7 0.4 collective-permute-start.17
  101.1 2.3 %collective-permute-start.18 = (bf16[32,1920]{1,0:T(8,128)(2,1)S(1)}, bf16[32,1920]{1,0:T(8,128)(2,1)S(1)}, u32[]{:S(2)}, u32[]{:S(2)}) collective-permute-start(bf16[32,1920]{1,0:T(8,128)(2,1)S(1)} %get-tuple-element.107), channel_id=1, source_target_pairs={{0,24},{2,26},{4,28},{6,30},{8,16},{10,18},{12,20},{14,22},{16,8},... | collective-permute-start | bytes 368648 | tf_op jit(solution)/shard_map/ppermute | solution.py:408
  103.4 0.7 collective-permute-start.19
  104.1 2.7 %collective-permute-start.20 = (bf16[32,1920]{1,0:T(8,128)(2,1)S(1)}, bf16[32,1920]{1,0:T(8,128)(2,1)S(1)}, u32[]{:S(2)}, u32[]{:S(2)}) collective-permute-start(bf16[32,1920]{1,0:T(8,128)(2,1)S(1)} %get-tuple-element.109), channel_id=1, source_target_pairs={{0,28},{2,30},{4,24},{6,26},{8,20},{10,22},{12,16},{14,18},{16,12}... | collective-permute-start | bytes 368648 | tf_op jit(solution)/shard_map/ppermute | solution.py:408
  106.7 0.5 collective-permute-start.21
  107.2 10.6 %collective-permute-done.17.refs_3_ = bf16[32,1920]{1,0:T(8,128)(2,1)S(1)} collective-permute-done((bf16[32,1920]{1,0:T(8,128)(2,1)S(1)}, bf16[32,1920]{1,0:T(8,128)(2,1)S(1)}, u32[]{:S(2)}, u32[]{:S(2)}) %collective-permute-start.17) | collective-permute-done | bytes 122912 | tf_op jit(solution)/shard_map/ppermute | solution.py:408
  117.8 4.7 %collective-permute-done.18.refs_4_ = bf16[32,1920]{1,0:T(8,128)(2,1)S(1)} collective-permute-done((bf16[32,1920]{1,0:T(8,128)(2,1)S(1)}, bf16[32,1920]{1,0:T(8,128)(2,1)S(1)}, u32[]{:S(2)}, u32[]{:S(2)}) %collective-permute-start.18) | collective-permute-done | bytes 122912 | tf_op jit(solution)/shard_map/ppermute | solution.py:408
  122.5 2.7 %collective-permute-done.19.refs_5_ = bf16[32,1920]{1,0:T(8,128)(2,1)S(1)} collective-permute-done((bf16[32,1920]{1,0:T(8,128)(2,1)S(1)}, bf16[32,1920]{1,0:T(8,128)(2,1)S(1)}, u32[]{:S(2)}, u32[]{:S(2)}) %collective-permute-start.19) | collective-permute-done | bytes 122912 | tf_op jit(solution)/shard_map/ppermute | solution.py:408
  125.2 3.2 %collective-permute-done.20.refs_6_ = bf16[32,1920]{1,0:T(8,128)(2,1)S(1)} collective-permute-done((bf16[32,1920]{1,0:T(8,128)(2,1)S(1)}, bf16[32,1920]{1,0:T(8,128)(2,1)S(1)}, u32[]{:S(2)}, u32[]{:S(2)}) %collective-permute-start.20) | collective-permute-done | bytes 122912 | tf_op jit(solution)/shard_map/ppermute | solution.py:408
  128.4 1.8 %collective-permute-done.21.refs_7_ = bf16[32,1920]{1,0:T(8,128)(2,1)S(1)} collective-permute-done((bf16[32,1920]{1,0:T(8,128)(2,1)S(1)}, bf16[32,1920]{1,0:T(8,128)(2,1)S(1)}, u32[]{:S(2)}, u32[]{:S(2)}) %collective-permute-start.21) | collective-permute-done | bytes 122912 | tf_op jit(solution)/shard_map/ppermute | solution.py:408
  130.2 0.0 all-to-all-done.1.near
  130.2 1.9 %shard_map.133 = bf16[256,1920]{1,0:T(8,128)(2,1)} custom-call(s32[16]{0:T(128)S(1)} %broadcast_subtract_fusion.run_ref, bf16[256,1920]{1,0:T(8,128)(2,1)S(1)} %get-tuple-element.70.hidden, bf16[8,32,1920]{2,1,0:T(8,128)(2,1)S(1)} %all-to-all-done.1.near, bf16[32,1920]{1,0:T(8,128)(2,1)S(1)} %collective-permute-done.14.refs_0_, ...), custom_call_target="tpu_custom_call" | custom-call | tf_op jit(solution)/shard_map/pallas_call | solution.py:223
  (12 shorter events, 0.1 us)
Async XLA Ops:
  0.0 9.1 %collective-permute-start = (bf16[960,1024]{1,0:T(8,128)(2,1)}, bf16[960,1024]{1,0:T(8,128)(2,1)}, u32[]{:S(2)}, u32[]{:S(2)}) collective-permute-start(bf16[960,1024]{1,0:T(8,128)(2,1)} %refs_0_.1), channel_id=1, source_target_pairs={{0,1},{1,0},{2,3},{3,2},{4,5},{5,4},{6,7},{7,6},{8,9},{9,8},{10,11... | collective-permute-start | bytes 5898248 | tf_op jit(solution)/shard_map/ppermute | solution.py:359
  0.0 9.1 %collective-permute-start.1 = (bf16[960,1024]{1,0:T(8,128)(2,1)}, bf16[960,1024]{1,0:T(8,128)(2,1)}, u32[]{:S(2)}, u32[]{:S(2)}) collective-permute-start(bf16[960,1024]{1,0:T(8,128)(2,1)} %refs_1_.1), channel_id=1, source_target_pairs={{0,1},{1,0},{2,3},{3,2},{4,5},{5,4},{6,7},{7,6},{8,9},{9,8},{10,11... | collective-permute-start | bytes 5898248 | tf_op jit(solution)/shard_map/ppermute | solution.py:359
  0.5 9.4 %collective-permute-start.2 = (bf16[960,1024]{1,0:T(8,128)(2,1)}, bf16[960,1024]{1,0:T(8,128)(2,1)}, u32[]{:S(2)}, u32[]{:S(2)}) collective-permute-start(bf16[960,1024]{1,0:T(8,128)(2,1)} %refs_2_.1), channel_id=1, source_target_pairs={{0,1},{1,0},{2,3},{3,2},{4,5},{5,4},{6,7},{7,6},{8,9},{9,8},{10,11... | collective-permute-start | bytes 5898248 | tf_op jit(solution)/shard_map/ppermute | solution.py:359
  0.5 14.1 %collective-permute-start.3 = (bf16[512,1920]{1,0:T(8,128)(2,1)}, bf16[512,1920]{1,0:T(8,128)(2,1)}, u32[]{:S(2)}, u32[]{:S(2)}) collective-permute-start(bf16[512,1920]{1,0:T(8,128)(2,1)} %refs_0_.2), channel_id=1, source_target_pairs={{0,1},{1,0},{2,3},{3,2},{4,5},{5,4},{6,7},{7,6},{8,9},{9,8},{10,11... | collective-permute-start | bytes 5898248 | tf_op jit(solution)/shard_map/ppermute | solution.py:359
  4.2 1.2 copy-start
  9.9 5.3 %copy-start.2 = (f32[1920]{0:T(1024)S(1)}, f32[1920]{0:T(1024)}, u32[]{:S(2)}) copy-start(f32[1920]{0:T(1024)} %param.23) | copy-start | bytes 23044
  9.9 5.3 %copy-start.1 = (bf16[256,1920]{1,0:T(8,128)(2,1)S(1)}, bf16[256,1920]{1,0:T(8,128)(2,1)}, u32[]{:S(2)}) copy-start(bf16[256,1920]{1,0:T(8,128)(2,1)} %tokens.3) | copy-start | bytes 2949124
  14.7 36.5 %collective-permute-start.12 = (bf16[1920,2048]{1,0:T(8,128)(2,1)}, bf16[1920,2048]{1,0:T(8,128)(2,1)}, u32[]{:S(2)}, u32[]{:S(2)}) collective-permute-start(bf16[1920,2048]{1,0:T(8,128)(2,1)} %bitcast.4.refs_4_.refs_5_), channel_id=1, source_target_pairs={{0,1},{1,0},{2,3},{3,2},{4,5},{5,4},{6,7},{7,6},{8,9},{9,8},{10,11... | collective-permute-start | bytes 23592968 | tf_op jit(solution)/shard_map/ppermute | solution.py:359
  14.9 36.3 %collective-permute-start.13 = (bf16[2048,1920]{1,0:T(8,128)(2,1)}, bf16[2048,1920]{1,0:T(8,128)(2,1)}, u32[]{:S(2)}, u32[]{:S(2)}) collective-permute-start(bf16[2048,1920]{1,0:T(8,128)(2,1)} %bitcast.5.refs_6_.refs_7_), channel_id=1, source_target_pairs={{0,1},{1,0},{2,3},{3,2},{4,5},{5,4},{6,7},{7,6},{8,9},{9,8},{10,11... | collective-permute-start | bytes 23592968 | tf_op jit(solution)/shard_map/ppermute | solution.py:359
  20.4 33.3 %all-to-all-start = ((bf16[8,32,1920]{2,1,0:T(8,128)(2,1)}), bf16[8,32,1920]{2,1,0:T(8,128)(2,1)S(1)}, u32[]{:S(2)}, u32[]{:S(2)}) async-start(bf16[8,32,1920]{2,1,0:T(8,128)(2,1)} %get-tuple-element.71), calls=%async_computation | async-start | bytes 1966080 | tf_op jit(solution)/shard_map/all_to_all | solution.py:416
  25.2 15.3 %collective-permute-start.4 = (bf16[32,1920]{1,0:T(8,128)(2,1)S(1)}, bf16[32,1920]{1,0:T(8,128)(2,1)S(1)}, u32[]{:S(2)}, u32[]{:S(2)}) collective-permute-start(bf16[32,1920]{1,0:T(8,128)(2,1)S(1)} %get-tuple-element.72), channel_id=1, source_target_pairs={{0,16},{2,18},{4,20},{6,22},{8,24},{10,26},{12,28},{14,30},{16,0},... | collective-permute-start | bytes 368648 | tf_op jit(solution)/shard_map/ppermute | solution.py:408
  25.5 19.2 %collective-permute-start.5 = (bf16[32,1920]{1,0:T(8,128)(2,1)S(1)}, bf16[32,1920]{1,0:T(8,128)(2,1)S(1)}, u32[]{:S(2)}, u32[]{:S(2)}) collective-permute-start(bf16[32,1920]{1,0:T(8,128)(2,1)S(1)} %get-tuple-element.73), channel_id=1, source_target_pairs={{0,18},{2,16},{4,22},{6,20},{8,26},{10,24},{12,30},{14,28},{16,2},... | collective-permute-start | bytes 368648 | tf_op jit(solution)/shard_map/ppermute | solution.py:408
  29.6 17.9 %collective-permute-start.6 = (bf16[32,1920]{1,0:T(8,128)(2,1)S(1)}, bf16[32,1920]{1,0:T(8,128)(2,1)S(1)}, u32[]{:S(2)}, u32[]{:S(2)}) collective-permute-start(bf16[32,1920]{1,0:T(8,128)(2,1)S(1)} %get-tuple-element.74), channel_id=1, source_target_pairs={{0,20},{2,22},{4,16},{6,18},{8,28},{10,30},{12,24},{14,26},{16,4},... | collective-permute-start | bytes 368648 | tf_op jit(solution)/shard_map/ppermute | solution.py:408
  40.5 32.4 %collective-permute-start.7 = (bf16[32,1920]{1,0:T(8,128)(2,1)}, bf16[32,1920]{1,0:T(8,128)(2,1)S(1)}, u32[]{:S(2)}, u32[]{:S(2)}) collective-permute-start(bf16[32,1920]{1,0:T(8,128)(2,1)} %get-tuple-element.76), channel_id=1, source_target_pairs={{0,22},{2,20},{4,18},{6,16},{8,30},{10,28},{12,26},{14,24},{16,6},... | collective-permute-start | bytes 368648 | tf_op jit(solution)/shard_map/ppermute | solution.py:408
  44.8 28.1 %collective-permute-start.8 = (bf16[32,1920]{1,0:T(8,128)(2,1)S(1)}, bf16[32,1920]{1,0:T(8,128)(2,1)S(1)}, u32[]{:S(2)}, u32[]{:S(2)}) collective-permute-start(bf16[32,1920]{1,0:T(8,128)(2,1)S(1)} %get-tuple-element.78), channel_id=1, source_target_pairs={{0,24},{2,26},{4,28},{6,30},{8,16},{10,18},{12,20},{14,22},{16,8},... | collective-permute-start | bytes 368648 | tf_op jit(solution)/shard_map/ppermute | solution.py:408
  47.4 25.4 %collective-permute-start.9 = (bf16[32,1920]{1,0:T(8,128)(2,1)S(1)}, bf16[32,1920]{1,0:T(8,128)(2,1)S(1)}, u32[]{:S(2)}, u32[]{:S(2)}) collective-permute-start(bf16[32,1920]{1,0:T(8,128)(2,1)S(1)} %get-tuple-element.80), channel_id=1, source_target_pairs={{0,26},{2,24},{4,30},{6,28},{8,18},{10,16},{12,22},{14,20},{16,10}... | collective-permute-start | bytes 368648 | tf_op jit(solution)/shard_map/ppermute | solution.py:408
  51.2 21.7 %collective-permute-start.10 = (bf16[32,1920]{1,0:T(8,128)(2,1)S(1)}, bf16[32,1920]{1,0:T(8,128)(2,1)S(1)}, u32[]{:S(2)}, u32[]{:S(2)}) collective-permute-start(bf16[32,1920]{1,0:T(8,128)(2,1)S(1)} %get-tuple-element.82), channel_id=1, source_target_pairs={{0,28},{2,30},{4,24},{6,26},{8,20},{10,22},{12,16},{14,18},{16,12}... | collective-permute-start | bytes 368648 | tf_op jit(solution)/shard_map/ppermute | solution.py:408
  51.2 22.2 %collective-permute-start.11 = (bf16[32,1920]{1,0:T(8,128)(2,1)S(1)}, bf16[32,1920]{1,0:T(8,128)(2,1)S(1)}, u32[]{:S(2)}, u32[]{:S(2)}) collective-permute-start(bf16[32,1920]{1,0:T(8,128)(2,1)S(1)} %get-tuple-element.84), channel_id=1, source_target_pairs={{0,30},{2,28},{4,26},{6,24},{8,22},{10,20},{12,18},{14,16},{16,14}... | collective-permute-start | bytes 368648 | tf_op jit(solution)/shard_map/ppermute | solution.py:408
  74.8 55.5 %all-to-all-start.1 = ((bf16[8,32,1920]{2,1,0:T(8,128)(2,1)}), bf16[8,32,1920]{2,1,0:T(8,128)(2,1)S(1)}, u32[]{:S(2)}, u32[]{:S(2)}) async-start(bf16[8,32,1920]{2,1,0:T(8,128)(2,1)} %get-tuple-element.91), calls=%async_computation.1 | async-start | bytes 1966080 | tf_op jit(solution)/shard_map/all_to_all | solution.py:416
  78.5 21.4 %collective-permute-start.14 = (bf16[32,1920]{1,0:T(8,128)(2,1)S(1)}, bf16[32,1920]{1,0:T(8,128)(2,1)S(1)}, u32[]{:S(2)}, u32[]{:S(2)}) collective-permute-start(bf16[32,1920]{1,0:T(8,128)(2,1)S(1)} %get-tuple-element.92), channel_id=1, source_target_pairs={{0,16},{2,18},{4,20},{6,22},{8,24},{10,26},{12,28},{14,30},{16,0},... | collective-permute-start | bytes 368648 | tf_op jit(solution)/shard_map/ppermute | solution.py:408
  80.3 19.7 %collective-permute-start.15 = (bf16[32,1920]{1,0:T(8,128)(2,1)S(1)}, bf16[32,1920]{1,0:T(8,128)(2,1)S(1)}, u32[]{:S(2)}, u32[]{:S(2)}) collective-permute-start(bf16[32,1920]{1,0:T(8,128)(2,1)S(1)} %get-tuple-element.93), channel_id=1, source_target_pairs={{0,18},{2,16},{4,22},{6,20},{8,26},{10,24},{12,30},{14,28},{16,2},... | collective-permute-start | bytes 368648 | tf_op jit(solution)/shard_map/ppermute | solution.py:408
  82.9 17.8 %collective-permute-start.16 = (bf16[32,1920]{1,0:T(8,128)(2,1)S(1)}, bf16[32,1920]{1,0:T(8,128)(2,1)S(1)}, u32[]{:S(2)}, u32[]{:S(2)}) collective-permute-start(bf16[32,1920]{1,0:T(8,128)(2,1)S(1)} %get-tuple-element.94), channel_id=1, source_target_pairs={{0,20},{2,22},{4,16},{6,18},{8,28},{10,30},{12,24},{14,26},{16,4},... | collective-permute-start | bytes 368648 | tf_op jit(solution)/shard_map/ppermute | solution.py:408
  100.7 17.1 %collective-permute-start.17 = (bf16[32,1920]{1,0:T(8,128)(2,1)S(1)}, bf16[32,1920]{1,0:T(8,128)(2,1)S(1)}, u32[]{:S(2)}, u32[]{:S(2)}) collective-permute-start(bf16[32,1920]{1,0:T(8,128)(2,1)S(1)} %get-tuple-element.106), channel_id=1, source_target_pairs={{0,22},{2,20},{4,18},{6,16},{8,30},{10,28},{12,26},{14,24},{16,6},... | collective-permute-start | bytes 368648 | tf_op jit(solution)/shard_map/ppermute | solution.py:408
  101.1 21.4 %collective-permute-start.18 = (bf16[32,1920]{1,0:T(8,128)(2,1)S(1)}, bf16[32,1920]{1,0:T(8,128)(2,1)S(1)}, u32[]{:S(2)}, u32[]{:S(2)}) collective-permute-start(bf16[32,1920]{1,0:T(8,128)(2,1)S(1)} %get-tuple-element.107), channel_id=1, source_target_pairs={{0,24},{2,26},{4,28},{6,30},{8,16},{10,18},{12,20},{14,22},{16,8},... | collective-permute-start | bytes 368648 | tf_op jit(solution)/shard_map/ppermute | solution.py:408
  103.4 21.8 %collective-permute-start.19 = (bf16[32,1920]{1,0:T(8,128)(2,1)S(1)}, bf16[32,1920]{1,0:T(8,128)(2,1)S(1)}, u32[]{:S(2)}, u32[]{:S(2)}) collective-permute-start(bf16[32,1920]{1,0:T(8,128)(2,1)S(1)} %get-tuple-element.108), channel_id=1, source_target_pairs={{0,26},{2,24},{4,30},{6,28},{8,18},{10,16},{12,22},{14,20},{16,10}... | collective-permute-start | bytes 368648 | tf_op jit(solution)/shard_map/ppermute | solution.py:408
  104.1 24.3 %collective-permute-start.20 = (bf16[32,1920]{1,0:T(8,128)(2,1)S(1)}, bf16[32,1920]{1,0:T(8,128)(2,1)S(1)}, u32[]{:S(2)}, u32[]{:S(2)}) collective-permute-start(bf16[32,1920]{1,0:T(8,128)(2,1)S(1)} %get-tuple-element.109), channel_id=1, source_target_pairs={{0,28},{2,30},{4,24},{6,26},{8,20},{10,22},{12,16},{14,18},{16,12}... | collective-permute-start | bytes 368648 | tf_op jit(solution)/shard_map/ppermute | solution.py:408
  106.7 23.5 %collective-permute-start.21 = (bf16[32,1920]{1,0:T(8,128)(2,1)S(1)}, bf16[32,1920]{1,0:T(8,128)(2,1)S(1)}, u32[]{:S(2)}, u32[]{:S(2)}) collective-permute-start(bf16[32,1920]{1,0:T(8,128)(2,1)S(1)} %get-tuple-element.110), channel_id=1, source_target_pairs={{0,30},{2,28},{4,26},{6,24},{8,22},{10,20},{12,18},{14,16},{16,14}... | collective-permute-start | bytes 368648 | tf_op jit(solution)/shard_map/ppermute | solution.py:408

commit v6 on v5

--- a/solution.py
+++ b/solution.py
@@ -9,8 +9,9 @@
 
 HDIM = 128
 BLOCK = 128
+AHEAD = 20_000_000_000
 VMEM_LIMIT = 42 * 1024 * 1024
-FRONT_LIMIT = 24 * 1024 * 1024
+FRONT_LIMIT = 48 * 1024 * 1024
 
 EMPTY = 1024.0
 
@@ -205,28 +206,50 @@
     return out[0], out[1:]
 
 
-def mix_kernel(runs, run_ref, hidden, near, *refs):
-    far, mixed = refs[:-1], refs[-1]
-    rows = hidden.shape[0] // runs
-    half = near.shape[0]
-    for k in range(half + len(far)):
+def mix_kernel(runs, run_ref, base, *refs):
+    ins, mixed = refs[:-1], refs[-1]
+    rows = base.shape[0] // runs
+    mixed[...] = base[...]
+    for k, ref in enumerate(ins):
 
         @pl.when(run_ref[k] < runs)
         def _():
             run = pl.ds(pl.multiple_of(run_ref[k] * rows, rows), rows)
-            expert = near[k] if k < half else far[k - half][...]
-            total = hidden[run, :].astype(jnp.float32) + expert.astype(jnp.float32)
+            total = base[run, :].astype(jnp.float32) + ref[...].astype(jnp.float32)
             mixed[run, :] = total.astype(jnp.bfloat16)
 
 
-def mix(run_of_slot, hidden, near, far, runs):
+def near_mix_kernel(runs, run_ref, base, near, *refs):
+    mix_kernel(runs, run_ref, base, *[near.at[k] for k in range(near.shape[0])], *refs)
+
+
+def mix(run_of_slot, base, ins, runs, weight=0):
+    kernel = near_mix_kernel if ins[0].ndim == 3 else mix_kernel
     return pl.pallas_call(
-        functools.partial(mix_kernel, runs),
-        in_specs=[pl.BlockSpec(memory_space=pltpu.SMEM)] + in_vmem(2 + len(far)),
+        functools.partial(kernel, runs),
+        in_specs=[pl.BlockSpec(memory_space=pltpu.SMEM)] + in_vmem(1 + len(ins)),
         out_specs=in_vmem(1)[0],
-        out_shape=jax.ShapeDtypeStruct(hidden.shape, jnp.bfloat16),
+        out_shape=jax.ShapeDtypeStruct(base.shape, jnp.bfloat16),
         compiler_params=pltpu.CompilerParams(vmem_limit_bytes=FRONT_LIMIT),
-    )(run_of_slot, hidden, near, *far)
+        cost_estimate=cost(weight, base, base, *ins),
+    )(run_of_slot, base, *ins)
+
+
+def stage_kernel(*refs):
+    count = len(refs) // 2
+    for ref, out in zip(refs[:count], refs[count:]):
+        out[...] = ref[...]
+
+
+def stage(arrays):
+    return pl.pallas_call(
+        stage_kernel,
+        in_specs=in_vmem(len(arrays)),
+        out_specs=in_vmem(len(arrays)),
+        out_shape=[pltpu.VMEM(a.shape, a.dtype) for a in arrays],
+        compiler_params=pltpu.CompilerParams(vmem_limit_bytes=FRONT_LIMIT),
+        cost_estimate=cost(AHEAD, *arrays),
+    )(*arrays)
 
 
 def live_kernel(first, at_ref, blocks_ref, near, *refs):
@@ -241,12 +264,8 @@
     for k in range(half + len(far)):
         before = sum(jnp.where(s < source[k], f, 0) for s, f in zip(source, full))
         live[k] = (before * rows // BLOCK < blocks_ref[0, 0]).astype(jnp.int32)
-    for k in range(half):
-        part = slice(k * rows, (k + 1) * rows)
-        kept = live[k] > 0
-        outs[0][k] = jnp.where(kept, results[0][part, :], jnp.zeros_like(outs[0][k]))
-    for k in range(1, first):
-        kept = live[half + k - 1] > 0
+    for k in range(first):
+        kept = live[half + k] > 0
         outs[k][...] = jnp.where(kept, results[k][...], jnp.zeros_like(results[k]))
 
 
@@ -257,7 +276,7 @@
         functools.partial(live_kernel, first),
         in_specs=[smem] * 2 + in_vmem(1 + len(far) + first),
         out_specs=in_vmem(first) + [smem],
-        out_shape=[jax.ShapeDtypeStruct(r.shape, r.dtype) for r in (near, *results[1:])]
+        out_shape=[jax.ShapeDtypeStruct(r.shape, r.dtype) for r in results]
         + [jax.ShapeDtypeStruct((near.shape[0] + len(far),), jnp.int32)],
         compiler_params=pltpu.CompilerParams(vmem_limit_bytes=FRONT_LIMIT),
     )(at, blocks, near, *far, *results)
@@ -420,23 +439,24 @@
         def after(arrays, *done):
             return list(lax.optimization_barrier((tuple(arrays), done))[0])
 
-        quarter = half * 3 // 8
+        quarter = half // 2
         far, last = range(half, half + quarter), range(half + quarter, lang_count)
         far_in = swap(far, slots[1 : 1 + quarter])
         near_in = within(slots[0])
         last_in = []
         for n, k in enumerate(last):
-            done = far_in[min(n, quarter - 1)]
+            done = far_in[min(n, quarter - 2)]
             last_in += swap([k], after([slots[1 + quarter + n]], done))
-        ins = [near_in.reshape(half * capacity, width), *far_in]
-        out = expert_ffn(ins, first, second)
-        (near_out, *far_out), live = live_rows(lang_scalar, blocks, near_in, [*far_in, *last_in], out)
-        last_in = after(last_in, far_out)
+        far_out = expert_ffn(stage(far_in), first, second)
+        far_out, live = live_rows(lang_scalar, blocks, near_in, [*far_in, *last_in], far_out)
+        ins = after([near_in.reshape(half * capacity, width), *last_in], far_out)
         far_back = swap(far, far_out)
-        near_back = within(near_out)
-        last_out = expert_ffn(last_in, first, second, live, [[k] for k in last])
-        last_back = swap(last, after(last_out, far_back))
-        return mix(run_of_slot, hidden, near_back, far_back + last_back, slots_dev)
+        held = [list(range(half)), *[[k] for k in last]]
+        near_out, *last_out = after(expert_ffn(ins, first, second, live, held), far_back)
+        last_back = swap(last, last_out)
+        near_back = within(near_out.reshape(half, capacity, width))
+        mixed = mix(run_of_slot[half + quarter :], hidden, last_back, slots_dev, AHEAD)
+        return mix(run_of_slot, mixed, [near_back, *far_back], slots_dev)
 
     dispatch = (group_ids[:, None] == run_group[None, :]).astype(jnp.bfloat16)
     runs = slots[0].reshape(slots_dev, capacity * width)

time: 132 us -> 132 us (level)
  waiting for transfers between devices: 36.4 us -> 24.1 us
  local copies, waits for them, and re-layouts: 2.65 us -> 8.91 us
  starting transfers between devices: 40.2 us -> 43.2 us
  Pallas kernels: 50.3 us -> 52 us
    ppermute x16, waiting for transfers between devices: 35.6 us -> 23.3 us  [swap(): lax.ppermute(a, 'lang', [(i, i ^ k) for i in range(lang_count)])]
    unnamed x6 -> x22, local copies, waits for them, and re-layouts: 1.21 us -> 7.4 us
    all_to_all x2, starting transfers between devices: 8.5 us -> 11.2 us  [within(): lax.all_to_all(array, 'lang', 0, 0, axis_index_groups=halves, tiled=True)]
  transfers between devices with their start and end apart: 24 -> 24, of which waited for: 10 -> 8; matrix products, arithmetic and copies ran while one was open for 2% -> 2% of each run, Pallas kernels for 36% -> 37%
where the time goes in v6:
time: 132 us; the launch traced here: 131 us
  Pallas kernels  52 us (39%)
  starting transfers between devices  43.2 us (33%)
  waiting for transfers between devices  24.1 us (18%)
  local copies, waits for them, and re-layouts  8.91 us (7%)
  other arithmetic  1.68 us (1%)
    pallas_call x2, Pallas kernels, expert_ffn(): pl.pallas_call(functools.partial(expert_kernel, sizes, pieces, per, slots...  34.6 us
    ppermute x16, starting transfers between devices, swap(): lax.ppermute(a, 'lang', [(i, i ^ k) for i in range(lang_count)])  30.4 us
    ppermute x16, waiting for transfers between devices, swap(): lax.ppermute(a, 'lang', [(i, i ^ k) for i in range(lang_count)])  23.3 us
    all_to_all x2, starting transfers between devices, within(): lax.all_to_all(array, 'lang', 0, 0, axis_index_groups=halves, tiled=True)  11.2 us
    unnamed x22, local copies, waits for them, and re-layouts  7.4 us
    pallas_call x1, Pallas kernels, hidden_states(): pl.pallas_call(functools.partial(hidden_kernel, len(weights), runs, slots...  5.29 us
    pallas_call x1, Pallas kernels, attend(): pl.pallas_call(functools.partial(attend_kernel, len(rest)), in_specs=in_v...  4.7 us
    pallas_call x1, Pallas kernels, project(): pl.pallas_call(functools.partial(project_kernel, pieces), in_specs=[pl.Bl...  3.7 us
  transfers between devices with their start and end apart: 24, of which 8 were waited for; matrix products, arithmetic and copies ran while one was open for 2% of the time, Pallas kernels for 37%

profile of v6, /device:TPU:16, one launch (start us, length us, event | category | flops | bytes accessed | tf_op | source)
XLA Modules:
  0.0 130.8 jit_solution(1473398437549733286)
XLA Ops:
  0.0 0.0 collective-permute-start
  0.0 0.5 collective-permute-start.1
  0.5 0.5 collective-permute-start.3
  1.0 0.7 broadcast_in_dim.71.gain
  1.7 0.7 copy.16
  2.5 0.1 reduce
  2.6 0.1 convert_reduce_fusion
  2.7 0.1 fusion.bias
  2.9 0.2 convert_reduce_fusion.1
  3.0 0.9 select_reduce_fusion
  3.9 0.2 select_reduce_fusion.2
  4.1 0.1 select_reduce_fusion.1
  4.2 1.2 copy-done
  5.4 3.7 %shard_map.127 = (bf16[256,960]{1,0:T(8,128)(2,1)S(1)}, f32[256,1024]{1,0:T(8,128)S(1)}, f32[256,1024]{1,0:T(8,128)S(1)}, f32[256,1024]{1,0:T(8,128)S(1)}) custom-call(s32[1]{0:T(128)} %bitcast.3.at_ref, bf16[256,1920]{1,0:T(8,128)(2,1)S(1)} %copy-done, f32[1,1920]{1,0:T(1,128)S(1)} %broadcast_in_dim.71.gain, bf16[960,1024]{1,0:T(8,128)(2,1)} %refs_0_.1, ...), custom_call_target="tpu_custom_call" | custom-call | flops 1509949440 | bytes 6881280 | tf_op jit(solution)/shard_map/pallas_call | solution.py:84
  9.1 0.0 collective-permute-done.1.refs_5_
  9.1 0.8 collective-permute-done.2.refs_6_
  9.9 4.7 %shard_map.128.context = bf16[256,1024]{1,0:T(8,128)(2,1)S(1)} custom-call(f32[256,128]{1,0:T(8,128)S(1)} %fusion.bias, bf16[256,960]{1,0:T(8,128)(2,1)S(1)} %get-tuple-element.63.refs_0_, f32[256,1024]{1,0:T(8,128)S(1)} %get-tuple-element.64.refs_1_, f32[256,1024]{1,0:T(8,128)S(1)} %get-tuple-element.65.refs_2_, f32[256,1024]{1,0:T(8,128)S(1)} %get-tuple-element.66.refs_3_, ...), custom_call_target="tpu_custom_call" | custom-call | flops 3019898880 | bytes 9043968 | tf_op jit(solution)/shard_map/pallas_call | solution.py:140
  14.7 0.2 collective-permute-start.12
  14.9 0.4 collective-permute-start.13
  15.3 5.3 %shard_map.129 = (bf16[256,1920]{1,0:T(8,128)(2,1)S(1)}, bf16[8,32,1920]{2,1,0:T(8,128)(2,1)}, bf16[32,1920]{1,0:T(8,128)(2,1)S(1)}, bf16[32,1920]{1,0:T(8,128)(...) custom-call(s32[1]{0:T(128)} %bitcast.3.at_ref, ...), custom_call_target="tpu_custom_call" | custom-call | flops 1006632960 | bytes 5439488 | tf_op jit(solution)/shard_map/pallas_call | solution.py:191
  20.6 0.1 collective-permute-start.4
  20.6 3.8 %collective-permute-start.5 = (bf16[32,1920]{1,0:T(8,128)(2,1)S(1)}, bf16[32,1920]{1,0:T(8,128)(2,1)S(1)}, u32[]{:S(2)}, u32[]{:S(2)}) collective-permute-start(bf16[32,1920]{1,0:T(8,128)(2,1)S(1)} %get-tuple-element.76), channel_id=1, source_target_pairs={{0,18},{2,16},{4,22},{6,20},{8,26},{10,24},{12,30},{14,28},{16,2},... | collective-permute-start | bytes 368648 | tf_op jit(solution)/shard_map/ppermute | solution.py:427
  24.5 1.3 collective-permute-start.6
  25.8 6.4 %collective-permute-done.4.refs_0_ = bf16[32,1920]{1,0:T(8,128)(2,1)S(1)} collective-permute-done((bf16[32,1920]{1,0:T(8,128)(2,1)S(1)}, bf16[32,1920]{1,0:T(8,128)(2,1)S(1)}, u32[]{:S(2)}, u32[]{:S(2)}) %collective-permute-start.4) | collective-permute-done | bytes 122912 | tf_op jit(solution)/shard_map/ppermute | solution.py:427
  32.2 5.6 %collective-permute-start.7 = (bf16[32,1920]{1,0:T(8,128)(2,1)S(1)}, bf16[32,1920]{1,0:T(8,128)(2,1)S(1)}, u32[]{:S(2)}, u32[]{:S(2)}) collective-permute-start(bf16[32,1920]{1,0:T(8,128)(2,1)S(1)} %get-tuple-element.78), channel_id=1, source_target_pairs={{0,22},{2,20},{4,18},{6,16},{8,30},{10,28},{12,26},{14,24},{16,6},... | collective-permute-start | bytes 368648 | tf_op jit(solution)/shard_map/ppermute | solution.py:427
  38.5 3.7 %all-to-all-start = ((bf16[8,32,1920]{2,1,0:T(8,128)(2,1)}), bf16[8,32,1920]{2,1,0:T(8,128)(2,1)S(1)}, u32[]{:S(2)}, u32[]{:S(2)}) async-start(bf16[8,32,1920]{2,1,0:T(8,128)(2,1)} %get-tuple-element.74), calls=%async_computation | async-start | bytes 1966080 | tf_op jit(solution)/shard_map/all_to_all | solution.py:435
  42.2 0.0 collective-permute-done.5.refs_1_
  42.2 1.9 %collective-permute-start.8 = (bf16[32,1920]{1,0:T(8,128)(2,1)}, bf16[32,1920]{1,0:T(8,128)(2,1)S(1)}, u32[]{:S(2)}, u32[]{:S(2)}) collective-permute-start(bf16[32,1920]{1,0:T(8,128)(2,1)} %get-tuple-element.80), channel_id=1, source_target_pairs={{0,24},{2,26},{4,28},{6,30},{8,16},{10,18},{12,20},{14,22},{16,8},... | collective-permute-start | bytes 368648 | tf_op jit(solution)/shard_map/ppermute | solution.py:427
  44.1 0.0 collective-permute-done.6.refs_2_
  44.1 1.3 %collective-permute-start.9 = (bf16[32,1920]{1,0:T(8,128)(2,1)}, bf16[32,1920]{1,0:T(8,128)(2,1)S(1)}, u32[]{:S(2)}, u32[]{:S(2)}) collective-permute-start(bf16[32,1920]{1,0:T(8,128)(2,1)} %get-tuple-element.82), channel_id=1, source_target_pairs={{0,26},{2,24},{4,30},{6,28},{8,18},{10,16},{12,22},{14,20},{16,10}... | collective-permute-start | bytes 368648 | tf_op jit(solution)/shard_map/ppermute | solution.py:427
  45.4 2.0 %collective-permute-start.10 = (bf16[32,1920]{1,0:T(8,128)(2,1)}, bf16[32,1920]{1,0:T(8,128)(2,1)S(1)}, u32[]{:S(2)}, u32[]{:S(2)}) collective-permute-start(bf16[32,1920]{1,0:T(8,128)(2,1)} %get-tuple-element.84), channel_id=1, source_target_pairs={{0,28},{2,30},{4,24},{6,26},{8,20},{10,22},{12,16},{14,18},{16,12}... | collective-permute-start | bytes 368648 | tf_op jit(solution)/shard_map/ppermute | solution.py:427
  47.5 0.7 collective-permute-start.11
  48.3 13.9 %shard_map.131 = (bf16[32,1920]{1,0:T(8,128)(2,1)S(1)}, bf16[32,1920]{1,0:T(8,128)(2,1)S(1)}, bf16[32,1920]{1,0:T(8,128)(2,1)S(1)}, bf16[32,1920]{1,0:T(8,128)(2,1)S(1)}) custom-call(s32[1]{0:T(128)} %constant.38.clone.1.live, bf16[32,1920]{1,0:T(8,128)(2,1)S(1)} %get-tuple-element.87.refs_0_, bf16[32,1920]{1,0:T(8,128)(2,1)S(1)} %get-tuple-element.88.refs_1_, ...), custom_call_target="tpu_custom_call" | custom-call | flops 4026531840 | bytes 31457280 | tf_op jit(solution)/shard_map/pallas_call | solution.py:332
  62.1 0.0 collective-permute-done.9.refs_5_.refs_2_
  62.1 1.9 %collective-permute-done.10.refs_6_.refs_3_ = bf16[32,1920]{1,0:T(8,128)(2,1)S(1)} collective-permute-done((bf16[32,1920]{1,0:T(8,128)(2,1)}, bf16[32,1920]{1,0:T(8,128)(2,1)S(1)}, u32[]{:S(2)}, u32[]{:S(2)}) %collective-permute-start.10) | collective-permute-done | bytes 122912 | tf_op jit(solution)/shard_map/ppermute | solution.py:427
  64.0 4.8 %collective-permute-done.11.refs_7_.refs_4_ = bf16[32,1920]{1,0:T(8,128)(2,1)S(1)} collective-permute-done((bf16[32,1920]{1,0:T(8,128)(2,1)}, bf16[32,1920]{1,0:T(8,128)(2,1)S(1)}, u32[]{:S(2)}, u32[]{:S(2)}) %collective-permute-start.11) | collective-permute-done | bytes 122912 | tf_op jit(solution)/shard_map/ppermute | solution.py:427
  68.8 0.0 all-to-all-done.near
  68.8 1.2 shard_map.132
  70.0 0.2 collective-permute-start.14
  70.1 2.9 %collective-permute-start.15 = (bf16[32,1920]{1,0:T(8,128)(2,1)S(1)}, bf16[32,1920]{1,0:T(8,128)(2,1)S(1)}, u32[]{:S(2)}, u32[]{:S(2)}) collective-permute-start(bf16[32,1920]{1,0:T(8,128)(2,1)S(1)} %get-tuple-element.99), channel_id=1, source_target_pairs={{0,18},{2,16},{4,22},{6,20},{8,26},{10,24},{12,30},{14,28},{16,2},... | collective-permute-start | bytes 368648 | tf_op jit(solution)/shard_map/ppermute | solution.py:427
  73.0 0.2 collective-permute-start.16
  73.2 4.5 %collective-permute-start.17 = (bf16[32,1920]{1,0:T(8,128)(2,1)S(1)}, bf16[32,1920]{1,0:T(8,128)(2,1)S(1)}, u32[]{:S(2)}, u32[]{:S(2)}) collective-permute-start(bf16[32,1920]{1,0:T(8,128)(2,1)S(1)} %get-tuple-element.101), channel_id=1, source_target_pairs={{0,22},{2,20},{4,18},{6,16},{8,30},{10,28},{12,26},{14,24},{16,6},... | collective-permute-start | bytes 368648 | tf_op jit(solution)/shard_map/ppermute | solution.py:427
  77.7 20.7 %shard_map.133 = (bf16[256,1920]{1,0:T(8,128)(2,1)}, bf16[32,1920]{1,0:T(8,128)(2,1)S(1)}, bf16[32,1920]{1,0:T(8,128)(2,1)S(1)}, bf16[32,1920]{1,0:T(8,128)(2,1)S(1)}, bf16[32,1920]{1,0:T(8,128)(2,1)S(1)}) custom-call(s32[16]{0:T(128)S(1)} %get-tuple-element.97.live, bf16[256,1920]{1,0:T(8,128)(2,1)S(1)} %bitcast.12, ...), custom_call_target="tpu_custom_call" | custom-call | flops 12079595520 | bytes 31457280 | tf_op jit(solution)/shard_map/pallas_call | solution.py:332
  98.4 0.0 collective-permute-done.15.refs_1_
  98.4 0.1 collective-permute-start.18
  98.5 2.1 %collective-permute-start.19 = (bf16[32,1920]{1,0:T(8,128)(2,1)S(1)}, bf16[32,1920]{1,0:T(8,128)(2,1)S(1)}, u32[]{:S(2)}, u32[]{:S(2)}) collective-permute-start(bf16[32,1920]{1,0:T(8,128)(2,1)S(1)} %get-tuple-element.113), channel_id=1, source_target_pairs={{0,26},{2,24},{4,30},{6,28},{8,18},{10,16},{12,22},{14,20},{16,10}... | collective-permute-start | bytes 368648 | tf_op jit(solution)/shard_map/ppermute | solution.py:427
  100.6 1.1 collective-permute-start.20
  101.7 2.6 %collective-permute-start.21 = (bf16[32,1920]{1,0:T(8,128)(2,1)S(1)}, bf16[32,1920]{1,0:T(8,128)(2,1)S(1)}, u32[]{:S(2)}, u32[]{:S(2)}) collective-permute-start(bf16[32,1920]{1,0:T(8,128)(2,1)S(1)} %get-tuple-element.115), channel_id=1, source_target_pairs={{0,30},{2,28},{4,26},{6,24},{8,22},{10,20},{12,18},{14,16},{16,14}... | collective-permute-start | bytes 368648 | tf_op jit(solution)/shard_map/ppermute | solution.py:427
  104.4 0.1 slice.3.run_ref
  104.4 7.4 %all-to-all-start.1 = ((bf16[8,32,1920]{2,1,0:T(8,128)(2,1)}), bf16[8,32,1920]{2,1,0:T(8,128)(2,1)S(1)}, u32[]{:S(2)}, u32[]{:S(2)}) async-start(bf16[8,32,1920]{2,1,0:T(8,128)(2,1)} %bitcast.8), calls=%async_computation.1 | async-start | bytes 1966080 | tf_op jit(solution)/shard_map/all_to_all | solution.py:435
  111.9 2.0 %collective-permute-done.18.refs_0_ = bf16[32,1920]{1,0:T(8,128)(2,1)S(1)} collective-permute-done((bf16[32,1920]{1,0:T(8,128)(2,1)S(1)}, bf16[32,1920]{1,0:T(8,128)(2,1)S(1)}, u32[]{:S(2)}, u32[]{:S(2)}) %collective-permute-start.18) | collective-permute-done | bytes 122912 | tf_op jit(solution)/shard_map/ppermute | solution.py:427
  113.9 0.6 copy-done.2
  114.5 5.2 %collective-permute-done.19.refs_1_ = bf16[32,1920]{1,0:T(8,128)(2,1)S(1)} collective-permute-done((bf16[32,1920]{1,0:T(8,128)(2,1)S(1)}, bf16[32,1920]{1,0:T(8,128)(2,1)S(1)}, u32[]{:S(2)}, u32[]{:S(2)}) %collective-permute-start.19) | collective-permute-done | bytes 122912 | tf_op jit(solution)/shard_map/ppermute | solution.py:427
  119.7 0.6 copy-done.4
  120.4 0.4 collective-permute-done.20.refs_2_
  120.8 0.6 copy-done.6
  121.4 2.6 %collective-permute-done.21.refs_3_ = bf16[32,1920]{1,0:T(8,128)(2,1)S(1)} collective-permute-done((bf16[32,1920]{1,0:T(8,128)(2,1)S(1)}, bf16[32,1920]{1,0:T(8,128)(2,1)S(1)}, u32[]{:S(2)}, u32[]{:S(2)}) %collective-permute-start.21) | collective-permute-done | bytes 122912 | tf_op jit(solution)/shard_map/ppermute | solution.py:427
  124.0 0.6 copy-done.8
  124.6 0.9 copy-done.3
  125.5 0.9 copy-done.5
  126.4 0.9 copy-done.7
  127.3 0.9 copy-done.9
  128.2 0.7 shard_map.134.base
  128.9 1.9 %shard_map.135 = bf16[256,1920]{1,0:T(8,128)(2,1)} custom-call(s32[16]{0:T(128)S(1)} %broadcast_subtract_fusion.run_ref, bf16[256,1920]{1,0:T(8,128)(2,1)S(1)} %shard_map.134.base, bf16[8,32,1920]{2,1,0:T(8,128)(2,1)S(1)} %all-to-all-done.1.near, bf16[32,1920]{1,0:T(8,128)(2,1)S(1)} %collective-permute-done.14.refs_0_, ...), custom_call_target="tpu_custom_call" | custom-call | bytes 3440640 | tf_op jit(solution)/shard_map/pallas_call | solution.py:228
  (31 shorter events, 0.1 us)
Async XLA Ops:
  0.0 9.1 %collective-permute-start = (bf16[960,1024]{1,0:T(8,128)(2,1)}, bf16[960,1024]{1,0:T(8,128)(2,1)}, u32[]{:S(2)}, u32[]{:S(2)}) collective-permute-start(bf16[960,1024]{1,0:T(8,128)(2,1)} %refs_0_.1), channel_id=1, source_target_pairs={{0,1},{1,0},{2,3},{3,2},{4,5},{5,4},{6,7},{7,6},{8,9},{9,8},{10,11... | collective-permute-start | bytes 5898248 | tf_op jit(solution)/shard_map/ppermute | solution.py:378
  0.0 9.1 %collective-permute-start.1 = (bf16[960,1024]{1,0:T(8,128)(2,1)}, bf16[960,1024]{1,0:T(8,128)(2,1)}, u32[]{:S(2)}, u32[]{:S(2)}) collective-permute-start(bf16[960,1024]{1,0:T(8,128)(2,1)} %refs_1_.1), channel_id=1, source_target_pairs={{0,1},{1,0},{2,3},{3,2},{4,5},{5,4},{6,7},{7,6},{8,9},{9,8},{10,11... | collective-permute-start | bytes 5898248 | tf_op jit(solution)/shard_map/ppermute | solution.py:378
  0.5 9.4 %collective-permute-start.2 = (bf16[960,1024]{1,0:T(8,128)(2,1)}, bf16[960,1024]{1,0:T(8,128)(2,1)}, u32[]{:S(2)}, u32[]{:S(2)}) collective-permute-start(bf16[960,1024]{1,0:T(8,128)(2,1)} %refs_2_.1), channel_id=1, source_target_pairs={{0,1},{1,0},{2,3},{3,2},{4,5},{5,4},{6,7},{7,6},{8,9},{9,8},{10,11... | collective-permute-start | bytes 5898248 | tf_op jit(solution)/shard_map/ppermute | solution.py:378
  0.5 14.1 %collective-permute-start.3 = (bf16[512,1920]{1,0:T(8,128)(2,1)}, bf16[512,1920]{1,0:T(8,128)(2,1)}, u32[]{:S(2)}, u32[]{:S(2)}) collective-permute-start(bf16[512,1920]{1,0:T(8,128)(2,1)} %refs_0_.2), channel_id=1, source_target_pairs={{0,1},{1,0},{2,3},{3,2},{4,5},{5,4},{6,7},{7,6},{8,9},{9,8},{10,11... | collective-permute-start | bytes 5898248 | tf_op jit(solution)/shard_map/ppermute | solution.py:378
  4.2 1.2 copy-start
  9.9 5.3 %copy-start.10 = (f32[1920]{0:T(1024)S(1)}, f32[1920]{0:T(1024)}, u32[]{:S(2)}) copy-start(f32[1920]{0:T(1024)} %param.23) | copy-start | bytes 23044
  9.9 5.3 %copy-start.1 = (bf16[256,1920]{1,0:T(8,128)(2,1)S(1)}, bf16[256,1920]{1,0:T(8,128)(2,1)}, u32[]{:S(2)}) copy-start(bf16[256,1920]{1,0:T(8,128)(2,1)} %tokens.3) | copy-start | bytes 2949124
  14.7 32.9 %collective-permute-start.12 = (bf16[1920,2048]{1,0:T(8,128)(2,1)}, bf16[1920,2048]{1,0:T(8,128)(2,1)}, u32[]{:S(2)}, u32[]{:S(2)}) collective-permute-start(bf16[1920,2048]{1,0:T(8,128)(2,1)} %bitcast.13), channel_id=1, source_target_pairs={{0,1},{1,0},{2,3},{3,2},{4,5},{5,4},{6,7},{7,6},{8,9},{9,8},{10,11... | collective-permute-start | bytes 23592968 | tf_op jit(solution)/shard_map/ppermute | solution.py:378
  14.9 33.4 %collective-permute-start.13 = (bf16[2048,1920]{1,0:T(8,128)(2,1)}, bf16[2048,1920]{1,0:T(8,128)(2,1)}, u32[]{:S(2)}, u32[]{:S(2)}) collective-permute-start(bf16[2048,1920]{1,0:T(8,128)(2,1)} %bitcast.16), channel_id=1, source_target_pairs={{0,1},{1,0},{2,3},{3,2},{4,5},{5,4},{6,7},{7,6},{8,9},{9,8},{10,11... | collective-permute-start | bytes 23592968 | tf_op jit(solution)/shard_map/ppermute | solution.py:378
  20.6 11.6 %collective-permute-start.4 = (bf16[32,1920]{1,0:T(8,128)(2,1)S(1)}, bf16[32,1920]{1,0:T(8,128)(2,1)S(1)}, u32[]{:S(2)}, u32[]{:S(2)}) collective-permute-start(bf16[32,1920]{1,0:T(8,128)(2,1)S(1)} %get-tuple-element.75), channel_id=1, source_target_pairs={{0,16},{2,18},{4,20},{6,22},{8,24},{10,26},{12,28},{14,30},{16,0},... | collective-permute-start | bytes 368648 | tf_op jit(solution)/shard_map/ppermute | solution.py:427
  20.6 21.6 %collective-permute-start.5 = (bf16[32,1920]{1,0:T(8,128)(2,1)S(1)}, bf16[32,1920]{1,0:T(8,128)(2,1)S(1)}, u32[]{:S(2)}, u32[]{:S(2)}) collective-permute-start(bf16[32,1920]{1,0:T(8,128)(2,1)S(1)} %get-tuple-element.76), channel_id=1, source_target_pairs={{0,18},{2,16},{4,22},{6,20},{8,26},{10,24},{12,30},{14,28},{16,2},... | collective-permute-start | bytes 368648 | tf_op jit(solution)/shard_map/ppermute | solution.py:427
  24.5 19.6 %collective-permute-start.6 = (bf16[32,1920]{1,0:T(8,128)(2,1)S(1)}, bf16[32,1920]{1,0:T(8,128)(2,1)S(1)}, u32[]{:S(2)}, u32[]{:S(2)}) collective-permute-start(bf16[32,1920]{1,0:T(8,128)(2,1)S(1)} %get-tuple-element.77), channel_id=1, source_target_pairs={{0,20},{2,22},{4,16},{6,18},{8,28},{10,30},{12,24},{14,26},{16,4},... | collective-permute-start | bytes 368648 | tf_op jit(solution)/shard_map/ppermute | solution.py:427
  32.2 13.3 %collective-permute-start.7 = (bf16[32,1920]{1,0:T(8,128)(2,1)S(1)}, bf16[32,1920]{1,0:T(8,128)(2,1)S(1)}, u32[]{:S(2)}, u32[]{:S(2)}) collective-permute-start(bf16[32,1920]{1,0:T(8,128)(2,1)S(1)} %get-tuple-element.78), channel_id=1, source_target_pairs={{0,22},{2,20},{4,18},{6,16},{8,30},{10,28},{12,26},{14,24},{16,6},... | collective-permute-start | bytes 368648 | tf_op jit(solution)/shard_map/ppermute | solution.py:427
  38.5 30.3 %all-to-all-start = ((bf16[8,32,1920]{2,1,0:T(8,128)(2,1)}), bf16[8,32,1920]{2,1,0:T(8,128)(2,1)S(1)}, u32[]{:S(2)}, u32[]{:S(2)}) async-start(bf16[8,32,1920]{2,1,0:T(8,128)(2,1)} %get-tuple-element.74), calls=%async_computation | async-start | bytes 1966080 | tf_op jit(solution)/shard_map/all_to_all | solution.py:435
  42.2 19.9 %collective-permute-start.8 = (bf16[32,1920]{1,0:T(8,128)(2,1)}, bf16[32,1920]{1,0:T(8,128)(2,1)S(1)}, u32[]{:S(2)}, u32[]{:S(2)}) collective-permute-start(bf16[32,1920]{1,0:T(8,128)(2,1)} %get-tuple-element.80), channel_id=1, source_target_pairs={{0,24},{2,26},{4,28},{6,30},{8,16},{10,18},{12,20},{14,22},{16,8},... | collective-permute-start | bytes 368648 | tf_op jit(solution)/shard_map/ppermute | solution.py:427
  44.1 18.0 %collective-permute-start.9 = (bf16[32,1920]{1,0:T(8,128)(2,1)}, bf16[32,1920]{1,0:T(8,128)(2,1)S(1)}, u32[]{:S(2)}, u32[]{:S(2)}) collective-permute-start(bf16[32,1920]{1,0:T(8,128)(2,1)} %get-tuple-element.82), channel_id=1, source_target_pairs={{0,26},{2,24},{4,30},{6,28},{8,18},{10,16},{12,22},{14,20},{16,10}... | collective-permute-start | bytes 368648 | tf_op jit(solution)/shard_map/ppermute | solution.py:427
  45.4 18.6 %collective-permute-start.10 = (bf16[32,1920]{1,0:T(8,128)(2,1)}, bf16[32,1920]{1,0:T(8,128)(2,1)S(1)}, u32[]{:S(2)}, u32[]{:S(2)}) collective-permute-start(bf16[32,1920]{1,0:T(8,128)(2,1)} %get-tuple-element.84), channel_id=1, source_target_pairs={{0,28},{2,30},{4,24},{6,26},{8,20},{10,22},{12,16},{14,18},{16,12}... | collective-permute-start | bytes 368648 | tf_op jit(solution)/shard_map/ppermute | solution.py:427
  47.5 21.3 %collective-permute-start.11 = (bf16[32,1920]{1,0:T(8,128)(2,1)}, bf16[32,1920]{1,0:T(8,128)(2,1)S(1)}, u32[]{:S(2)}, u32[]{:S(2)}) collective-permute-start(bf16[32,1920]{1,0:T(8,128)(2,1)} %get-tuple-element.86), channel_id=1, source_target_pairs={{0,30},{2,28},{4,26},{6,24},{8,22},{10,20},{12,18},{14,16},{16,14}... | collective-permute-start | bytes 368648 | tf_op jit(solution)/shard_map/ppermute | solution.py:427
  70.0 28.5 %collective-permute-start.14 = (bf16[32,1920]{1,0:T(8,128)(2,1)S(1)}, bf16[32,1920]{1,0:T(8,128)(2,1)S(1)}, u32[]{:S(2)}, u32[]{:S(2)}) collective-permute-start(bf16[32,1920]{1,0:T(8,128)(2,1)S(1)} %get-tuple-element.98), channel_id=1, source_target_pairs={{0,16},{2,18},{4,20},{6,22},{8,24},{10,26},{12,28},{14,30},{16,0},... | collective-permute-start | bytes 368648 | tf_op jit(solution)/shard_map/ppermute | solution.py:427
  70.1 28.3 %collective-permute-start.15 = (bf16[32,1920]{1,0:T(8,128)(2,1)S(1)}, bf16[32,1920]{1,0:T(8,128)(2,1)S(1)}, u32[]{:S(2)}, u32[]{:S(2)}) collective-permute-start(bf16[32,1920]{1,0:T(8,128)(2,1)S(1)} %get-tuple-element.99), channel_id=1, source_target_pairs={{0,18},{2,16},{4,22},{6,20},{8,26},{10,24},{12,30},{14,28},{16,2},... | collective-permute-start | bytes 368648 | tf_op jit(solution)/shard_map/ppermute | solution.py:427
  73.0 25.4 %collective-permute-start.16 = (bf16[32,1920]{1,0:T(8,128)(2,1)S(1)}, bf16[32,1920]{1,0:T(8,128)(2,1)S(1)}, u32[]{:S(2)}, u32[]{:S(2)}) collective-permute-start(bf16[32,1920]{1,0:T(8,128)(2,1)S(1)} %get-tuple-element.100), channel_id=1, source_target_pairs={{0,20},{2,22},{4,16},{6,18},{8,28},{10,30},{12,24},{14,26},{16,4},... | collective-permute-start | bytes 368648 | tf_op jit(solution)/shard_map/ppermute | solution.py:427
  73.2 25.2 %collective-permute-start.17 = (bf16[32,1920]{1,0:T(8,128)(2,1)S(1)}, bf16[32,1920]{1,0:T(8,128)(2,1)S(1)}, u32[]{:S(2)}, u32[]{:S(2)}) collective-permute-start(bf16[32,1920]{1,0:T(8,128)(2,1)S(1)} %get-tuple-element.101), channel_id=1, source_target_pairs={{0,22},{2,20},{4,18},{6,16},{8,30},{10,28},{12,26},{14,24},{16,6},... | collective-permute-start | bytes 368648 | tf_op jit(solution)/shard_map/ppermute | solution.py:427
  98.4 15.5 %collective-permute-start.18 = (bf16[32,1920]{1,0:T(8,128)(2,1)S(1)}, bf16[32,1920]{1,0:T(8,128)(2,1)S(1)}, u32[]{:S(2)}, u32[]{:S(2)}) collective-permute-start(bf16[32,1920]{1,0:T(8,128)(2,1)S(1)} %get-tuple-element.112), channel_id=1, source_target_pairs={{0,24},{2,26},{4,28},{6,30},{8,16},{10,18},{12,20},{14,22},{16,8},... | collective-permute-start | bytes 368648 | tf_op jit(solution)/shard_map/ppermute | solution.py:427
  98.5 21.2 %collective-permute-start.19 = (bf16[32,1920]{1,0:T(8,128)(2,1)S(1)}, bf16[32,1920]{1,0:T(8,128)(2,1)S(1)}, u32[]{:S(2)}, u32[]{:S(2)}) collective-permute-start(bf16[32,1920]{1,0:T(8,128)(2,1)S(1)} %get-tuple-element.113), channel_id=1, source_target_pairs={{0,26},{2,24},{4,30},{6,28},{8,18},{10,16},{12,22},{14,20},{16,10}... | collective-permute-start | bytes 368648 | tf_op jit(solution)/shard_map/ppermute | solution.py:427
  100.6 20.2 %collective-permute-start.20 = (bf16[32,1920]{1,0:T(8,128)(2,1)S(1)}, bf16[32,1920]{1,0:T(8,128)(2,1)S(1)}, u32[]{:S(2)}, u32[]{:S(2)}) collective-permute-start(bf16[32,1920]{1,0:T(8,128)(2,1)S(1)} %get-tuple-element.114), channel_id=1, source_target_pairs={{0,28},{2,30},{4,24},{6,26},{8,20},{10,22},{12,16},{14,18},{16,12}... | collective-permute-start | bytes 368648 | tf_op jit(solution)/shard_map/ppermute | solution.py:427
  101.7 22.3 %collective-permute-start.21 = (bf16[32,1920]{1,0:T(8,128)(2,1)S(1)}, bf16[32,1920]{1,0:T(8,128)(2,1)S(1)}, u32[]{:S(2)}, u32[]{:S(2)}) collective-permute-start(bf16[32,1920]{1,0:T(8,128)(2,1)S(1)} %get-tuple-element.115), channel_id=1, source_target_pairs={{0,30},{2,28},{4,26},{6,24},{8,22},{10,20},{12,18},{14,16},{16,14}... | collective-permute-start | bytes 368648 | tf_op jit(solution)/shard_map/ppermute | solution.py:427
  104.4 24.5 %all-to-all-start.1 = ((bf16[8,32,1920]{2,1,0:T(8,128)(2,1)}), bf16[8,32,1920]{2,1,0:T(8,128)(2,1)S(1)}, u32[]{:S(2)}, u32[]{:S(2)}) async-start(bf16[8,32,1920]{2,1,0:T(8,128)(2,1)} %bitcast.8), calls=%async_computation.1 | async-start | bytes 1966080 | tf_op jit(solution)/shard_map/all_to_all | solution.py:435
  113.9 0.6 copy-start.2
  119.7 0.6 copy-start.4
  120.8 0.6 copy-start.6
  124.0 0.6 copy-start.8
  124.6 0.9 copy-start.3
  125.5 0.9 copy-start.5
  126.4 0.9 copy-start.7
  127.3 0.9 copy-start.9
